TPU v7x, 32 devices: a whole 2x2x4 slice. The times are simulated.
32 devices in a mesh: row: 4 (over y, x), col: 8 (over z, core).
Axes of the slice: x: 2, y: 2, z: 4, core: 2. Of those that a mesh axis runs over, the one named last changes fastest.
Arguments:
- src_cent: float32 [16, 4096], P(None, 'row'), may hold values from -6.5 to 6.5
- tgt_cent: float32 [16, 1024], P(None, 'col'), may hold values from -6.5 to 6.5
- src_mass: float32 [4096], P('row'), may hold values from 6.1035156e-05 to 0.0009765625
- tgt_mass: float32 [1024], P('col'), may hold values from 0.00024414062 to 0.00390625
- src_pts: float32 [16, 65536], P(None, ('row', 'col')), may hold values from -6.5 to 6.5
- tgt_pts: float32 [16, 262144], P(None, ('row', 'col')), may hold values from -6.5 to 6.5
- src_cluster: int32 [65536], P(('row', 'col')), may hold values from 0 to 4095
- tgt_cluster: int32 [262144], P(('row', 'col')), may hold values from 0 to 1023
- support: int32 [256, 16], P(('row', 'col')), may hold values from 0 to 1023, as said below
Outputs:
- coarse_f: float32 [4096], P('row')
- coarse_g: float32 [1024], P('col')
- fine_f: float32 [65536], P(('row', 'col'))
- fine_g: float32 [262144], P(('row', 'col'))
Inputs may be any that keep to these rules, and one draw needn't show every extreme that they name: `support`: each row names 16 different target blocks; every target block is named by some row; among the rows of one device (aligned blocks of 8 rows) at most 5 entries fall in any one range k * 32 to (k + 1) * 32 - 1, and exactly 5 in some such range for every device.
All inputs are finite; a program needn't handle non-finite values.
Results may differ from a plain program's by a relative error of at most 0.0003.
Values sent between devices are 32-bit elements; how exact they have to be, the bound alone decides.
No kernel may reach another device: no remote copies, remote signals or barrier semaphores. Data moves between devices by JAX's collectives and lax.ppermute only.
A program may use at most 64 MiB of HBM per device.

v0:
```python
import jax
import jax.numpy as jnp
from jax import lax
from jax.sharding import PartitionSpec as P

F = 16
BLK = 256
SUPP = 16
ITERS = 8
SB_DEV = 8
TB_DEV = 32


EPS = 0.1


def combined_all(x, axis, combine):
    everything = jax.tree.map(lambda part: lax.all_gather(part, axis), x)
    leading = jax.tree.map(lambda part: part[0], everything)

    def hop(k, so_far):
        return combine(so_far, jax.tree.map(lambda part: part[k], everything))

    return lax.fori_loop(1, lax.axis_size(axis), hop, leading)


def pair_cost(left_pts, right_pts):
    cross = jnp.einsum(
        "fi,fj->ij",
        left_pts,
        right_pts,
        precision=lax.Precision.HIGHEST,
        preferred_element_type=jnp.float32,
    )
    return (
        jnp.sum(left_pts * left_pts, 0)[:, None]
        + jnp.sum(right_pts * right_pts, 0)[None, :]
        - 2.0 * cross
    )


def combine_lse(left_pair, right_pair):
    left_max, left_sum = left_pair
    right_max, right_sum = right_pair
    joined = jnp.maximum(left_max, right_max)
    return (joined, left_sum * jnp.exp(left_max - joined) + right_sum * jnp.exp(right_max - joined))


def on_device(
    src_cent, tgt_cent, src_mass, tgt_mass, src_pts, tgt_pts, src_cluster, tgt_cluster, support
):
    coarse_cost = pair_cost(src_cent, tgt_cent)
    log_src = jnp.log(src_mass)
    log_tgt = jnp.log(tgt_mass)
    coarse_g = jnp.zeros(coarse_cost.shape[1], jnp.float32)
    coarse_f = jnp.zeros(coarse_cost.shape[0], jnp.float32)
    for turn_index in range(ITERS):
        scores = log_tgt[None, :] + (coarse_g[None, :] - coarse_cost) / EPS
        maxima = jnp.max(scores, 1)
        totals = jnp.sum(jnp.exp(scores - maxima[:, None]), 1)
        maxima, totals = combined_all((maxima, totals), "col", combine_lse)
        coarse_f = -EPS * (maxima + jnp.log(totals))
        scores = log_src[:, None] + (coarse_f[:, None] - coarse_cost) / EPS
        maxima = jnp.max(scores, 0)
        totals = jnp.sum(jnp.exp(scores - maxima[None, :]), 0)
        maxima, totals = combined_all((maxima, totals), "row", combine_lse)
        coarse_g = -EPS * (maxima + jnp.log(totals))
    all_f = lax.all_gather(coarse_f, "row", axis=0, tiled=True)
    all_g = lax.all_gather(coarse_g, "col", axis=0, tiled=True)
    start_f = jnp.take(all_f, src_cluster)
    start_g = jnp.take(all_g, tgt_cluster)
    devices = lax.axis_size(("row", "col"))
    requests_each = SB_DEV * SUPP
    slots_each = requests_each // devices + 1
    wanted = support.reshape(-1)
    owners = wanted // TB_DEV
    local_ids = wanted % TB_DEV
    positions = jnp.arange(requests_each, dtype=jnp.int32)
    earlier = (owners[None, :] == owners[:, None]) & (positions[None, :] < positions[:, None])
    occurs = jnp.sum(earlier.astype(jnp.int32), 1)
    slot_ids = owners * slots_each + occurs
    matches = slot_ids[None, :] == jnp.arange(devices * slots_each, dtype=jnp.int32)[:, None]
    table_ids = jnp.sum(jnp.where(matches, local_ids[None, :] + 1, 0), 1) - 1
    incoming = lax.all_to_all(
        table_ids.reshape(devices, slots_each),
        ("row", "col"),
        split_axis=0,
        concat_axis=0,
        tiled=True,
    )
    picked = jnp.maximum(incoming, 0).reshape(-1)
    send_pts = jnp.take(tgt_pts.reshape(F, TB_DEV, BLK), picked, axis=1)
    send_duals = jnp.take(start_g.reshape(TB_DEV, BLK), picked, axis=0)
    bundle = jnp.concatenate([send_pts, send_duals[None]], 0).reshape(
        F + 1, devices, slots_each, BLK
    )
    received = lax.all_to_all(bundle, ("row", "col"), split_axis=1, concat_axis=1, tiled=True)
    flat_recv = received.reshape(F + 1, devices * slots_each, BLK)
    tiles = jnp.take(flat_recv, slot_ids, axis=1).reshape(F + 1, SB_DEV, SUPP, BLK)

    def block_terms(block_index):
        start = block_index * BLK
        src_block = lax.dynamic_slice_in_dim(src_pts, start, BLK, 1)
        src_dual = lax.dynamic_slice_in_dim(start_f, start, BLK, 0)
        tile = lax.dynamic_slice_in_dim(tiles, block_index, 1, 1)[:, 0]
        tgt_sel = tile[:F]
        tgt_dual = tile[F]
        cross = jnp.einsum(
            "fi,fkj->ikj",
            src_block,
            tgt_sel,
            precision=lax.Precision.HIGHEST,
            preferred_element_type=jnp.float32,
        )
        distance = (
            jnp.sum(src_block * src_block, 0)[:, None, None]
            + jnp.sum(tgt_sel * tgt_sel, 0)[None, :, :]
            - 2.0 * cross
        )
        block_scores = (tgt_dual[None, :, :] - distance) / EPS
        row_max = jnp.max(block_scores, (1, 2))
        row_term = -EPS * (
            row_max
            + jnp.log(jnp.sum(jnp.exp(block_scores - row_max[:, None, None]), (1, 2)))
            - jnp.log(float(SUPP * BLK))
        )
        block_scores = (src_dual[:, None, None] - distance) / EPS
        part_max = jnp.max(block_scores, 0)
        part_sum = jnp.sum(jnp.exp(block_scores - part_max[None]), 0)
        return (row_term, part_max, part_sum)

    row_terms, part_max, part_sum = lax.map(block_terms, jnp.arange(SB_DEV, dtype=jnp.int32))
    match_float = matches.astype(jnp.float32)
    back_max = jnp.dot(
        match_float,
        part_max.reshape(requests_each, BLK),
        precision=lax.Precision.HIGHEST,
        preferred_element_type=jnp.float32,
    )
    back_sum = jnp.dot(
        match_float,
        part_sum.reshape(requests_each, BLK),
        precision=lax.Precision.HIGHEST,
        preferred_element_type=jnp.float32,
    )
    ret_max, ret_sum = (
        lax.all_to_all(
            back_max.reshape(devices, slots_each, BLK),
            ("row", "col"),
            split_axis=0,
            concat_axis=0,
            tiled=True,
        ),
        lax.all_to_all(
            back_sum.reshape(devices, slots_each, BLK),
            ("row", "col"),
            split_axis=0,
            concat_axis=0,
            tiled=True,
        ),
    )
    ret_max = ret_max.reshape(devices * slots_each, BLK)
    ret_sum = ret_sum.reshape(devices * slots_each, BLK)
    owner_mask = incoming.reshape(-1)[:, None] == jnp.arange(TB_DEV, dtype=jnp.int32)[None, :]
    col_max = jnp.max(jnp.where(owner_mask[:, :, None], ret_max[:, None, :], -jnp.inf), 0)
    col_sum = jnp.sum(
        jnp.where(
            owner_mask[:, :, None],
            ret_sum[:, None, :] * jnp.exp(ret_max[:, None, :] - col_max[None]),
            0.0,
        ),
        0,
    )
    named = jnp.sum(owner_mask.astype(jnp.float32), 0)
    col_term = -EPS * (col_max + jnp.log(col_sum) - jnp.log(named * BLK)[:, None])
    fine_f = 0.5 * (start_f + row_terms.reshape(-1))
    fine_g = 0.5 * (start_g + col_term.reshape(-1))
    return (coarse_f, coarse_g, fine_f, fine_g)


def solution(mesh):
    in_specs = (
        P(None, "row"),
        P(None, "col"),
        P("row"),
        P("col"),
        P(None, ("row", "col")),
        P(None, ("row", "col")),
        P(("row", "col")),
        P(("row", "col")),
        P(("row", "col"), None),
    )
    out_specs = (P("row"), P("col"), P(("row", "col")), P(("row", "col")))
    return jax.shard_map(
        on_device, mesh=mesh, in_specs=in_specs, out_specs=out_specs, check_vma=False
    )
```

profile of v0, /device:TPU:0, one launch (start us, length us, event | category | flops | bytes accessed | tf_op | source)
XLA Modules:
  0.0 663.4 jit_solution(3613208877395278518)
XLA Ops:
  2.4 7.3 %all-to-all-start = ((s32[32,1,5]{2,1,0:T(1,128)}), s32[32,1,5]{2,1,0:T(1,128)S(1)}, u32[]{:S(2)}, u32[]{:S(2)}) async-start(s32[32,1,5]{2,1,0:T(1,128)} %bitcast.86), calls=%async_computation | async-start | bytes 32768 | tf_op jit(solution)/shard_map/all_to_all | solution.py:84
  14.4 14.3 %all-gather.1 = f32[8192]{0:T(1024)S(1)} all-gather(f32[1024]{0:T(1024)S(1)} %exponential_reduce_fusion.17), channel_id=3, replica_groups=mesh['row'=4,'col'=8] {'col'}, dimensions={0}, use_global_device_ids=true | all-gather | bytes 36864 | tf_op jit(solution)/shard_map/all_gather | solution.py:18
  28.8 14.0 %all-gather = f32[8192]{0:T(1024)S(1)} all-gather(f32[1024]{0:T(1024)S(1)} %get-tuple-element.2503), channel_id=2, replica_groups=mesh['row'=4,'col'=8] {'col'}, dimensions={0}, use_global_device_ids=true | all-gather | bytes 36864 | tf_op jit(solution)/shard_map/all_gather | solution.py:18
  44.6 7.9 %all-gather.33 = f32[4,1,128]{2,1,0:T(1,128)S(1)} all-gather(f32[1,1,128]{2,1,0:T(1,128)S(1)} %bitcast.352), channel_id=5, replica_groups=mesh['row'=4,'col'=8] {'row'}, dimensions={0}, use_global_device_ids=true | all-gather | bytes 2560 | tf_op jit(solution)/shard_map/all_gather | solution.py:18
  52.5 7.9 %all-gather.32 = f32[4,1,128]{2,1,0:T(1,128)S(1)} all-gather(f32[1,1,128]{2,1,0:T(1,128)S(1)} %bitcast.344), channel_id=4, replica_groups=mesh['row'=4,'col'=8] {'row'}, dimensions={0}, use_global_device_ids=true | all-gather | bytes 2560 | tf_op jit(solution)/shard_map/all_gather | solution.py:18
  61.1 14.0 %all-gather.5 = f32[8192]{0:T(1024)S(1)} all-gather(f32[1024]{0:T(1024)S(1)} %exponential_reduce_fusion.15), channel_id=7, replica_groups=mesh['row'=4,'col'=8] {'col'}, dimensions={0}, use_global_device_ids=true | all-gather | bytes 36864 | tf_op jit(solution)/shard_map/all_gather | solution.py:18
  75.1 14.0 %all-gather.4 = f32[8192]{0:T(1024)S(1)} all-gather(f32[1024]{0:T(1024)S(1)} %fusion.24), channel_id=6, replica_groups=mesh['row'=4,'col'=8] {'col'}, dimensions={0}, use_global_device_ids=true | all-gather | bytes 36864 | tf_op jit(solution)/shard_map/all_gather | solution.py:18
  90.3 7.0 %all-gather.35 = f32[4,1,128]{2,1,0:T(1,128)S(1)} all-gather(f32[1,1,128]{2,1,0:T(1,128)S(1)} %bitcast.353), channel_id=9, replica_groups=mesh['row'=4,'col'=8] {'row'}, dimensions={0}, use_global_device_ids=true | all-gather | bytes 2560 | tf_op jit(solution)/shard_map/all_gather | solution.py:18
  97.3 7.9 %all-gather.34 = f32[4,1,128]{2,1,0:T(1,128)S(1)} all-gather(f32[1,1,128]{2,1,0:T(1,128)S(1)} %bitcast.345), channel_id=8, replica_groups=mesh['row'=4,'col'=8] {'row'}, dimensions={0}, use_global_device_ids=true | all-gather | bytes 2560 | tf_op jit(solution)/shard_map/all_gather | solution.py:18
  105.9 14.0 %all-gather.9 = f32[8192]{0:T(1024)S(1)} all-gather(f32[1024]{0:T(1024)S(1)} %exponential_reduce_fusion.13), channel_id=11, replica_groups=mesh['row'=4,'col'=8] {'col'}, dimensions={0}, use_global_device_ids=true | all-gather | bytes 36864 | tf_op jit(solution)/shard_map/all_gather | solution.py:18
  119.9 14.0 %all-gather.8 = f32[8192]{0:T(1024)S(1)} all-gather(f32[1024]{0:T(1024)S(1)} %fusion.26), channel_id=10, replica_groups=mesh['row'=4,'col'=8] {'col'}, dimensions={0}, use_global_device_ids=true | all-gather | bytes 36864 | tf_op jit(solution)/shard_map/all_gather | solution.py:18
  135.1 7.0 %all-gather.37 = f32[4,1,128]{2,1,0:T(1,128)S(1)} all-gather(f32[1,1,128]{2,1,0:T(1,128)S(1)} %bitcast.354), channel_id=13, replica_groups=mesh['row'=4,'col'=8] {'row'}, dimensions={0}, use_global_device_ids=true | all-gather | bytes 2560 | tf_op jit(solution)/shard_map/all_gather | solution.py:18
  142.1 7.9 %all-gather.36 = f32[4,1,128]{2,1,0:T(1,128)S(1)} all-gather(f32[1,1,128]{2,1,0:T(1,128)S(1)} %bitcast.346), channel_id=12, replica_groups=mesh['row'=4,'col'=8] {'row'}, dimensions={0}, use_global_device_ids=true | all-gather | bytes 2560 | tf_op jit(solution)/shard_map/all_gather | solution.py:18
  150.7 14.0 %all-gather.13 = f32[8192]{0:T(1024)S(1)} all-gather(f32[1024]{0:T(1024)S(1)} %exponential_reduce_fusion.11), channel_id=15, replica_groups=mesh['row'=4,'col'=8] {'col'}, dimensions={0}, use_global_device_ids=true | all-gather | bytes 36864 | tf_op jit(solution)/shard_map/all_gather | solution.py:18
  164.7 14.0 %all-gather.12 = f32[8192]{0:T(1024)S(1)} all-gather(f32[1024]{0:T(1024)S(1)} %fusion.28), channel_id=14, replica_groups=mesh['row'=4,'col'=8] {'col'}, dimensions={0}, use_global_device_ids=true | all-gather | bytes 36864 | tf_op jit(solution)/shard_map/all_gather | solution.py:18
  179.9 7.0 %all-gather.39 = f32[4,1,128]{2,1,0:T(1,128)S(1)} all-gather(f32[1,1,128]{2,1,0:T(1,128)S(1)} %bitcast.355), channel_id=17, replica_groups=mesh['row'=4,'col'=8] {'row'}, dimensions={0}, use_global_device_ids=true | all-gather | bytes 2560 | tf_op jit(solution)/shard_map/all_gather | solution.py:18
  186.8 8.1 %all-gather.38 = f32[4,1,128]{2,1,0:T(1,128)S(1)} all-gather(f32[1,1,128]{2,1,0:T(1,128)S(1)} %bitcast.347), channel_id=16, replica_groups=mesh['row'=4,'col'=8] {'row'}, dimensions={0}, use_global_device_ids=true | all-gather | bytes 2560 | tf_op jit(solution)/shard_map/all_gather | solution.py:18
  195.6 14.0 %all-gather.17 = f32[8192]{0:T(1024)S(1)} all-gather(f32[1024]{0:T(1024)S(1)} %exponential_reduce_fusion.9), channel_id=19, replica_groups=mesh['row'=4,'col'=8] {'col'}, dimensions={0}, use_global_device_ids=true | all-gather | bytes 36864 | tf_op jit(solution)/shard_map/all_gather | solution.py:18
  209.6 14.0 %all-gather.16 = f32[8192]{0:T(1024)S(1)} all-gather(f32[1024]{0:T(1024)S(1)} %fusion.30), channel_id=18, replica_groups=mesh['row'=4,'col'=8] {'col'}, dimensions={0}, use_global_device_ids=true | all-gather | bytes 36864 | tf_op jit(solution)/shard_map/all_gather | solution.py:18
  224.8 7.0 %all-gather.41 = f32[4,1,128]{2,1,0:T(1,128)S(1)} all-gather(f32[1,1,128]{2,1,0:T(1,128)S(1)} %bitcast.356), channel_id=21, replica_groups=mesh['row'=4,'col'=8] {'row'}, dimensions={0}, use_global_device_ids=true | all-gather | bytes 2560 | tf_op jit(solution)/shard_map/all_gather | solution.py:18
  231.8 7.9 %all-gather.40 = f32[4,1,128]{2,1,0:T(1,128)S(1)} all-gather(f32[1,1,128]{2,1,0:T(1,128)S(1)} %bitcast.348), channel_id=20, replica_groups=mesh['row'=4,'col'=8] {'row'}, dimensions={0}, use_global_device_ids=true | all-gather | bytes 2560 | tf_op jit(solution)/shard_map/all_gather | solution.py:18
  240.4 14.0 %all-gather.21 = f32[8192]{0:T(1024)S(1)} all-gather(f32[1024]{0:T(1024)S(1)} %exponential_reduce_fusion.7), channel_id=23, replica_groups=mesh['row'=4,'col'=8] {'col'}, dimensions={0}, use_global_device_ids=true | all-gather | bytes 36864 | tf_op jit(solution)/shard_map/all_gather | solution.py:18
  254.4 14.0 %all-gather.20 = f32[8192]{0:T(1024)S(1)} all-gather(f32[1024]{0:T(1024)S(1)} %fusion.32), channel_id=22, replica_groups=mesh['row'=4,'col'=8] {'col'}, dimensions={0}, use_global_device_ids=true | all-gather | bytes 36864 | tf_op jit(solution)/shard_map/all_gather | solution.py:18
  269.6 7.0 %all-gather.43 = f32[4,1,128]{2,1,0:T(1,128)S(1)} all-gather(f32[1,1,128]{2,1,0:T(1,128)S(1)} %bitcast.357), channel_id=25, replica_groups=mesh['row'=4,'col'=8] {'row'}, dimensions={0}, use_global_device_ids=true | all-gather | bytes 2560 | tf_op jit(solution)/shard_map/all_gather | solution.py:18
  276.6 7.9 %all-gather.42 = f32[4,1,128]{2,1,0:T(1,128)S(1)} all-gather(f32[1,1,128]{2,1,0:T(1,128)S(1)} %bitcast.349), channel_id=24, replica_groups=mesh['row'=4,'col'=8] {'row'}, dimensions={0}, use_global_device_ids=true | all-gather | bytes 2560 | tf_op jit(solution)/shard_map/all_gather | solution.py:18
  285.2 14.0 %all-gather.25 = f32[8192]{0:T(1024)S(1)} all-gather(f32[1024]{0:T(1024)S(1)} %exponential_reduce_fusion.5), channel_id=27, replica_groups=mesh['row'=4,'col'=8] {'col'}, dimensions={0}, use_global_device_ids=true | all-gather | bytes 36864 | tf_op jit(solution)/shard_map/all_gather | solution.py:18
  299.2 14.0 %all-gather.24 = f32[8192]{0:T(1024)S(1)} all-gather(f32[1024]{0:T(1024)S(1)} %fusion.34), channel_id=26, replica_groups=mesh['row'=4,'col'=8] {'col'}, dimensions={0}, use_global_device_ids=true | all-gather | bytes 36864 | tf_op jit(solution)/shard_map/all_gather | solution.py:18
  314.4 7.0 %all-gather.45 = f32[4,1,128]{2,1,0:T(1,128)S(1)} all-gather(f32[1,1,128]{2,1,0:T(1,128)S(1)} %bitcast.358), channel_id=29, replica_groups=mesh['row'=4,'col'=8] {'row'}, dimensions={0}, use_global_device_ids=true | all-gather | bytes 2560 | tf_op jit(solution)/shard_map/all_gather | solution.py:18
  321.3 7.9 %all-gather.44 = f32[4,1,128]{2,1,0:T(1,128)S(1)} all-gather(f32[1,1,128]{2,1,0:T(1,128)S(1)} %bitcast.350), channel_id=28, replica_groups=mesh['row'=4,'col'=8] {'row'}, dimensions={0}, use_global_device_ids=true | all-gather | bytes 2560 | tf_op jit(solution)/shard_map/all_gather | solution.py:18
  329.9 14.0 %all-gather.29 = f32[8192]{0:T(1024)S(1)} all-gather(f32[1024]{0:T(1024)S(1)} %exponential_reduce_fusion.3), channel_id=31, replica_groups=mesh['row'=4,'col'=8] {'col'}, dimensions={0}, use_global_device_ids=true | all-gather | bytes 36864 | tf_op jit(solution)/shard_map/all_gather | solution.py:18
  344.0 14.0 %all-gather.28 = f32[8192]{0:T(1024)S(1)} all-gather(f32[1024]{0:T(1024)S(1)} %fusion.36), channel_id=30, replica_groups=mesh['row'=4,'col'=8] {'col'}, dimensions={0}, use_global_device_ids=true | all-gather | bytes 36864 | tf_op jit(solution)/shard_map/all_gather | solution.py:18
  359.1 7.0 %all-gather.47 = f32[4,1,128]{2,1,0:T(1,128)S(1)} all-gather(f32[1,1,128]{2,1,0:T(1,128)S(1)} %bitcast.351), channel_id=33, replica_groups=mesh['row'=4,'col'=8] {'row'}, dimensions={0}, use_global_device_ids=true | all-gather | bytes 2560 | tf_op jit(solution)/shard_map/all_gather | solution.py:18
  366.1 7.9 %all-gather.46 = f32[4,1,128]{2,1,0:T(1,128)S(1)} all-gather(f32[1,1,128]{2,1,0:T(1,128)S(1)} %bitcast.343), channel_id=32, replica_groups=mesh['row'=4,'col'=8] {'row'}, dimensions={0}, use_global_device_ids=true | all-gather | bytes 2560 | tf_op jit(solution)/shard_map/all_gather | solution.py:18
  374.1 11.5 %all-gather.48 = f32[8,1,128]{2,1,0:T(1,128)S(1)} all-gather(f32[1,1,128]{2,1,0:T(1,128)S(1)} %bitcast.359), channel_id=1, replica_groups=mesh['row'=4,'col'=8] {'col'}, dimensions={0}, use_global_device_ids=true | all-gather | bytes 4608 | tf_op jit(solution)/shard_map/all_gather | solution.py:69
  385.6 32.9 %gather_fusion.2 = f32[8192]{0:T(1024)S(1)} fusion(f32[1024]{0:T(1024)S(1)} %bitcast.298, s32[8192]{0:T(1024)S(1)} %fusion.47), kind=kCustom, calls=%fused_computation.2 | custom fusion | bytes 98304 | tf_op jit(solution)/shard_map/jit(_take)/gather | solution.py:71
  427.6 25.1 %all_gather.262 = f32[4096]{0:T(1024)S(1)} all-gather(f32[1024]{0:T(1024)S(1)} %add_multiply_fusion.3), channel_id=1, replica_groups=mesh['row'=4,'col'=8] {'row'}, dimensions={0}, use_global_device_ids=true | all-gather | bytes 20480 | tf_op jit(solution)/shard_map/all_gather | solution.py:68
  452.7 11.8 %gather_fusion = f32[2048]{0:T(1024)S(1)} fusion(f32[4096]{0:T(1024)S(1)} %all_gather.262, s32[2048]{0:T(1024)S(1)} %fusion.48), kind=kCustom, calls=%fused_computation | custom fusion | bytes 24576 | tf_op jit(solution)/shard_map/jit(_take)/gather | solution.py:70
  466.0 50.9 %all-to-all-done.1 = f32[17,32,5,256]{3,0,2,1:T(8,128)} async-done(((f32[17,32,5,256]{3,0,2,1:T(8,128)}), f32[17,32,5,256]{3,0,2,1:T(8,128)}, u32[]{:S(2)}, u32[]{:S(2)}) %all-to-all-start.1) | async-done | bytes 2785312 | tf_op jit(solution)/shard_map/all_to_all | solution.py:97
  525.2 109.1 %while.304 = (s32[]{:T(128)}, f32[8,256]{1,0:T(8,128)S(1)}, f32[8,16,256]{2,1,0:T(8,128)S(1)}, f32[8,16,256]{2,1,0:T(8,128)S(1)}, s32[8]{0:T(128)S(1)}, /*index=...) while((s32[]{:T(128)}, f32[8,256]{1,0:T(8,128)S(1)}, ...), condition=%wide.region_75.76_spmd, body=%wide.region_68.75_spmd.sunk | while | flops 219279376 | bytes 9206033 | solution.py:132
  531.2 5.6 fusion.76
  544.8 5.6 fusion.76
  558.5 5.6 fusion.76
  572.1 5.6 fusion.76
  585.7 5.6 fusion.76
  599.4 5.6 fusion.76
  613.0 5.6 fusion.76
  639.2 9.2 %all-to-all-done.2 = f32[32,5,256]{2,1,0:T(8,128)S(1)} async-done(((f32[32,5,256]{2,1,0:T(8,128)}), f32[32,5,256]{2,1,0:T(8,128)S(1)}, u32[]{:S(2)}, u32[]{:S(2)}) %all-to-all-start.2) | async-done | bytes 163872 | tf_op jit(solution)/shard_map/all_to_all | solution.py:147
  652.6 8.7 %all-to-all-done.3 = f32[32,5,256]{2,1,0:T(8,128)S(1)} async-done(((f32[32,5,256]{2,1,0:T(8,128)}), f32[32,5,256]{2,1,0:T(8,128)S(1)}, u32[]{:S(2)}, u32[]{:S(2)}) %all-to-all-start.3) | async-done | bytes 163872 | tf_op jit(solution)/shard_map/all_to_all | solution.py:154
  (407 shorter events, 101.7 us)
Async XLA Ops:
  2.4 416.2 %all-to-all-start = ((s32[32,1,5]{2,1,0:T(1,128)}), s32[32,1,5]{2,1,0:T(1,128)S(1)}, u32[]{:S(2)}, u32[]{:S(2)}) async-start(s32[32,1,5]{2,1,0:T(1,128)} %bitcast.86), calls=%async_computation | async-start | bytes 32768 | tf_op jit(solution)/shard_map/all_to_all | solution.py:84
  240.4 145.2 %copy-start.1 = (s32[8192]{0:T(1024)S(1)}, s32[8192]{0:T(1024)}, u32[]{:S(2)}) copy-start(s32[8192]{0:T(1024)} %param.50) | copy-start | bytes 98308
  358.4 69.1 %copy-start.2 = (f32[1024]{0:T(1024)}, f32[1024]{0:T(1024)S(1)}, u32[]{:S(2)}) copy-start(f32[1024]{0:T(1024)S(1)} %add_multiply_fusion.3) | copy-start | bytes 12292
  374.1 44.4 %copy-start.5 = (f32[128]{0:T(128)}, f32[128]{0:T(128)S(1)}, u32[]{:S(2)}) copy-start(f32[128]{0:T(128)S(1)} %add_multiply_fusion.11) | copy-start | bytes 1540
  385.6 32.9 %copy-start = (f32[16,8192]{1,0:T(8,128)S(1)}, f32[16,8192]{1,0:T(8,128)}, u32[]{:S(2)}) copy-start(f32[16,8192]{1,0:T(8,128)} %param.48) | copy-start | bytes 1572868
  423.7 3.7 copy-start.3
  423.7 29.0 %copy-start.4 = (s32[2048]{0:T(1024)S(1)}, s32[2048]{0:T(1024)}, u32[]{:S(2)}) copy-start(s32[2048]{0:T(1024)} %param.49) | copy-start | bytes 24580
  423.7 93.2 %all-to-all-start.1 = ((f32[17,32,5,256]{3,0,2,1:T(8,128)}), f32[17,32,5,256]{3,0,2,1:T(8,128)}, u32[]{:S(2)}, u32[]{:S(2)}) async-start(f32[17,32,5,256]{3,0,2,1:T(8,128)} %pad_maximum_fusion), calls=%async_computation.1 | async-start | bytes 7864320 | tf_op jit(solution)/shard_map/all_to_all | solution.py:97
  635.4 13.0 %all-to-all-start.2 = ((f32[32,5,256]{2,1,0:T(8,128)}), f32[32,5,256]{2,1,0:T(8,128)S(1)}, u32[]{:S(2)}, u32[]{:S(2)}) async-start(f32[32,5,256]{2,1,0:T(8,128)} %copy.52), calls=%async_computation.2 | async-start | bytes 524288 | tf_op jit(solution)/shard_map/all_to_all | solution.py:147
  648.4 13.0 %all-to-all-start.3 = ((f32[32,5,256]{2,1,0:T(8,128)}), f32[32,5,256]{2,1,0:T(8,128)S(1)}, u32[]{:S(2)}, u32[]{:S(2)}) async-start(f32[32,5,256]{2,1,0:T(8,128)} %copy.53), calls=%async_computation.3 | async-start | bytes 524288 | tf_op jit(solution)/shard_map/all_to_all | solution.py:154
where the time goes:
time: 666 us; the launch traced here: 663 us
  blocking collectives  381 us (57%)
  local copies, waits for them, and re-layouts  71 us (11%)
  waiting for transfers between devices  68.8 us (10%)
  other arithmetic  54.3 us (8%)
  matrix products  47.7 us (7%)
  loops' own time  23.3 us (3%)
  starting transfers between devices  16.1 us (2%)
    all_gather x32, blocking collectives, combined_all(): everything = jax.tree.map(lambda part: lax.all_gather(part, axis), x)  344 us
    all_to_all x1, waiting for transfers between devices, on_device(): lax.all_to_all(bundle, ('row', 'col'), split_axis=1, concat_axis=1, tiled...  50.9 us
    dot_general x8, matrix products, block_terms(): jnp.einsum('fi,fkj->ikj', src_block, tgt_sel, precision=lax.Precision.HIG...  45.1 us
    gather x1, local copies, waits for them, and re-layouts, on_device(): start_g = jnp.take(all_g, tgt_cluster)  32.9 us
    all_gather x1, blocking collectives, on_device(): all_f = lax.all_gather(coarse_f, 'row', axis=0, tiled=True)  25.1 us
    another operation x1, loops' own time, on_device(): lax.map(block_terms, jnp.arange(SB_DEV, dtype=jnp.int32))  21.2 us
    reduce_sum x8, other arithmetic, block_terms(): part_sum = jnp.sum(jnp.exp(block_scores - part_max[None]), 0)  15.6 us
  transfers between devices with their start and end apart: 4, of which 3 were waited for; matrix products, arithmetic and copies ran while one was open for 10% of the time, Pallas kernels for 0%

commit v1 on v0

v1 whole, which is shorter than its diff:
```python
import functools
import math

import jax
import jax.numpy as jnp
from jax import lax
from jax.experimental import pallas as pl
from jax.experimental.pallas import tpu as pltpu
from jax.sharding import PartitionSpec as P

F = 16
BLK = 256
SUPP = 16
ITERS = 8
SB_DEV = 8
TB_DEV = 32
EPS = 0.1

SCALE = math.log2(math.e) / EPS
KDIM = 7 * F
LANES = 128
ROWS = 256
UNROLL = 2
MIB = 1024 * 1024
AXES = ("row", "col")

VMEM = pl.BlockSpec(memory_space=pltpu.VMEM)
SMEM = pl.BlockSpec(memory_space=pltpu.SMEM)
CONTRACT_FIRST = (((0,), (0,)), ((), ()))


def split3(x):
    first = x.astype(jnp.bfloat16)
    rest = x - first.astype(jnp.float32)
    second = rest.astype(jnp.bfloat16)
    rest = rest - second.astype(jnp.float32)
    return first, second, rest.astype(jnp.bfloat16)


def constant_rows(values, at, ones_at):
    width = values.shape[1]
    parts = split3(jnp.broadcast_to(values, (F, width)))
    row = lax.broadcasted_iota(jnp.int32, (F, width), 0)
    rows = jnp.zeros((F, width), jnp.float32)
    for k, part in enumerate(parts):
        rows = jnp.where(row == at + k, part.astype(jnp.float32), rows)
    if ones_at is not None:
        rows = jnp.where((row >= ones_at) & (row < ones_at + 3), 1.0, rows)
    return rows.astype(jnp.bfloat16)


def pack_left(x, constant):
    a, b, c = split3(x * (2.0 * SCALE))
    return jnp.concatenate([a, a, b, b, a, c, constant_rows(constant, 0, 3)], 0)


def pack_right(y, constant):
    a, b, c = split3(y)
    return jnp.concatenate([a, b, a, b, c, a, constant_rows(constant, 3, 0)], 0)


def contract(left, right):
    return lax.dot_general(left, right, CONTRACT_FIRST, preferred_element_type=jnp.float32)


def square_norm(x):
    return jnp.sum(x * x, 0, keepdims=True)


def fold(values, combine):
    out = values[0:8]
    for k in range(1, values.shape[0] // 8):
        out = combine(out, values[8 * k : 8 * k + 8])
    return out


def coarse_kernel(n_src, n_tgt, stored, *refs):
    src = refs[:n_src]
    tgt = refs[n_src : n_src + n_tgt]
    f_out, g_out, scores, mass, dual = refs[n_src + n_tgt :]
    ks, kt = f_out.shape[1], g_out.shape[1]
    piece = src[0].shape[1]
    tiles = kt // LANES
    y = jnp.concatenate([ref[0:F, :] for ref in tgt], 1)
    log_b = jnp.log2(jnp.concatenate([ref[F : F + 1, :] for ref in tgt], 1))
    right = pack_right(y, log_b - SCALE * square_norm(y))
    ones = jnp.ones((F, LANES), jnp.bfloat16)

    def left_of(s, k):
        span = pl.ds(pl.multiple_of(k * ROWS, ROWS), ROWS)
        x = src[s][0:F, span]
        return pack_left(x, -SCALE * square_norm(x))

    def over_chunks(body, carry):
        for s in range(n_src):

            def chunk(k, carry, s=s):
                base = pl.multiple_of(s * piece + k * ROWS, ROWS)
                return body(s, k, pl.ds(base, ROWS), carry)

            carry = lax.fori_loop(0, piece // ROWS, chunk, carry)
        return carry

    def begin(s, k, rows, largest):
        span = pl.ds(pl.multiple_of(k * ROWS, ROWS), ROWS)
        z = contract(left_of(s, k), right)
        parts = constant_rows(src[s][F : F + 1, span], 0, None)
        mass[rows, :] = contract(parts, ones)
        top = jnp.max(z, 1, keepdims=True)
        f = -(top + jnp.log2(jnp.sum(jnp.exp2(z - top), 1, keepdims=True)))
        z = z + f
        if stored:
            scores[rows, :] = z
        dual[rows, :] = jnp.broadcast_to(f, (ROWS, LANES))
        return jnp.maximum(largest, fold(z, jnp.maximum))

    def read(s, k, rows):
        if stored:
            return scores[rows, :]
        return contract(left_of(s, k), right) + jnp.tile(dual[rows, :], (1, tiles))

    largest = over_chunks(begin, jnp.full((8, kt), -jnp.inf, jnp.float32))
    largest = jnp.max(largest, 0, keepdims=True)
    zero = jnp.zeros((8, kt), jnp.float32)

    def first(s, k, rows, total):
        e = jnp.exp2(read(s, k, rows) - largest)
        return total + fold(e * jnp.tile(mass[rows, :], (1, tiles)), jnp.add)

    total = over_chunks(first, zero)
    g = log_b - (largest + jnp.log2(jnp.sum(total, 0, keepdims=True)))

    def sweep(g, rebase):
        def step(s, k, rows, total):
            z = read(s, k, rows)
            e = jnp.exp2(z + g)
            row_sum = jnp.sum(e, 1, keepdims=True)
            weight = mass[rows, :] / row_sum
            if rebase:
                shift = jnp.log2(row_sum)
                if stored:
                    scores[rows, :] = z - shift
                dual[rows, :] = dual[rows, :] - shift
            return total + fold(e * jnp.tile(weight, (1, tiles)), jnp.add)

        total = over_chunks(step, zero)
        return g + (log_b - jnp.log2(jnp.sum(total, 0, keepdims=True)))

    half = ITERS // 2
    g = lax.fori_loop(0, half - 1, lambda _, g: sweep(g, False), g)
    g = sweep(g, True)
    g = lax.fori_loop(0, ITERS - half - 2, lambda _, g: sweep(g, False), g)
    g = sweep(g, True)
    g_out[...] = g * (1.0 / SCALE)
    diagonal = lax.broadcasted_iota(jnp.int32, (LANES, LANES), 0) == lax.broadcasted_iota(
        jnp.int32, (LANES, LANES), 1
    )

    def to_lanes(k, carry):
        span = pl.ds(pl.multiple_of(k * LANES, LANES), LANES)
        picked = jnp.sum(jnp.where(diagonal, dual[span, :], 0.0), 0, keepdims=True)
        f_out[:, span] = picked * (1.0 / SCALE)
        return carry

    lax.fori_loop(0, ks // LANES, to_lanes, 0)


def coarse_duals(src, tgt):
    ks = sum(part.shape[1] for part in src)
    kt = sum(part.shape[1] for part in tgt)
    stored = ks * kt * 4 <= 16 * MIB
    return pl.pallas_call(
        functools.partial(coarse_kernel, len(src), len(tgt), stored),
        out_shape=(
            jax.ShapeDtypeStruct((1, ks), jnp.float32),
            jax.ShapeDtypeStruct((1, kt), jnp.float32),
        ),
        in_specs=[VMEM] * (len(src) + len(tgt)),
        out_specs=(VMEM, VMEM),
        scratch_shapes=[
            pltpu.VMEM((ks, kt) if stored else (8, LANES), jnp.float32),
            pltpu.VMEM((ks, LANES), jnp.float32),
            pltpu.VMEM((ks, LANES), jnp.float32),
        ],
        compiler_params=pltpu.CompilerParams(vmem_limit_bytes=48 * MIB),
        cost_estimate=pl.CostEstimate(
            flops=40 * ks * kt, bytes_accessed=4 * 24 * (ks + kt), transcendentals=9 * ks * kt
        ),
        name="coarse",
    )(*src, *tgt)


def look_up(table_ref, index):
    low = index & (LANES - 1)
    high = index >> 7
    out = jnp.zeros(index.shape, jnp.float32)
    for h in range(table_ref.shape[1] // LANES):
        row = jnp.broadcast_to(table_ref[0:1, h * LANES : (h + 1) * LANES], index.shape)
        out = jnp.where(high == h, jnp.take_along_axis(row, low, axis=1), out)
    return out


def fine_kernel(
    slots_each,
    slot_ref,
    where_ref,
    bundle,
    tgt_pts,
    tgt_cluster,
    f_table,
    g_table,
    partial_out,
    start_f_out,
    fine_g_out,
    start_f,
    start_g,
    packed,
    col_top,
    col_sum,
    col_count,
    scores_a,
    scores_b,
    order,
):
    devices = bundle.shape[0]
    me, src_flip, tgt_flip = where_ref[0], where_ref[1], where_ref[2]

    def starting_f(d, carry):
        index = bundle[d, 2 * BLK // 2 : 2 * BLK // 2 + F, :].astype(jnp.int32) ^ src_flip
        for half in range(2):
            start_f[d, 8 * half : 8 * half + 8, :] = look_up(f_table, index[8 * half : 8 * half + 8])
        return carry

    lax.fori_loop(0, devices, starting_f, 0)
    start_f_out[...] = start_f[me]
    for k in range(2 * TB_DEV // 8):
        index = tgt_cluster[8 * k : 8 * k + 8, :] ^ tgt_flip
        start_g[8 * k : 8 * k + 8, :] = look_up(g_table, index)

    def pack_target(t, carry):
        y = tgt_pts[:, pl.ds(pl.multiple_of(t * BLK, BLK), BLK)]
        g = jnp.concatenate([start_g[pl.ds(2 * t, 1), :], start_g[pl.ds(2 * t + 1, 1), :]], 1)
        packed[t] = pack_right(y, SCALE * (g - square_norm(y)))
        return carry

    lax.fori_loop(0, TB_DEV, pack_target, 0)
    packed[TB_DEV] = jnp.zeros((KDIM, BLK), jnp.bfloat16)
    col_top[...] = jnp.full(col_top.shape, -jnp.inf, jnp.float32)
    col_sum[...] = jnp.zeros(col_sum.shape, jnp.float32)
    col_count[...] = jnp.zeros(col_count.shape, jnp.float32)

    total = devices * slots_each

    def place(p, carry):
        used, unused = carry
        valid = slot_ref[p] > 0
        order[jnp.where(valid, used, unused)] = p
        step = valid.astype(jnp.int32)
        return used + step, unused - (1 - step)

    used, _ = lax.fori_loop(0, total, place, (jnp.int32(0), jnp.int32(total - 1)))

    def pair(p, scores):
        code = slot_ref[p] - 1
        valid = code >= 0
        block = jnp.where(valid, code // TB_DEV, 0)
        t = jnp.where(valid, code % TB_DEV, TB_DEV)
        d = p // slots_each
        tile = [
            [
                bundle[d, pl.ds(pl.multiple_of(half * 128 + 16 * block + 8 * k, 8), 8), :]
                for k in range(2)
            ]
            for half in range(2)
        ]
        x = jnp.concatenate([jnp.concatenate(row, 1) for row in tile], 0)
        f = jnp.concatenate(
            [start_f[d, pl.ds(2 * block + k, 1), :] for k in range(2)], 1
        )
        left = pack_left(x, SCALE * (f - square_norm(x)))
        right = packed[t]
        scores[0] = contract(left, right)
        scores[1] = contract(right, left)
        z = scores[0]
        top = jnp.max(z, 0, keepdims=True)
        mass = jnp.sum(jnp.exp2(z - top), 0, keepdims=True)
        for k in range(2):
            span = slice(k * LANES, (k + 1) * LANES)
            row = pl.ds(2 * t + k, 1)
            old = col_top[row, :]
            new = jnp.maximum(old, top[:, span])
            col_sum[row, :] = col_sum[row, :] * jnp.exp2(old - new) + mass[:, span] * jnp.exp2(
                top[:, span] - new
            )
            col_top[row, :] = new
            col_count[row, :] = col_count[row, :] + 1.0
        z = scores[1]
        top = jnp.max(z, 0, keepdims=True)
        mass = jnp.sum(jnp.exp2(z - top), 0, keepdims=True)
        partial_out[d, pl.ds(p % slots_each, 1), :] = top + jnp.log2(mass) - SCALE * f

    def pairs(n, carry):
        pair(order[UNROLL * n], scores_a)
        pair(order[UNROLL * n + 1], scores_b)
        return carry

    lax.fori_loop(0, (used + UNROLL - 1) // UNROLL, pairs, 0)
    rows = slice(0, 2 * TB_DEV)
    g = start_g[...]
    lse = (col_top[rows, :] + jnp.log2(col_sum[rows, :])) * (1.0 / SCALE) - g
    term = EPS * jnp.log(col_count[rows, :] * float(BLK)) - lse
    fine_g_out[...] = 0.5 * (g + term)


def fine_update(slots, where, bundle, tgt_pts, tgt_cluster, f_table, g_table, slots_each):
    devices = bundle.shape[0]
    return pl.pallas_call(
        functools.partial(fine_kernel, slots_each),
        out_shape=(
            jax.ShapeDtypeStruct((devices, slots_each, BLK), jnp.float32),
            jax.ShapeDtypeStruct((F, LANES), jnp.float32),
            jax.ShapeDtypeStruct((2 * TB_DEV, LANES), jnp.float32),
        ),
        in_specs=[SMEM, SMEM] + [VMEM] * 5,
        out_specs=(VMEM, VMEM, VMEM),
        scratch_shapes=[
            pltpu.VMEM((devices, F, LANES), jnp.float32),
            pltpu.VMEM((2 * TB_DEV, LANES), jnp.float32),
            pltpu.VMEM((TB_DEV + 1, KDIM, BLK), jnp.bfloat16),
            pltpu.VMEM((2 * TB_DEV + 8, LANES), jnp.float32),
            pltpu.VMEM((2 * TB_DEV + 8, LANES), jnp.float32),
            pltpu.VMEM((2 * TB_DEV + 8, LANES), jnp.float32),
            pltpu.VMEM((2, BLK, BLK), jnp.float32),
            pltpu.VMEM((2, BLK, BLK), jnp.float32),
            pltpu.SMEM((devices * slots_each,), jnp.int32),
        ],
        compiler_params=pltpu.CompilerParams(vmem_limit_bytes=48 * MIB),
        name="fine",
    )(slots, where, bundle, tgt_pts, tgt_cluster, f_table, g_table)


def finish_kernel(slots_each, slot_ref, partial, start_f, fine_f_out, gathered):
    for block in range(SB_DEV):
        for k in range(SUPP):
            slot = slot_ref[block * SUPP + k]
            gathered[k, block : block + 1, :] = partial[
                slot // slots_each, pl.ds(slot % slots_each, 1), :
            ]
    values = gathered[...]
    top = jnp.max(values, 0)
    lse = top + jnp.log2(jnp.sum(jnp.exp2(values - top[None]), 0))
    term = EPS * math.log(float(SUPP * BLK)) - lse * (1.0 / SCALE)
    for block in range(SB_DEV):
        for k in range(2):
            row = slice(2 * block + k, 2 * block + k + 1)
            piece = term[block : block + 1, k * LANES : (k + 1) * LANES]
            fine_f_out[row, :] = 0.5 * (start_f[row, :] + piece)


def finish(slot_ids, partial, start_f, slots_each):
    return pl.pallas_call(
        functools.partial(finish_kernel, slots_each),
        out_shape=jax.ShapeDtypeStruct((F, LANES), jnp.float32),
        in_specs=[SMEM, VMEM, VMEM],
        out_specs=VMEM,
        scratch_shapes=[pltpu.VMEM((SUPP, SB_DEV, BLK), jnp.float32)],
        name="finish",
    )(slot_ids, partial, start_f)


def exchange(x, axis, flip):
    count = lax.axis_size(axis)
    return lax.ppermute(x, axis, [(i, i ^ flip) for i in range(count)])


def on_device(
    src_cent, tgt_cent, src_mass, tgt_mass, src_pts, tgt_pts, src_cluster, tgt_cluster, support
):
    n_row, n_col = lax.axis_size("row"), lax.axis_size("col")
    devices = n_row * n_col
    row, col = lax.axis_index("row"), lax.axis_index("col")
    me = row * n_col + col

    requests_each = SB_DEV * SUPP
    slots_each = requests_each // devices + 1
    wanted = support.reshape(-1)
    owners = wanted // TB_DEV
    positions = jnp.arange(requests_each, dtype=jnp.int32)
    earlier = (owners[None, :] == owners[:, None]) & (positions[None, :] < positions[:, None])
    slot_ids = owners * slots_each + jnp.sum(earlier.astype(jnp.int32), 1)
    codes = (positions // SUPP) * TB_DEV + wanted % TB_DEV + 1
    width = -(-devices * slots_each // LANES) * LANES
    table = jnp.sum(
        jnp.where(slot_ids[None, :] == jnp.arange(width, dtype=jnp.int32)[:, None], codes[None, :], 0), 1
    )
    tiles = src_pts.reshape(2, 8, F, LANES).transpose(0, 2, 1, 3).reshape(2 * BLK // 2, LANES)
    table = jnp.pad(table.reshape(-1, LANES), ((0, -(width // LANES) % 8), (0, 0)))
    bundle = jnp.concatenate(
        [tiles, src_cluster.reshape(F, LANES).astype(jnp.float32), table.astype(jnp.float32)], 0
    )
    bundles = lax.all_gather(bundle, AXES)

    src_own = jnp.concatenate([src_cent, src_mass[None]], 0)
    tgt_own = jnp.concatenate([tgt_cent, tgt_mass[None]], 0)
    tgt_pair = jnp.concatenate([tgt_own, exchange(tgt_own, "col", 1)], 1)
    src_all = [src_own] + [exchange(src_own, "row", k) for k in range(1, n_row)]
    tgt_all = [tgt_pair] + [exchange(tgt_pair, "col", k) for k in range(2, n_col, 2)]
    f_table, g_table = coarse_duals(src_all, tgt_all)
    coarse_f = f_table[0, : src_cent.shape[1]]
    coarse_g = g_table[0, : tgt_cent.shape[1]]

    slots = bundles[:, 2 * BLK // 2 + F :, :].reshape(devices, -1)
    slots = lax.dynamic_slice_in_dim(slots, me * slots_each, slots_each, 1)
    slots = slots.reshape(-1).astype(jnp.int32)
    where = jnp.stack([me, row * src_cent.shape[1], col * tgt_cent.shape[1]]).astype(jnp.int32)
    partial, start_f, fine_g = fine_update(
        slots,
        where,
        bundles,
        tgt_pts,
        tgt_cluster.reshape(2 * TB_DEV, LANES),
        f_table,
        g_table,
        slots_each,
    )
    returned = lax.all_to_all(partial, AXES, split_axis=0, concat_axis=0, tiled=True)
    fine_f = finish(slot_ids, returned, start_f, slots_each)
    return coarse_f, coarse_g, fine_f.reshape(-1), fine_g.reshape(-1)


def solution(mesh):
    in_specs = (
        P(None, "row"),
        P(None, "col"),
        P("row"),
        P("col"),
        P(None, AXES),
        P(None, AXES),
        P(AXES),
        P(AXES),
        P(AXES, None),
    )
    out_specs = (P("row"), P("col"), P(AXES), P(AXES))
    return jax.shard_map(
        on_device, mesh=mesh, in_specs=in_specs, out_specs=out_specs, check_vma=False
    )
```

time: 666 us -> 143 us (0.21)
  blocking collectives: 381 us -> 0 us
  Pallas kernels: 0 us -> 81.8 us
  local copies, waits for them, and re-layouts: 71 us -> 6.51 us
  other arithmetic: 54.3 us -> 5.05 us
  matrix products: 47.7 us -> 0 us
  waiting for transfers between devices: 68.8 us -> 22.9 us
  loops' own time: 23.3 us -> 0 us
  between operations: 1.43 us -> 14.1 us
    all_gather x34 -> x0, blocking collectives: 381 us -> none  [the longest x32 344 us: combined_all(): everything = jax.tree.map(lambda part: lax.all_gather(part, axis), x)]
    pallas_call x0 -> x3, Pallas kernels: none -> 81.8 us  [the longest x1 41.2 us: coarse_duals(): pl.pallas_call(functools.partial(coarse_kernel, len(src), len(tgt), store...]
    all_to_all x4 -> x1, waiting for transfers between devices: 68.8 us -> 9.28 us  [on_device(): lax.all_to_all(partial, AXES, split_axis=0, concat_axis=0, tiled=True)]
    gather x6 -> x0, local copies, waits for them, and re-layouts: 51 us -> none  [the longest x1 32.9 us: on_device(): start_g = jnp.take(all_g, tgt_cluster)]
    dot_general x11 -> x0, matrix products: 47.7 us -> none  [the longest x8 45.1 us: block_terms(): jnp.einsum('fi,fkj->ikj', src_block, tgt_sel, precision=lax.Precision.HIG...]
    reduce_sum x46 -> x2, other arithmetic: 38.8 us -> 0.29 us  [the longest x1 0.17 us: on_device(): slot_ids = owners * slots_each + jnp.sum(earlier.astype(jnp.int32), 1)]
    another operation x17 -> x0, loops' own time: 23.3 us -> none  [the longest x1 21.2 us: on_device(): lax.map(block_terms, jnp.arange(SB_DEV, dtype=jnp.int32))]
    all_to_all x4 -> x1, starting transfers between devices: 16.1 us -> 2.9 us  [on_device(): lax.all_to_all(partial, AXES, split_axis=0, concat_axis=0, tiled=True)]
  transfers between devices with their start and end apart: 4 -> 9, of which waited for: 3 -> 5; matrix products, arithmetic and copies ran while one was open for 10% -> 2% of each run, Pallas kernels for 0% -> 29%
where the time goes in v1:
time: 143 us
  Pallas kernels  81.8 us (57%)
  waiting for transfers between devices  22.9 us (16%)
  between operations  14.1 us (10%)
  starting transfers between devices  12.4 us (9%)
  local copies, waits for them, and re-layouts  6.51 us (5%)
  other arithmetic  5.05 us (4%)
    pallas_call x1, Pallas kernels, coarse_duals(): pl.pallas_call(functools.partial(coarse_kernel, len(src), len(tgt), store...  41.2 us
    pallas_call x1, Pallas kernels, fine_update(): pl.pallas_call(functools.partial(fine_kernel, slots_each), out_shape=(jax...  38 us
    ppermute x7, starting transfers between devices, exchange(): return lax.ppermute(x, axis, [(i, i ^ flip) for i in range(count)])  9.51 us
    all_to_all x1, waiting for transfers between devices, on_device(): lax.all_to_all(partial, AXES, split_axis=0, concat_axis=0, tiled=True)  9.28 us
    all_gather x1, waiting for transfers between devices, on_device(): bundles = lax.all_gather(bundle, AXES)  7.24 us
    ppermute x7, waiting for transfers between devices, exchange(): return lax.ppermute(x, axis, [(i, i ^ flip) for i in range(count)])  6.41 us
    unnamed x13, local copies, waits for them, and re-layouts  3.62 us
    all_to_all x1, starting transfers between devices, on_device(): lax.all_to_all(partial, AXES, split_axis=0, concat_axis=0, tiled=True)  2.9 us
  transfers between devices with their start and end apart: 9, of which 5 were waited for; matrix products, arithmetic and copies ran while one was open for 2% of the time, Pallas kernels for 29%

profile of v1, /device:TPU:0, one launch (start us, length us, event | category | flops | bytes accessed | tf_op | source)
XLA Modules:
  0.0 142.9 jit_solution(974717116665492757)
XLA Ops:
  7.2 0.0 all-gather.3.cloned.1.call-start
  7.2 0.8 reshape.142
  8.0 0.2 convert_reduce_fusion
  8.2 0.0 copy-start.5
  8.2 0.1 select_reduce_fusion
  8.3 0.7 convert_bitcast_fusion
  9.0 1.6 %pad_maximum_fusion = f32[280,128]{1,0:T(8,128)} fusion(f32[8,128]{1,0:T(8,128)S(1)} %pad_convert_fusion, f32[16,128]{1,0:T(8,128)S(1)} %convert_bitcast_fusion, f32[256,128]{1,0:T(8,128)} %bitcast.29), kind=kLoop, calls=%fused_computation | loop fusion | flops 71680 | bytes 286720 | tf_op jit(solution)/shard_map/concatenate | solution.py:398
  10.6 0.0 all-gather.3.cloned.1.call-update
  10.6 0.7 pad_maximum_fusion.3
  11.3 0.5 collective-permute-start.3
  11.8 0.8 collective-permute-done.3
  12.6 0.7 pad_maximum_fusion.2.refs_4_
  13.3 2.9 %collective-permute-start.4 = (f32[17,256]{1,0:T(8,128)S(1)}, f32[17,256]{1,0:T(8,128)S(1)}, u32[]{:S(2)}, u32[]{:S(2)}) collective-permute-start(f32[17,256]{1,0:T(8,128)S(1)} %pad_maximum_fusion.2.refs_4_), channel_id=1, source_target_pairs={{0,2},{1,3},{2,0},{3,1},{4,6},{5,7},{6,4},{7,5},{8,10},{9,11},{10,... | collective-permute-start | bytes 52232 | tf_op jit(solution)/shard_map/ppermute | solution.py:373
  16.3 0.9 pad_maximum_fusion.1.refs_0_
  17.1 1.6 %collective-permute-start = (f32[17,1024]{1,0:T(8,128)S(1)}, f32[17,1024]{1,0:T(8,128)S(1)}, u32[]{:S(2)}, u32[]{:S(2)}) collective-permute-start(f32[17,1024]{1,0:T(8,128)S(1)} %pad_maximum_fusion.1.refs_0_), channel_id=1, source_target_pairs={{0,8},{8,0},{16,24},{24,16},{1,9},{9,1},{17,25},{25,17},{2,10},{10... | collective-permute-start | bytes 208904 | tf_op jit(solution)/shard_map/ppermute | solution.py:373
  18.7 1.5 %collective-permute-start.1 = (f32[17,1024]{1,0:T(8,128)S(1)}, f32[17,1024]{1,0:T(8,128)S(1)}, u32[]{:S(2)}, u32[]{:S(2)}) collective-permute-start(f32[17,1024]{1,0:T(8,128)S(1)} %pad_maximum_fusion.1.refs_0_), channel_id=1, source_target_pairs={{0,16},{8,24},{16,0},{24,8},{1,17},{9,25},{17,1},{25,9},{2,18},{10... | collective-permute-start | bytes 208904 | tf_op jit(solution)/shard_map/ppermute | solution.py:373
  20.2 0.5 collective-permute-start.2
  20.7 2.6 %collective-permute-start.5 = (f32[17,256]{1,0:T(8,128)S(1)}, f32[17,256]{1,0:T(8,128)S(1)}, u32[]{:S(2)}, u32[]{:S(2)}) collective-permute-start(f32[17,256]{1,0:T(8,128)S(1)} %pad_maximum_fusion.2.refs_4_), channel_id=1, source_target_pairs={{0,4},{1,5},{2,6},{3,7},{4,0},{5,1},{6,2},{7,3},{8,12},{9,13},{10,... | collective-permute-start | bytes 52232 | tf_op jit(solution)/shard_map/ppermute | solution.py:373
  23.3 0.0 collective-permute-done.4.refs_5_
  23.3 0.0 collective-permute-start.6
  23.3 0.1 pad_add_fusion.where_ref
  23.3 0.0 copy-start.1
  23.3 0.0 copy-start.2
  23.3 2.1 %collective-permute-done.5.refs_6_ = f32[17,256]{1,0:T(8,128)S(1)} collective-permute-done((f32[17,256]{1,0:T(8,128)S(1)}, f32[17,256]{1,0:T(8,128)S(1)}, u32[]{:S(2)}, u32[]{:S(2)}) %collective-permute-start.5) | collective-permute-done | bytes 17440 | tf_op jit(solution)/shard_map/ppermute | solution.py:373
  25.4 3.5 %collective-permute-done.6.refs_7_ = f32[17,256]{1,0:T(8,128)S(1)} collective-permute-done((f32[17,256]{1,0:T(8,128)S(1)}, f32[17,256]{1,0:T(8,128)S(1)}, u32[]{:S(2)}, u32[]{:S(2)}) %collective-permute-start.6) | collective-permute-done | bytes 17440 | tf_op jit(solution)/shard_map/ppermute | solution.py:373
  28.9 0.0 collective-permute-done.refs_1_
  28.9 0.0 collective-permute-done.1.refs_2_
  28.9 0.0 collective-permute-done.2.refs_3_
  28.9 41.2 %coarse.1 = (f32[1,4096]{1,0:T(1,128)S(1)}, f32[1,1024]{1,0:T(1,128)S(1)}) custom-call(f32[17,1024]{1,0:T(8,128)S(1)} %pad_maximum_fusion.1.refs_0_, f32[17,1024]{1,0:T(8,128)S(1)} %collective-permute-done.refs_1_, f32[17,1024]{1,0:T(8,128)S(1)} %collective-permute-done.1.refs_2_, f32[17,1024]{1,0:T(8,128)S(1)} %collective-permute-done.2.refs_3_, ...), custom_call_target="tpu_custom_call" | custom-call | flops 167772160 | bytes 491520 | tf_op jit(solution)/shard_map/coarse/pallas_call | solution.py:172
  70.2 0.0 copy-done.5
  70.2 7.2 %all-gather.3.cloned.1.call-done = f32[8960,128]{1,0:T(8,128)} async-done(((f32[280,128]{1,0:T(8,128)}), f32[8960,128]{1,0:T(8,128)}) %all-gather.3.cloned.1.call-update) | async-done | bytes 4587536 | tf_op jit(solution)/shard_map/all_gather | solution.py:401
  77.4 0.9 slice.12
  78.4 0.1 dynamic-slice_convert_fusion
  78.5 0.1 convert_element_type.22.slot_ref
  78.6 0.0 copy-done.1
  78.6 0.0 copy-done.2
  78.6 0.0 copy-start
  78.6 2.3 %copy-done = f32[8960,128]{1,0:T(8,128)S(1)} copy-done((f32[8960,128]{1,0:T(8,128)S(1)}, f32[8960,128]{1,0:T(8,128)}, u32[]{:S(2)}) %copy-start) | copy-done | bytes 4587544
  80.9 38.0 %fine.1 = (f32[32,5,256]{2,1,0:T(8,128)}, f32[16,128]{1,0:T(8,128)S(1)}, f32[64,128]{1,0:T(8,128)}) custom-call(s32[160]{0:T(256)S(1)} %convert_element_type.22.slot_ref, s32[3]{0:T(128)S(1)} %pad_add_fusion.where_ref, f32[32,280,128]{2,1,0:T(8,128)S(1)} %bitcast.25, f32[16,8192]{1,0:T(8,128)S(1)} %copy-done.1, s32[64,128]{1,0:T(8,128)S(1)} %bitcast.26, ...), custom_call_target="tpu_custom_call" | custom-call | tf_op jit(solution)/shard_map/fine/pallas_call | solution.py:317
  118.8 0.0 copy-start.3
  118.8 0.6 copy-done.3
  119.4 2.9 %all-to-all-start = ((f32[32,5,256]{2,1,0:T(8,128)}), f32[32,5,256]{2,1,0:T(8,128)S(1)}, u32[]{:S(2)}, u32[]{:S(2)}) async-start(f32[32,5,256]{2,1,0:T(8,128)} %get-tuple-element.11), calls=%async_computation | async-start | bytes 524288 | tf_op jit(solution)/shard_map/all_to_all | solution.py:426
  122.3 0.6 slice.9
  122.9 0.5 slice_bitcast_fusion
  123.5 9.3 %all-to-all-done.partial = f32[32,5,256]{2,1,0:T(8,128)S(1)} async-done(((f32[32,5,256]{2,1,0:T(8,128)}), f32[32,5,256]{2,1,0:T(8,128)S(1)}, u32[]{:S(2)}, u32[]{:S(2)}) %all-to-all-start) | async-done | bytes 163872 | tf_op jit(solution)/shard_map/all_to_all | solution.py:426
  132.7 0.0 copy-start.4
  132.7 0.7 copy-done.4
  133.4 2.6 %finish.1 = f32[16,128]{1,0:T(8,128)} custom-call(s32[128]{0:T(128)} %copy-done.5, f32[32,5,256]{2,1,0:T(8,128)} %copy-done.4, f32[16,128]{1,0:T(8,128)} %copy-done.3), custom_call_target="tpu_custom_call" | custom-call | tf_op jit(solution)/shard_map/finish/pallas_call | solution.py:361
  (4 shorter events, 0.1 us)
Async XLA Ops:
  7.2 70.3 %all-gather.3.cloned.1.call-start = ((), (), s32[]{:S(2)}) async-start(), calls=%async_computation.1 | async-start | bytes 4730880 | tf_op jit(solution)/shard_map/all_gather | solution.py:401
  8.2 62.0 %copy-start.5 = (s32[128]{0:T(128)}, s32[128]{0:T(128)S(1)}, u32[]{:S(2)}) copy-start(s32[128]{0:T(128)S(1)} %multiply_add_fusion.slot_ref) | copy-start | bytes 1540
  11.3 1.3 collective-permute-start.3
  13.3 9.9 %collective-permute-start.4 = (f32[17,256]{1,0:T(8,128)S(1)}, f32[17,256]{1,0:T(8,128)S(1)}, u32[]{:S(2)}, u32[]{:S(2)}) collective-permute-start(f32[17,256]{1,0:T(8,128)S(1)} %pad_maximum_fusion.2.refs_4_), channel_id=1, source_target_pairs={{0,2},{1,3},{2,0},{3,1},{4,6},{5,7},{6,4},{7,5},{8,10},{9,11},{10,... | collective-permute-start | bytes 52232 | tf_op jit(solution)/shard_map/ppermute | solution.py:373
  17.1 11.8 %collective-permute-start = (f32[17,1024]{1,0:T(8,128)S(1)}, f32[17,1024]{1,0:T(8,128)S(1)}, u32[]{:S(2)}, u32[]{:S(2)}) collective-permute-start(f32[17,1024]{1,0:T(8,128)S(1)} %pad_maximum_fusion.1.refs_0_), channel_id=1, source_target_pairs={{0,8},{8,0},{16,24},{24,16},{1,9},{9,1},{17,25},{25,17},{2,10},{10... | collective-permute-start | bytes 208904 | tf_op jit(solution)/shard_map/ppermute | solution.py:373
  18.7 10.2 %collective-permute-start.1 = (f32[17,1024]{1,0:T(8,128)S(1)}, f32[17,1024]{1,0:T(8,128)S(1)}, u32[]{:S(2)}, u32[]{:S(2)}) collective-permute-start(f32[17,1024]{1,0:T(8,128)S(1)} %pad_maximum_fusion.1.refs_0_), channel_id=1, source_target_pairs={{0,16},{8,24},{16,0},{24,8},{1,17},{9,25},{17,1},{25,9},{2,18},{10... | collective-permute-start | bytes 208904 | tf_op jit(solution)/shard_map/ppermute | solution.py:373
  20.2 8.7 %collective-permute-start.2 = (f32[17,1024]{1,0:T(8,128)S(1)}, f32[17,1024]{1,0:T(8,128)S(1)}, u32[]{:S(2)}, u32[]{:S(2)}) collective-permute-start(f32[17,1024]{1,0:T(8,128)S(1)} %pad_maximum_fusion.1.refs_0_), channel_id=1, source_target_pairs={{0,24},{8,16},{16,8},{24,0},{1,25},{9,17},{17,9},{25,1},{2,26},{10... | collective-permute-start | bytes 208904 | tf_op jit(solution)/shard_map/ppermute | solution.py:373
  20.7 4.7 %collective-permute-start.5 = (f32[17,256]{1,0:T(8,128)S(1)}, f32[17,256]{1,0:T(8,128)S(1)}, u32[]{:S(2)}, u32[]{:S(2)}) collective-permute-start(f32[17,256]{1,0:T(8,128)S(1)} %pad_maximum_fusion.2.refs_4_), channel_id=1, source_target_pairs={{0,4},{1,5},{2,6},{3,7},{4,0},{5,1},{6,2},{7,3},{8,12},{9,13},{10,... | collective-permute-start | bytes 52232 | tf_op jit(solution)/shard_map/ppermute | solution.py:373
  23.3 5.6 %collective-permute-start.6 = (f32[17,256]{1,0:T(8,128)S(1)}, f32[17,256]{1,0:T(8,128)S(1)}, u32[]{:S(2)}, u32[]{:S(2)}) collective-permute-start(f32[17,256]{1,0:T(8,128)S(1)} %pad_maximum_fusion.2.refs_4_), channel_id=1, source_target_pairs={{0,6},{1,7},{2,4},{3,5},{4,2},{5,3},{6,0},{7,1},{8,14},{9,15},{10,... | collective-permute-start | bytes 52232 | tf_op jit(solution)/shard_map/ppermute | solution.py:373
  23.3 55.2 %copy-start.1 = (f32[16,8192]{1,0:T(8,128)S(1)}, f32[16,8192]{1,0:T(8,128)}, u32[]{:S(2)}) copy-start(f32[16,8192]{1,0:T(8,128)} %tgt_pts.1) | copy-start | bytes 1572868
  23.3 55.2 %copy-start.2 = (s32[8192]{0:T(1024)S(1)}, s32[8192]{0:T(1024)}, u32[]{:S(2)}) copy-start(s32[8192]{0:T(1024)} %param.16) | copy-start | bytes 98308
  78.6 2.3 %copy-start = (f32[8960,128]{1,0:T(8,128)S(1)}, f32[8960,128]{1,0:T(8,128)}, u32[]{:S(2)}) copy-start(f32[8960,128]{1,0:T(8,128)} %all-gather.3.cloned.1.call-done) | copy-start | bytes 13762564
  118.8 0.6 copy-start.3
  119.4 13.3 %all-to-all-start = ((f32[32,5,256]{2,1,0:T(8,128)}), f32[32,5,256]{2,1,0:T(8,128)S(1)}, u32[]{:S(2)}, u32[]{:S(2)}) async-start(f32[32,5,256]{2,1,0:T(8,128)} %get-tuple-element.11), calls=%async_computation | async-start | bytes 524288 | tf_op jit(solution)/shard_map/all_to_all | solution.py:426
  132.7 0.7 copy-start.4
Sparse Core Ops, SparseCore 0:
  10.9 66.5 all-gather.2

commit v2 on v1

--- a/solution.py
+++ b/solution.py
@@ -20,7 +20,14 @@
 KDIM = 7 * F
 LANES = 128
 ROWS = 256
-UNROLL = 2
+ROWS_PRODUCT = 1024
+ROWS_BEGIN = 1024
+ROWS_TURN = 512
+PAIRS = 16
+BLOCKS = 8
+LOW = 2.0**-30
+SMALL = 2.0**-80
+LARGE = 2.0**100
 MIB = 1024 * 1024
 AXES = ("row", "col")
 
@@ -77,93 +84,141 @@
 def coarse_kernel(n_src, n_tgt, stored, *refs):
     src = refs[:n_src]
     tgt = refs[n_src : n_src + n_tgt]
-    f_out, g_out, scores, mass, dual = refs[n_src + n_tgt :]
+    f_out, g_out, kernel, mass, dual, sums = refs[n_src + n_tgt :]
     ks, kt = f_out.shape[1], g_out.shape[1]
     piece = src[0].shape[1]
     tiles = kt // LANES
     y = jnp.concatenate([ref[0:F, :] for ref in tgt], 1)
-    log_b = jnp.log2(jnp.concatenate([ref[F : F + 1, :] for ref in tgt], 1))
-    right = pack_right(y, log_b - SCALE * square_norm(y))
+    b = jnp.concatenate([ref[F : F + 1, :] for ref in tgt], 1)
+    right = pack_right(y, jnp.log2(b) - SCALE * square_norm(y))
     ones = jnp.ones((F, LANES), jnp.bfloat16)
-
-    def left_of(s, k):
-        span = pl.ds(pl.multiple_of(k * ROWS, ROWS), ROWS)
-        x = src[s][0:F, span]
-        return pack_left(x, -SCALE * square_norm(x))
-
-    def over_chunks(body, carry):
+    zero = jnp.zeros((8, kt), jnp.float32)
+    high = jnp.full((8, LANES), jnp.inf, jnp.float32)
+
+    def wide(values):
+        return jnp.tile(values, (1, tiles))
+
+    def over_sources(size, body, carry):
         for s in range(n_src):
 
             def chunk(k, carry, s=s):
-                base = pl.multiple_of(s * piece + k * ROWS, ROWS)
-                return body(s, k, pl.ds(base, ROWS), carry)
-
-            carry = lax.fori_loop(0, piece // ROWS, chunk, carry)
+                span = pl.ds(pl.multiple_of(k * size, size), size)
+                rows = pl.ds(pl.multiple_of(s * piece + k * size, size), size)
+                x = src[s][0:F, span]
+                left = pack_left(x, -SCALE * square_norm(x))
+                return body(src[s][F : F + 1, span], rows, left, carry)
+
+            carry = lax.fori_loop(0, piece // size, chunk, carry)
         return carry
 
-    def begin(s, k, rows, largest):
-        span = pl.ds(pl.multiple_of(k * ROWS, ROWS), ROWS)
-        z = contract(left_of(s, k), right)
-        parts = constant_rows(src[s][F : F + 1, span], 0, None)
-        mass[rows, :] = contract(parts, ones)
+    def over_rows(size, body, carry):
+        def chunk(k, carry):
+            return body(pl.ds(pl.multiple_of(k * size, size), size), carry)
+
+        return lax.fori_loop(0, ks // size, chunk, carry)
+
+    def weigh(e, weighted, rows, carry):
+        total, least = carry
+        row_sum = jnp.broadcast_to(jnp.sum(weighted, 1, keepdims=True), (e.shape[0], LANES))
+        sums[rows, :] = row_sum
+        weight = mass[rows, :] / row_sum
+        return total + fold(e * wide(weight), jnp.add), jnp.minimum(least, fold(row_sum, jnp.minimum))
+
+    def close(total, least):
+        total = jnp.sum(total, 0, keepdims=True)
+        small = jnp.minimum(jnp.min(total), jnp.min(least)) < LOW
+        return b / total, small.astype(jnp.int32)
+
+    def spread_mass(values, rows, left, carry):
+        mass[rows, :] = contract(constant_rows(values, 0, None), ones)
+        if stored:
+            kernel[rows, :] = contract(left, right)
+        return carry
+
+    over_sources(ROWS_PRODUCT, spread_mass, 0)
+
+    def begin_rows(z, rows, carry):
         top = jnp.max(z, 1, keepdims=True)
-        f = -(top + jnp.log2(jnp.sum(jnp.exp2(z - top), 1, keepdims=True)))
-        z = z + f
+        dual[rows, :] = jnp.broadcast_to(-top, (z.shape[0], LANES))
+        e = jnp.exp2(z - top)
         if stored:
-            scores[rows, :] = z
-        dual[rows, :] = jnp.broadcast_to(f, (ROWS, LANES))
-        return jnp.maximum(largest, fold(z, jnp.maximum))
-
-    def read(s, k, rows):
-        if stored:
-            return scores[rows, :]
-        return contract(left_of(s, k), right) + jnp.tile(dual[rows, :], (1, tiles))
-
-    largest = over_chunks(begin, jnp.full((8, kt), -jnp.inf, jnp.float32))
-    largest = jnp.max(largest, 0, keepdims=True)
-    zero = jnp.zeros((8, kt), jnp.float32)
-
-    def first(s, k, rows, total):
-        e = jnp.exp2(read(s, k, rows) - largest)
-        return total + fold(e * jnp.tile(mass[rows, :], (1, tiles)), jnp.add)
-
-    total = over_chunks(first, zero)
-    g = log_b - (largest + jnp.log2(jnp.sum(total, 0, keepdims=True)))
-
-    def sweep(g, rebase):
-        def step(s, k, rows, total):
-            z = read(s, k, rows)
-            e = jnp.exp2(z + g)
-            row_sum = jnp.sum(e, 1, keepdims=True)
-            weight = mass[rows, :] / row_sum
-            if rebase:
-                shift = jnp.log2(row_sum)
-                if stored:
-                    scores[rows, :] = z - shift
-                dual[rows, :] = dual[rows, :] - shift
-            return total + fold(e * jnp.tile(weight, (1, tiles)), jnp.add)
-
-        total = over_chunks(step, zero)
-        return g + (log_b - jnp.log2(jnp.sum(total, 0, keepdims=True)))
-
-    half = ITERS // 2
-    g = lax.fori_loop(0, half - 1, lambda _, g: sweep(g, False), g)
-    g = sweep(g, True)
-    g = lax.fori_loop(0, ITERS - half - 2, lambda _, g: sweep(g, False), g)
-    g = sweep(g, True)
-    g_out[...] = g * (1.0 / SCALE)
+            kernel[rows, :] = e
+        return weigh(e, e, rows, carry)
+
+    if stored:
+        carry = over_rows(ROWS_BEGIN, lambda rows, c: begin_rows(kernel[rows, :], rows, c), (zero, high))
+    else:
+        carry = over_sources(ROWS, lambda _, rows, left, c: begin_rows(contract(left, right), rows, c), (zero, high))
+    scale, small = close(*carry)
+    base = jnp.zeros((1, kt), jnp.float32)
+
+    def rescue(base, scale):
+        def rebase(rows, carry):
+            dual[rows, :] = dual[rows, :] - jnp.log2(sums[rows, :])
+            return carry
+
+        over_rows(ROWS, rebase, 0)
+
+        def tops(_, rows, left, top):
+            return jnp.maximum(top, fold(contract(left, right) + wide(dual[rows, :]), jnp.maximum))
+
+        top = jnp.max(over_sources(ROWS, tops, zero - jnp.inf), 0, keepdims=True)
+
+        def step(_, rows, left, total):
+            e = jnp.exp2(contract(left, right) + wide(dual[rows, :]) - top)
+            return total + fold(e * wide(mass[rows, :]), jnp.add)
+
+        total = jnp.sum(over_sources(ROWS, step, zero), 0, keepdims=True)
+        over_rows(ROWS, unit, 0)
+        return jnp.log2(b) - (top + jnp.log2(total)), jnp.ones_like(scale)
+
+    def unit(rows, carry):
+        sums[rows, :] = jnp.ones((ROWS, LANES), jnp.float32)
+        return carry
+
+    base, scale = lax.cond(small > 0, rescue, lambda base, scale: (base, scale), base, scale)
+
+    def renew(base, scale):
+        base = base + jnp.log2(scale)
+
+        def step(_, rows, left, carry):
+            f = dual[rows, :] - jnp.log2(sums[rows, :])
+            dual[rows, :] = f
+            e = jnp.exp2(contract(left, right) + wide(f) + base)
+            if stored:
+                kernel[rows, :] = e
+            return weigh(e, e, rows, carry)
+
+        scale, small = close(*over_sources(ROWS, step, (zero, high)))
+        return base, scale, small
+
+    def reuse(base, scale):
+        def step(rows, carry):
+            e = kernel[rows, :]
+            return weigh(e, e * scale, rows, carry)
+
+        scale, small = close(*over_rows(ROWS_TURN, step, (zero, high)))
+        return base, scale, small
+
+    def turn(_, state):
+        base, scale, small = state
+        if not stored:
+            return renew(base, scale)
+        return lax.cond(small > 0, renew, reuse, base, scale)
+
+    base, scale, small = lax.fori_loop(1, ITERS, turn, (base, scale, small))
+    g_out[...] = (base + jnp.log2(scale)) * (1.0 / SCALE)
     diagonal = lax.broadcasted_iota(jnp.int32, (LANES, LANES), 0) == lax.broadcasted_iota(
         jnp.int32, (LANES, LANES), 1
     )
 
     def to_lanes(k, carry):
         span = pl.ds(pl.multiple_of(k * LANES, LANES), LANES)
-        picked = jnp.sum(jnp.where(diagonal, dual[span, :], 0.0), 0, keepdims=True)
-        f_out[:, span] = picked * (1.0 / SCALE)
+        f = dual[span, :] - jnp.log2(sums[span, :])
+        f_out[:, span] = jnp.sum(jnp.where(diagonal, f, 0.0), 0, keepdims=True) * (1.0 / SCALE)
         return carry
 
     lax.fori_loop(0, ks // LANES, to_lanes, 0)
-
 
 def coarse_duals(src, tgt):
     ks = sum(part.shape[1] for part in src)
@@ -181,6 +236,7 @@
             pltpu.VMEM((ks, kt) if stored else (8, LANES), jnp.float32),
             pltpu.VMEM((ks, LANES), jnp.float32),
             pltpu.VMEM((ks, LANES), jnp.float32),
+            pltpu.VMEM((ks, LANES), jnp.float32),
         ],
         compiler_params=pltpu.CompilerParams(vmem_limit_bytes=48 * MIB),
         cost_estimate=pl.CostEstimate(
@@ -200,39 +256,16 @@
     return out
 
 
-def fine_kernel(
-    slots_each,
-    slot_ref,
-    where_ref,
-    bundle,
-    tgt_pts,
-    tgt_cluster,
-    f_table,
-    g_table,
-    partial_out,
-    start_f_out,
-    fine_g_out,
-    start_f,
-    start_g,
-    packed,
-    col_top,
-    col_sum,
-    col_count,
-    scores_a,
-    scores_b,
-    order,
-):
+def fine_kernel(slots_each, slot_ref, where_ref, bundle, tgt_pts, tgt_cluster, f_table, g_table,
+    partial_out, start_f_out, fine_g_out,
+    start_g, packed, col_sum, col_top, order, count):
     devices = bundle.shape[0]
     me, src_flip, tgt_flip = where_ref[0], where_ref[1], where_ref[2]
 
-    def starting_f(d, carry):
-        index = bundle[d, 2 * BLK // 2 : 2 * BLK // 2 + F, :].astype(jnp.int32) ^ src_flip
-        for half in range(2):
-            start_f[d, 8 * half : 8 * half + 8, :] = look_up(f_table, index[8 * half : 8 * half + 8])
-        return carry
-
-    lax.fori_loop(0, devices, starting_f, 0)
-    start_f_out[...] = start_f[me]
+    index = bundle[me, 2 * LANES : 2 * LANES + F, :].astype(jnp.int32) ^ src_flip
+    for half in range(2):
+        rows = slice(8 * half, 8 * half + 8)
+        start_f_out[rows, :] = look_up(f_table, index[rows])
     for k in range(2 * TB_DEV // 8):
         index = tgt_cluster[8 * k : 8 * k + 8, :] ^ tgt_flip
         start_g[8 * k : 8 * k + 8, :] = look_up(g_table, index)
@@ -240,77 +273,136 @@
     def pack_target(t, carry):
         y = tgt_pts[:, pl.ds(pl.multiple_of(t * BLK, BLK), BLK)]
         g = jnp.concatenate([start_g[pl.ds(2 * t, 1), :], start_g[pl.ds(2 * t + 1, 1), :]], 1)
-        packed[t] = pack_right(y, SCALE * (g - square_norm(y)))
+        rows = pack_right(y, SCALE * (g - square_norm(y)))
+        rows = jnp.concatenate([rows, jnp.zeros((LANES - KDIM, BLK), jnp.bfloat16)], 0)
+        packed[t] = jnp.transpose(rows.astype(jnp.float32)).astype(jnp.bfloat16)
+        count[t] = 0
         return carry
 
-    lax.fori_loop(0, TB_DEV, pack_target, 0)
-    packed[TB_DEV] = jnp.zeros((KDIM, BLK), jnp.bfloat16)
-    col_top[...] = jnp.full(col_top.shape, -jnp.inf, jnp.float32)
-    col_sum[...] = jnp.zeros(col_sum.shape, jnp.float32)
-    col_count[...] = jnp.zeros(col_count.shape, jnp.float32)
+    lax.fori_loop(0, TB_DEV, pack_target, 0, unroll=BLOCKS)
+    packed[TB_DEV] = jnp.zeros((BLK, LANES), jnp.bfloat16)
+    count[TB_DEV] = 0
 
     total = devices * slots_each
+    unroll = math.gcd(PAIRS, total)
 
     def place(p, carry):
         used, unused = carry
-        valid = slot_ref[p] > 0
+        code = slot_ref[p]
+        valid = code > 0
         order[jnp.where(valid, used, unused)] = p
+        t = jnp.where(valid, (code - 1) % TB_DEV, TB_DEV)
+        count[t] = count[t] + 1
         step = valid.astype(jnp.int32)
         return used + step, unused - (1 - step)
 
-    used, _ = lax.fori_loop(0, total, place, (jnp.int32(0), jnp.int32(total - 1)))
-
-    def pair(p, scores):
+    used, _ = lax.fori_loop(0, total, place, (jnp.int32(0), jnp.int32(total - 1)), unroll=16)
+
+    def cluster_rows(p):
+        code = slot_ref[p] - 1
+        block = jnp.where(code >= 0, code // TB_DEV, 0)
+        d = p // slots_each
+        return [bundle[d, pl.ds(2 * LANES + 2 * block + k, 1), :] for k in range(2)]
+
+    def starts(ps):
+        out = []
+        for n in range(0, len(ps), 4):
+            rows = jnp.concatenate([r for p in ps[n:n+4] for r in cluster_rows(p)], 0)
+            f = look_up(f_table, rows.astype(jnp.int32) ^ src_flip)
+            for m in range(len(ps[n:n+4])):
+                out.append(jnp.concatenate([f[2*m:2*m+1], f[2*m+1:2*m+2]], 1))
+        return out
+
+    def product(p, f):
         code = slot_ref[p] - 1
         valid = code >= 0
         block = jnp.where(valid, code // TB_DEV, 0)
         t = jnp.where(valid, code % TB_DEV, TB_DEV)
         d = p // slots_each
-        tile = [
-            [
-                bundle[d, pl.ds(pl.multiple_of(half * 128 + 16 * block + 8 * k, 8), 8), :]
-                for k in range(2)
-            ]
-            for half in range(2)
-        ]
+        tile = [[bundle[d, pl.ds(pl.multiple_of(half * LANES + 16 * block + 8 * k, 8), 8), :] for k in range(2)] for half in range(2)]
         x = jnp.concatenate([jnp.concatenate(row, 1) for row in tile], 0)
-        f = jnp.concatenate(
-            [start_f[d, pl.ds(2 * block + k, 1), :] for k in range(2)], 1
-        )
         left = pack_left(x, SCALE * (f - square_norm(x)))
-        right = packed[t]
-        scores[0] = contract(left, right)
-        scores[1] = contract(right, left)
-        z = scores[0]
-        top = jnp.max(z, 0, keepdims=True)
-        mass = jnp.sum(jnp.exp2(z - top), 0, keepdims=True)
+        left = jnp.concatenate([left, jnp.zeros((LANES - KDIM, BLK), jnp.bfloat16)], 0)
+        z = jnp.dot(packed[t], left, preferred_element_type=jnp.float32)
+        return t, d, SCALE * f, z
+
+    def put(p, d, value):
+        partial_out[d, pl.ds(p % slots_each, 1), :] = value
+
+    def fill(ref, value):
+        def body(t, carry):
+            ref[t] = jnp.full(ref.shape[1:], value, jnp.float32)
+            return carry
+        lax.fori_loop(0, ref.shape[0], body, 0)
+
+    def pair(p, f, least, most):
+        t, d, f, z = product(p, f)
+        e = jnp.exp2(z)
+        row = fold(e, jnp.add)
+        col_sum[t] = col_sum[t] + (e[:, :LANES] + e[:, LANES:])
+        row = jnp.sum(row, 0, keepdims=True)
+        put(p, d, jnp.log2(row) - f)
+        return jnp.minimum(least, row), jnp.maximum(most, row)
+
+    def pairs(n, carry):
+        ps = [order[unroll * n + u] for u in range(unroll)]
+        fs = starts(ps)
+        for u in range(unroll):
+            carry = pair(ps[u], fs[u], *carry)
+        return carry
+
+    def lanes(t, carry):
+        least, most = carry
+        g = start_g[pl.ds(pl.multiple_of(2 * t, 2), 2), :]
+        halves = []
         for k in range(2):
-            span = slice(k * LANES, (k + 1) * LANES)
-            row = pl.ds(2 * t + k, 1)
-            old = col_top[row, :]
-            new = jnp.maximum(old, top[:, span])
-            col_sum[row, :] = col_sum[row, :] * jnp.exp2(old - new) + mass[:, span] * jnp.exp2(
-                top[:, span] - new
-            )
-            col_top[row, :] = new
-            col_count[row, :] = col_count[row, :] + 1.0
-        z = scores[1]
-        top = jnp.max(z, 0, keepdims=True)
-        mass = jnp.sum(jnp.exp2(z - top), 0, keepdims=True)
-        partial_out[d, pl.ds(p % slots_each, 1), :] = top + jnp.log2(mass) - SCALE * f
-
-    def pairs(n, carry):
-        pair(order[UNROLL * n], scores_a)
-        pair(order[UNROLL * n + 1], scores_b)
-        return carry
-
-    lax.fori_loop(0, (used + UNROLL - 1) // UNROLL, pairs, 0)
-    rows = slice(0, 2 * TB_DEV)
-    g = start_g[...]
-    lse = (col_top[rows, :] + jnp.log2(col_sum[rows, :])) * (1.0 / SCALE) - g
-    term = EPS * jnp.log(col_count[rows, :] * float(BLK)) - lse
-    fine_g_out[...] = 0.5 * (g + term)
-
+            block = col_sum[t, k * LANES : (k + 1) * LANES, :]
+            halves.append(jnp.sum(jnp.transpose(block), 0, keepdims=True))
+        s = jnp.concatenate(halves, 0)
+        named = jnp.full((2, LANES), count[t].astype(jnp.float32) * float(BLK))
+        term = EPS * jnp.log(named) - (jnp.log2(s) * (1.0 / SCALE) - g)
+        fine_g_out[pl.ds(pl.multiple_of(2 * t, 2), 2), :] = 0.5 * (g + term)
+        return jnp.minimum(least, s), jnp.maximum(most, s)
+
+    fill(col_sum, 0.0)
+    least = jnp.full((1, BLK), jnp.inf, jnp.float32)
+    least, most = lax.fori_loop(0, (used + unroll - 1) // unroll, pairs, (least, jnp.zeros((1, BLK), jnp.float32)))
+    low, high = jnp.full((2, LANES), jnp.inf, jnp.float32), jnp.zeros((2, LANES), jnp.float32)
+    low, high = lax.fori_loop(0, TB_DEV, lanes, (low, high), unroll=BLOCKS)
+    fits = (jnp.minimum(jnp.min(least), jnp.min(low)) >= SMALL) & (jnp.maximum(jnp.max(most), jnp.max(high)) <= LARGE)
+
+    @pl.when(jnp.logical_not(fits))
+    def _():
+        fill(col_sum, 0.0)
+        fill(col_top, -1e30)
+
+        def pair(n, carry):
+            p = order[n]
+            t, d, f, z = product(p, starts([p])[0])
+            top = jnp.max(z, 0, keepdims=True)
+            put(p, d, top + jnp.log2(jnp.sum(jnp.exp2(z - top), 0, keepdims=True)) - f)
+            a, b = z[:, :LANES], z[:, LANES:]
+            old = col_top[t]
+            new = jnp.maximum(old, jnp.maximum(a, b))
+            col_sum[t] = col_sum[t] * jnp.exp2(old - new) + (jnp.exp2(a - new) + jnp.exp2(b - new))
+            col_top[t] = new
+            return carry
+
+        lax.fori_loop(0, used, pair, 0)
+
+        def lanes(t, carry):
+            for k in range(2):
+                rows = slice(k * LANES, (k + 1) * LANES)
+                top = jnp.transpose(col_top[t, rows, :])
+                most = jnp.max(top, 0, keepdims=True)
+                s = jnp.sum(jnp.transpose(col_sum[t, rows, :]) * jnp.exp2(top - most), 0, keepdims=True)
+                g = start_g[pl.ds(2 * t + k, 1), :]
+                named = jnp.full((1, LANES), count[t].astype(jnp.float32) * float(BLK))
+                term = EPS * jnp.log(named) - ((most + jnp.log2(s)) * (1.0 / SCALE) - g)
+                fine_g_out[pl.ds(2 * t + k, 1), :] = 0.5 * (g + term)
+            return carry
+
+        lax.fori_loop(0, TB_DEV, lanes, 0)
 
 def fine_update(slots, where, bundle, tgt_pts, tgt_cluster, f_table, g_table, slots_each):
     devices = bundle.shape[0]
@@ -324,15 +416,12 @@
         in_specs=[SMEM, SMEM] + [VMEM] * 5,
         out_specs=(VMEM, VMEM, VMEM),
         scratch_shapes=[
-            pltpu.VMEM((devices, F, LANES), jnp.float32),
             pltpu.VMEM((2 * TB_DEV, LANES), jnp.float32),
-            pltpu.VMEM((TB_DEV + 1, KDIM, BLK), jnp.bfloat16),
-            pltpu.VMEM((2 * TB_DEV + 8, LANES), jnp.float32),
-            pltpu.VMEM((2 * TB_DEV + 8, LANES), jnp.float32),
-            pltpu.VMEM((2 * TB_DEV + 8, LANES), jnp.float32),
-            pltpu.VMEM((2, BLK, BLK), jnp.float32),
-            pltpu.VMEM((2, BLK, BLK), jnp.float32),
+            pltpu.VMEM((TB_DEV + 1, BLK, LANES), jnp.bfloat16),
+            pltpu.VMEM((TB_DEV + 1, BLK, LANES), jnp.float32),
+            pltpu.VMEM((TB_DEV + 1, BLK, LANES), jnp.float32),
             pltpu.SMEM((devices * slots_each,), jnp.int32),
+            pltpu.SMEM((TB_DEV + 1,), jnp.int32),
         ],
         compiler_params=pltpu.CompilerParams(vmem_limit_bytes=48 * MIB),
         name="fine",

time: 143 us -> 174 us (1.22)
  Pallas kernels: 81.8 us -> 118 us
  waiting for transfers between devices: 22.9 us -> 17.6 us
    pallas_call x1, Pallas kernels: 38 us -> 69 us  [fine_update(): pl.pallas_call(functools.partial(fine_kernel, slots_each), out_shape=(jax...]
    all_gather x1, waiting for transfers between devices: 7.24 us -> 1.95 us  [on_device(): bundles = lax.all_gather(bundle, AXES)]
    pallas_call x1, Pallas kernels: 41.2 us -> 46.5 us  [coarse_duals(): pl.pallas_call(functools.partial(coarse_kernel, len(src), len(tgt), store...]
  transfers between devices with their start and end apart: 9 -> 9, of which waited for: 5 -> 5; matrix products, arithmetic and copies ran while one was open for 2% -> 2% of each run, Pallas kernels for 29% -> 27%
where the time goes in v2:
time: 174 us
  Pallas kernels  118 us (68%)
  waiting for transfers between devices  17.6 us (10%)
  between operations  14.1 us (8%)
  starting transfers between devices  12.5 us (7%)
  local copies, waits for them, and re-layouts  6.51 us (4%)
  other arithmetic  5.05 us (3%)
    pallas_call x1, Pallas kernels, fine_update(): pl.pallas_call(functools.partial(fine_kernel, slots_each), out_shape=(jax...  69 us
    pallas_call x1, Pallas kernels, coarse_duals(): pl.pallas_call(functools.partial(coarse_kernel, len(src), len(tgt), store...  46.5 us
    ppermute x7, starting transfers between devices, exchange(): return lax.ppermute(x, axis, [(i, i ^ flip) for i in range(count)])  9.51 us
    all_to_all x1, waiting for transfers between devices, on_device(): lax.all_to_all(partial, AXES, split_axis=0, concat_axis=0, tiled=True)  9.28 us
    ppermute x7, waiting for transfers between devices, exchange(): return lax.ppermute(x, axis, [(i, i ^ flip) for i in range(count)])  6.41 us
    unnamed x13, local copies, waits for them, and re-layouts  3.62 us
  transfers between devices with their start and end apart: 9, of which 5 were waited for; matrix products, arithmetic and copies ran while one was open for 2% of the time, Pallas kernels for 27%

profile of v2, /device:TPU:0, one launch (start us, length us, event | category | flops | bytes accessed | tf_op | source)
XLA Modules:
  0.0 173.9 jit_solution(18227128725741885289)
XLA Ops:
  7.2 0.0 all-gather.3.cloned.1.call-start
  7.2 0.8 reshape.142
  8.0 0.2 convert_reduce_fusion
  8.2 0.0 copy-start.5
  8.2 0.1 select_reduce_fusion
  8.3 0.7 convert_bitcast_fusion
  9.0 1.6 pad_maximum_fusion
  10.6 0.0 all-gather.3.cloned.1.call-update
  10.6 0.7 pad_maximum_fusion.3
  11.3 0.5 collective-permute-start.3
  11.8 0.8 collective-permute-done.3
  12.6 0.7 pad_maximum_fusion.2.refs_4_
  13.3 2.9 %collective-permute-start.4 = (f32[17,256]{1,0:T(8,128)S(1)}, f32[17,256]{1,0:T(8,128)S(1)}, u32[]{:S(2)}, u32[]{:S(2)}) collective-permute-start(f32[17,256]{1,0:T(8,128)S(1)} %pad_maximum_fusion.2.refs_4_), channel_id=1, source_target_pairs={{0,2},{1,3},{2,0},{3,1},{4,6},{5,7},{6,4},{7,5},{8,10},{9,11},{10,... | collective-permute-start | bytes 52232 | tf_op jit(solution)/shard_map/ppermute | solution.py:462
  16.3 0.9 pad_maximum_fusion.1.refs_0_
  17.1 1.6 collective-permute-start
  18.7 1.5 collective-permute-start.1
  20.2 0.5 collective-permute-start.2
  20.7 2.6 %collective-permute-start.5 = (f32[17,256]{1,0:T(8,128)S(1)}, f32[17,256]{1,0:T(8,128)S(1)}, u32[]{:S(2)}, u32[]{:S(2)}) collective-permute-start(f32[17,256]{1,0:T(8,128)S(1)} %pad_maximum_fusion.2.refs_4_), channel_id=1, source_target_pairs={{0,4},{1,5},{2,6},{3,7},{4,0},{5,1},{6,2},{7,3},{8,12},{9,13},{10,... | collective-permute-start | bytes 52232 | tf_op jit(solution)/shard_map/ppermute | solution.py:462
  23.3 0.0 collective-permute-done.4.refs_5_
  23.3 0.0 collective-permute-start.6
  23.3 0.1 pad_add_fusion.where_ref
  23.3 0.0 copy-start.1
  23.3 0.0 copy-start.2
  23.3 2.1 %collective-permute-done.5.refs_6_ = f32[17,256]{1,0:T(8,128)S(1)} collective-permute-done((f32[17,256]{1,0:T(8,128)S(1)}, f32[17,256]{1,0:T(8,128)S(1)}, u32[]{:S(2)}, u32[]{:S(2)}) %collective-permute-start.5) | collective-permute-done | bytes 17440 | tf_op jit(solution)/shard_map/ppermute | solution.py:462
  25.4 3.5 %collective-permute-done.6.refs_7_ = f32[17,256]{1,0:T(8,128)S(1)} collective-permute-done((f32[17,256]{1,0:T(8,128)S(1)}, f32[17,256]{1,0:T(8,128)S(1)}, u32[]{:S(2)}, u32[]{:S(2)}) %collective-permute-start.6) | collective-permute-done | bytes 17440 | tf_op jit(solution)/shard_map/ppermute | solution.py:462
  28.9 0.0 collective-permute-done.refs_1_
  28.9 0.0 collective-permute-done.1.refs_2_
  28.9 0.0 collective-permute-done.2.refs_3_
  28.9 46.5 %coarse.1 = (f32[1,4096]{1,0:T(1,128)S(1)}, f32[1,1024]{1,0:T(1,128)S(1)}) custom-call(f32[17,1024]{1,0:T(8,128)S(1)} %pad_maximum_fusion.1.refs_0_, f32[17,1024]{1,0:T(8,128)S(1)} %collective-permute-done.refs_1_, f32[17,1024]{1,0:T(8,128)S(1)} %collective-permute-done.1.refs_2_, f32[17,1024]{1,0:T(8,128)S(1)} %collective-permute-done.2.refs_3_, ...), custom_call_target="tpu_custom_call" | custom-call | flops 167772160 | bytes 491520 | tf_op jit(solution)/shard_map/coarse/pallas_call | solution.py:227
  75.5 0.0 copy-done.5
  75.5 1.9 %all-gather.3.cloned.1.call-done = f32[8960,128]{1,0:T(8,128)} async-done(((f32[280,128]{1,0:T(8,128)}), f32[8960,128]{1,0:T(8,128)}) %all-gather.3.cloned.1.call-update) | async-done | bytes 4587536 | tf_op jit(solution)/shard_map/all_gather | solution.py:490
  77.4 0.9 slice.12
  78.4 0.1 dynamic-slice_convert_fusion
  78.4 0.1 convert_element_type.22.slot_ref
  78.6 0.0 copy-done.1
  78.6 0.0 copy-done.2
  78.6 0.0 copy-start
  78.6 2.3 %copy-done = f32[8960,128]{1,0:T(8,128)S(1)} copy-done((f32[8960,128]{1,0:T(8,128)S(1)}, f32[8960,128]{1,0:T(8,128)}, u32[]{:S(2)}) %copy-start) | copy-done | bytes 4587544
  80.9 69.0 %fine.1 = (f32[32,5,256]{2,1,0:T(8,128)}, f32[16,128]{1,0:T(8,128)S(1)}, f32[64,128]{1,0:T(8,128)}) custom-call(s32[160]{0:T(256)S(1)} %convert_element_type.22.slot_ref, s32[3]{0:T(128)S(1)} %pad_add_fusion.where_ref, f32[32,280,128]{2,1,0:T(8,128)S(1)} %bitcast.25, f32[16,8192]{1,0:T(8,128)S(1)} %copy-done.1, s32[64,128]{1,0:T(8,128)S(1)} %bitcast.26, ...), custom_call_target="tpu_custom_call" | custom-call | tf_op jit(solution)/shard_map/fine/pallas_call | solution.py:409
  149.9 0.0 copy-start.3
  149.9 0.6 copy-done.3
  150.4 2.9 %all-to-all-start = ((f32[32,5,256]{2,1,0:T(8,128)}), f32[32,5,256]{2,1,0:T(8,128)S(1)}, u32[]{:S(2)}, u32[]{:S(2)}) async-start(f32[32,5,256]{2,1,0:T(8,128)} %get-tuple-element.11), calls=%async_computation | async-start | bytes 524288 | tf_op jit(solution)/shard_map/all_to_all | solution.py:515
  153.4 0.6 slice.9
  154.0 0.5 slice_bitcast_fusion
  154.5 9.3 %all-to-all-done.partial = f32[32,5,256]{2,1,0:T(8,128)S(1)} async-done(((f32[32,5,256]{2,1,0:T(8,128)}), f32[32,5,256]{2,1,0:T(8,128)S(1)}, u32[]{:S(2)}, u32[]{:S(2)}) %all-to-all-start) | async-done | bytes 163872 | tf_op jit(solution)/shard_map/all_to_all | solution.py:515
  163.8 0.0 copy-start.4
  163.8 0.7 copy-done.4
  164.5 2.6 %finish.1 = f32[16,128]{1,0:T(8,128)} custom-call(s32[128]{0:T(128)} %copy-done.5, f32[32,5,256]{2,1,0:T(8,128)} %copy-done.4, f32[16,128]{1,0:T(8,128)} %copy-done.3), custom_call_target="tpu_custom_call" | custom-call | tf_op jit(solution)/shard_map/finish/pallas_call | solution.py:450
  (4 shorter events, 0.1 us)
Async XLA Ops:
  7.2 70.2 %all-gather.3.cloned.1.call-start = ((), (), s32[]{:S(2)}) async-start(), calls=%async_computation.1 | async-start | bytes 4730880 | tf_op jit(solution)/shard_map/all_gather | solution.py:490
  8.2 67.3 %copy-start.5 = (s32[128]{0:T(128)}, s32[128]{0:T(128)S(1)}, u32[]{:S(2)}) copy-start(s32[128]{0:T(128)S(1)} %multiply_add_fusion.slot_ref) | copy-start | bytes 1540
  11.3 1.3 collective-permute-start.3
  13.3 9.9 %collective-permute-start.4 = (f32[17,256]{1,0:T(8,128)S(1)}, f32[17,256]{1,0:T(8,128)S(1)}, u32[]{:S(2)}, u32[]{:S(2)}) collective-permute-start(f32[17,256]{1,0:T(8,128)S(1)} %pad_maximum_fusion.2.refs_4_), channel_id=1, source_target_pairs={{0,2},{1,3},{2,0},{3,1},{4,6},{5,7},{6,4},{7,5},{8,10},{9,11},{10,... | collective-permute-start | bytes 52232 | tf_op jit(solution)/shard_map/ppermute | solution.py:462
  17.1 11.8 %collective-permute-start = (f32[17,1024]{1,0:T(8,128)S(1)}, f32[17,1024]{1,0:T(8,128)S(1)}, u32[]{:S(2)}, u32[]{:S(2)}) collective-permute-start(f32[17,1024]{1,0:T(8,128)S(1)} %pad_maximum_fusion.1.refs_0_), channel_id=1, source_target_pairs={{0,8},{8,0},{16,24},{24,16},{1,9},{9,1},{17,25},{25,17},{2,10},{10... | collective-permute-start | bytes 208904 | tf_op jit(solution)/shard_map/ppermute | solution.py:462
  18.7 10.2 %collective-permute-start.1 = (f32[17,1024]{1,0:T(8,128)S(1)}, f32[17,1024]{1,0:T(8,128)S(1)}, u32[]{:S(2)}, u32[]{:S(2)}) collective-permute-start(f32[17,1024]{1,0:T(8,128)S(1)} %pad_maximum_fusion.1.refs_0_), channel_id=1, source_target_pairs={{0,16},{8,24},{16,0},{24,8},{1,17},{9,25},{17,1},{25,9},{2,18},{10... | collective-permute-start | bytes 208904 | tf_op jit(solution)/shard_map/ppermute | solution.py:462
  20.2 8.7 %collective-permute-start.2 = (f32[17,1024]{1,0:T(8,128)S(1)}, f32[17,1024]{1,0:T(8,128)S(1)}, u32[]{:S(2)}, u32[]{:S(2)}) collective-permute-start(f32[17,1024]{1,0:T(8,128)S(1)} %pad_maximum_fusion.1.refs_0_), channel_id=1, source_target_pairs={{0,24},{8,16},{16,8},{24,0},{1,25},{9,17},{17,9},{25,1},{2,26},{10... | collective-permute-start | bytes 208904 | tf_op jit(solution)/shard_map/ppermute | solution.py:462
  20.7 4.7 %collective-permute-start.5 = (f32[17,256]{1,0:T(8,128)S(1)}, f32[17,256]{1,0:T(8,128)S(1)}, u32[]{:S(2)}, u32[]{:S(2)}) collective-permute-start(f32[17,256]{1,0:T(8,128)S(1)} %pad_maximum_fusion.2.refs_4_), channel_id=1, source_target_pairs={{0,4},{1,5},{2,6},{3,7},{4,0},{5,1},{6,2},{7,3},{8,12},{9,13},{10,... | collective-permute-start | bytes 52232 | tf_op jit(solution)/shard_map/ppermute | solution.py:462
  23.3 5.6 %collective-permute-start.6 = (f32[17,256]{1,0:T(8,128)S(1)}, f32[17,256]{1,0:T(8,128)S(1)}, u32[]{:S(2)}, u32[]{:S(2)}) collective-permute-start(f32[17,256]{1,0:T(8,128)S(1)} %pad_maximum_fusion.2.refs_4_), channel_id=1, source_target_pairs={{0,6},{1,7},{2,4},{3,5},{4,2},{5,3},{6,0},{7,1},{8,14},{9,15},{10,... | collective-permute-start | bytes 52232 | tf_op jit(solution)/shard_map/ppermute | solution.py:462
  23.3 55.2 %copy-start.1 = (f32[16,8192]{1,0:T(8,128)S(1)}, f32[16,8192]{1,0:T(8,128)}, u32[]{:S(2)}) copy-start(f32[16,8192]{1,0:T(8,128)} %tgt_pts.1) | copy-start | bytes 1572868
  23.3 55.2 %copy-start.2 = (s32[8192]{0:T(1024)S(1)}, s32[8192]{0:T(1024)}, u32[]{:S(2)}) copy-start(s32[8192]{0:T(1024)} %param.16) | copy-start | bytes 98308
  78.6 2.3 %copy-start = (f32[8960,128]{1,0:T(8,128)S(1)}, f32[8960,128]{1,0:T(8,128)}, u32[]{:S(2)}) copy-start(f32[8960,128]{1,0:T(8,128)} %all-gather.3.cloned.1.call-done) | copy-start | bytes 13762564
  149.9 0.6 copy-start.3
  150.4 13.3 %all-to-all-start = ((f32[32,5,256]{2,1,0:T(8,128)}), f32[32,5,256]{2,1,0:T(8,128)S(1)}, u32[]{:S(2)}, u32[]{:S(2)}) async-start(f32[32,5,256]{2,1,0:T(8,128)} %get-tuple-element.11), calls=%async_computation | async-start | bytes 524288 | tf_op jit(solution)/shard_map/all_to_all | solution.py:515
  163.8 0.7 copy-start.4
Sparse Core Ops, SparseCore 0:
  10.9 66.5 all-gather.2

commit v3 on v2

--- a/solution.py
+++ b/solution.py
@@ -81,15 +81,65 @@
     return out
 
 
+def source_columns(ref, count, k, n):
+    halves = [
+        jnp.concatenate(
+            [
+                ref[pl.ds(pl.multiple_of(8 * (half * count + k * n + i), 8), 8), :]
+                for i in range(n)
+            ],
+            1,
+        )
+        for half in range(2)
+    ]
+    values = [ref[pl.ds(F * count + k * n + i, 1), :] for i in range(n)]
+    return jnp.concatenate(halves, 0), jnp.concatenate(values, 1)
+
+
+def prepare_kernel(
+    src_pts, cluster, table, src_cent, src_mass, tgt_cent, tgt_mass, bundle, src_own, tgt_own
+):
+    for half in range(2):
+        rows = slice(8 * half, 8 * half + 8)
+        for ref, out in ((src_pts, bundle), (src_cent, src_own)):
+            count = ref.shape[1] // LANES
+            for i in range(count):
+                at = 8 * (half * count + i)
+                out[at : at + 8, :] = ref[rows, i * LANES : (i + 1) * LANES]
+    at = 2 * LANES
+    bundle[at : at + F, :] = cluster[...].astype(jnp.float32)
+    bundle[at + F : at + F + 8, :] = jnp.zeros((8, LANES), jnp.float32)
+    bundle[at + F : at + F + table.shape[0], :] = table[...].astype(jnp.float32)
+    at = F * src_mass.shape[0]
+    src_own[at : at + src_mass.shape[0], :] = src_mass[...]
+    tgt_own[0, 0:F, :] = tgt_cent[...]
+    tgt_own[0, F : F + 8, :] = jnp.broadcast_to(tgt_mass[...], (8, LANES))
+
+
+def prepare(src_pts, cluster, table, src_cent, src_mass, tgt_cent, tgt_mass):
+    return pl.pallas_call(
+        prepare_kernel,
+        out_shape=(
+            jax.ShapeDtypeStruct((2 * LANES + F + 8, LANES), jnp.float32),
+            jax.ShapeDtypeStruct(((F + 1) * src_mass.shape[0], LANES), jnp.float32),
+            jax.ShapeDtypeStruct((1, F + 8, LANES), jnp.float32),
+        ),
+        in_specs=[VMEM] * 7,
+        out_specs=(VMEM,) * 3,
+        name="prepare",
+    )(src_pts, cluster, table, src_cent, src_mass, tgt_cent, tgt_mass)
+
+
 def coarse_kernel(n_src, n_tgt, stored, *refs):
     src = refs[:n_src]
     tgt = refs[n_src : n_src + n_tgt]
     f_out, g_out, kernel, mass, dual, sums = refs[n_src + n_tgt :]
     ks, kt = f_out.shape[1], g_out.shape[1]
-    piece = src[0].shape[1]
+    wide_src = src[0].shape[0] // (F + 1)
+    piece = wide_src * LANES
     tiles = kt // LANES
-    y = jnp.concatenate([ref[0:F, :] for ref in tgt], 1)
-    b = jnp.concatenate([ref[F : F + 1, :] for ref in tgt], 1)
+    y = jnp.concatenate([ref[e, 0:F, :] for ref in tgt for e in range(2)], 1)
+    b = jnp.concatenate([ref[e, F : F + 1, :] for ref in tgt for e in range(2)], 1)
     right = pack_right(y, jnp.log2(b) - SCALE * square_norm(y))
     ones = jnp.ones((F, LANES), jnp.bfloat16)
     zero = jnp.zeros((8, kt), jnp.float32)
@@ -102,11 +152,10 @@
         for s in range(n_src):
 
             def chunk(k, carry, s=s):
-                span = pl.ds(pl.multiple_of(k * size, size), size)
                 rows = pl.ds(pl.multiple_of(s * piece + k * size, size), size)
-                x = src[s][0:F, span]
+                x, values = source_columns(src[s], wide_src, k, size // LANES)
                 left = pack_left(x, -SCALE * square_norm(x))
-                return body(src[s][F : F + 1, span], rows, left, carry)
+                return body(values, rows, left, carry)
 
             carry = lax.fori_loop(0, piece // size, chunk, carry)
         return carry
@@ -221,8 +270,8 @@
     lax.fori_loop(0, ks // LANES, to_lanes, 0)
 
 def coarse_duals(src, tgt):
-    ks = sum(part.shape[1] for part in src)
-    kt = sum(part.shape[1] for part in tgt)
+    ks = sum(part.shape[0] // (F + 1) * LANES for part in src)
+    kt = sum(2 * part.shape[2] for part in tgt)
     stored = ks * kt * 4 <= 16 * MIB
     return pl.pallas_call(
         functools.partial(coarse_kernel, len(src), len(tgt), stored),
@@ -256,16 +305,31 @@
     return out
 
 
-def fine_kernel(slots_each, slot_ref, where_ref, bundle, tgt_pts, tgt_cluster, f_table, g_table,
-    partial_out, start_f_out, fine_g_out,
-    start_g, packed, col_sum, col_top, order, count):
+def fine_kernel(n_stacks, slots_each, stride, where_ref, *refs):
+    stacks = refs[:n_stacks]
+    tgt_pts, tgt_cluster, f_table, g_table, partial_out, start_f_out, fine_g_out = refs[
+        n_stacks : n_stacks + 7
+    ]
+    bundle, start_g, packed, col_sum, col_top, codes, arrived, slots, order, count = refs[
+        n_stacks + 7 :
+    ]
     devices = bundle.shape[0]
+    depth = devices // n_stacks
     me, src_flip, tgt_flip = where_ref[0], where_ref[1], where_ref[2]
 
-    index = bundle[me, 2 * LANES : 2 * LANES + F, :].astype(jnp.int32) ^ src_flip
-    for half in range(2):
-        rows = slice(8 * half, 8 * half + 8)
-        start_f_out[rows, :] = look_up(f_table, index[rows])
+    copies = [
+        pltpu.make_async_copy(
+            stacks[n], bundle.at[pl.ds(n * depth, depth)], arrived.at[n]
+        )
+        for n in range(n_stacks)
+    ]
+    for copy in copies:
+        copy.start()
+
+    def sender(place):
+        stack = place // depth
+        return me ^ (2 * depth * (stack // 2) + 2 * (place % depth) + stack % 2)
+
     for k in range(2 * TB_DEV // 8):
         index = tgt_cluster[8 * k : 8 * k + 8, :] ^ tgt_flip
         start_g[8 * k : 8 * k + 8, :] = look_up(g_table, index)
@@ -283,12 +347,31 @@
     packed[TB_DEV] = jnp.zeros((BLK, LANES), jnp.bfloat16)
     count[TB_DEV] = 0
 
+    for copy in copies:
+        copy.wait()
+    index = bundle[0, 2 * LANES : 2 * LANES + F, :].astype(jnp.int32) ^ src_flip
+    for half in range(2):
+        rows = slice(8 * half, 8 * half + 8)
+        start_f_out[rows, :] = look_up(f_table, index[rows])
+
+    at = me * stride
+
+    def slot_row(n, carry):
+        codes[pl.ds(n, 1), :] = bundle[n, pl.ds(2 * LANES + F + at // LANES, 1), :].astype(jnp.int32)
+        return carry
+
+    lax.fori_loop(0, devices, slot_row, 0, unroll=BLOCKS)
+    codes[...] = pltpu.roll(codes[...], (LANES - at % LANES) % LANES, 1)
+    copy = pltpu.make_async_copy(codes, slots, arrived.at[0])
+    copy.start()
+    copy.wait()
+
     total = devices * slots_each
     unroll = math.gcd(PAIRS, total)
 
     def place(p, carry):
         used, unused = carry
-        code = slot_ref[p]
+        code = slots[p // slots_each, p % slots_each]
         valid = code > 0
         order[jnp.where(valid, used, unused)] = p
         t = jnp.where(valid, (code - 1) % TB_DEV, TB_DEV)
@@ -299,7 +382,7 @@
     used, _ = lax.fori_loop(0, total, place, (jnp.int32(0), jnp.int32(total - 1)), unroll=16)
 
     def cluster_rows(p):
-        code = slot_ref[p] - 1
+        code = slots[p // slots_each, p % slots_each] - 1
         block = jnp.where(code >= 0, code // TB_DEV, 0)
         d = p // slots_each
         return [bundle[d, pl.ds(2 * LANES + 2 * block + k, 1), :] for k in range(2)]
@@ -314,7 +397,7 @@
         return out
 
     def product(p, f):
-        code = slot_ref[p] - 1
+        code = slots[p // slots_each, p % slots_each] - 1
         valid = code >= 0
         block = jnp.where(valid, code // TB_DEV, 0)
         t = jnp.where(valid, code % TB_DEV, TB_DEV)
@@ -327,7 +410,8 @@
         return t, d, SCALE * f, z
 
     def put(p, d, value):
-        partial_out[d, pl.ds(p % slots_each, 1), :] = value
+        span = pl.ds(pl.multiple_of(p % slots_each * BLK, BLK), BLK)
+        partial_out[sender(d), :, span] = value
 
     def fill(ref, value):
         def body(t, carry):
@@ -404,37 +488,40 @@
 
         lax.fori_loop(0, TB_DEV, lanes, 0)
 
-def fine_update(slots, where, bundle, tgt_pts, tgt_cluster, f_table, g_table, slots_each):
-    devices = bundle.shape[0]
+def fine_update(where, stacks, tgt_pts, tgt_cluster, f_table, g_table, slots_each, stride):
+    devices = sum(stack.shape[0] for stack in stacks)
     return pl.pallas_call(
-        functools.partial(fine_kernel, slots_each),
+        functools.partial(fine_kernel, len(stacks), slots_each, stride),
         out_shape=(
-            jax.ShapeDtypeStruct((devices, slots_each, BLK), jnp.float32),
+            jax.ShapeDtypeStruct((devices, 1, slots_each * BLK), jnp.float32),
             jax.ShapeDtypeStruct((F, LANES), jnp.float32),
             jax.ShapeDtypeStruct((2 * TB_DEV, LANES), jnp.float32),
         ),
-        in_specs=[SMEM, SMEM] + [VMEM] * 5,
+        in_specs=[SMEM] + [pl.BlockSpec(memory_space=pl.ANY)] * len(stacks) + [VMEM] * 4,
         out_specs=(VMEM, VMEM, VMEM),
         scratch_shapes=[
+            pltpu.VMEM((devices,) + stacks[0].shape[1:], jnp.float32),
             pltpu.VMEM((2 * TB_DEV, LANES), jnp.float32),
             pltpu.VMEM((TB_DEV + 1, BLK, LANES), jnp.bfloat16),
             pltpu.VMEM((TB_DEV + 1, BLK, LANES), jnp.float32),
             pltpu.VMEM((TB_DEV + 1, BLK, LANES), jnp.float32),
+            pltpu.VMEM((devices, LANES), jnp.int32),
+            pltpu.SemaphoreType.DMA((len(stacks),)),
+            pltpu.SMEM((devices, LANES), jnp.int32),
             pltpu.SMEM((devices * slots_each,), jnp.int32),
             pltpu.SMEM((TB_DEV + 1,), jnp.int32),
         ],
         compiler_params=pltpu.CompilerParams(vmem_limit_bytes=48 * MIB),
         name="fine",
-    )(slots, where, bundle, tgt_pts, tgt_cluster, f_table, g_table)
+    )(where, *stacks, tgt_pts, tgt_cluster, f_table, g_table)
 
 
 def finish_kernel(slots_each, slot_ref, partial, start_f, fine_f_out, gathered):
     for block in range(SB_DEV):
         for k in range(SUPP):
             slot = slot_ref[block * SUPP + k]
-            gathered[k, block : block + 1, :] = partial[
-                slot // slots_each, pl.ds(slot % slots_each, 1), :
-            ]
+            span = pl.ds(pl.multiple_of(slot % slots_each * BLK, BLK), BLK)
+            gathered[k, block : block + 1, :] = partial[slot // slots_each, :, span]
     values = gathered[...]
     top = jnp.max(values, 0)
     lse = top + jnp.log2(jnp.sum(jnp.exp2(values - top[None]), 0))
@@ -478,39 +565,41 @@
     earlier = (owners[None, :] == owners[:, None]) & (positions[None, :] < positions[:, None])
     slot_ids = owners * slots_each + jnp.sum(earlier.astype(jnp.int32), 1)
     codes = (positions // SUPP) * TB_DEV + wanted % TB_DEV + 1
-    width = -(-devices * slots_each // LANES) * LANES
-    table = jnp.sum(
-        jnp.where(slot_ids[None, :] == jnp.arange(width, dtype=jnp.int32)[:, None], codes[None, :], 0), 1
+    stride = 1 << (slots_each - 1).bit_length()
+    filled = owners * stride + slot_ids % slots_each
+    places = jnp.arange(devices * stride, dtype=jnp.int32)
+    table = jnp.sum(jnp.where(filled[None, :] == places[:, None], codes[None, :], 0), 1)
+    bundle, src_own, tgt_own = prepare(
+        src_pts,
+        src_cluster.reshape(F, LANES),
+        table.reshape(-1, LANES),
+        src_cent,
+        src_mass.reshape(-1, LANES),
+        tgt_cent,
+        tgt_mass.reshape(-1, LANES),
     )
-    tiles = src_pts.reshape(2, 8, F, LANES).transpose(0, 2, 1, 3).reshape(2 * BLK // 2, LANES)
-    table = jnp.pad(table.reshape(-1, LANES), ((0, -(width // LANES) % 8), (0, 0)))
-    bundle = jnp.concatenate(
-        [tiles, src_cluster.reshape(F, LANES).astype(jnp.float32), table.astype(jnp.float32)], 0
-    )
-    bundles = lax.all_gather(bundle, AXES)
-
-    src_own = jnp.concatenate([src_cent, src_mass[None]], 0)
-    tgt_own = jnp.concatenate([tgt_cent, tgt_mass[None]], 0)
-    tgt_pair = jnp.concatenate([tgt_own, exchange(tgt_own, "col", 1)], 1)
+
+    tgt_pair = jnp.concatenate([tgt_own, exchange(tgt_own, "col", 1)], 0)
     src_all = [src_own] + [exchange(src_own, "row", k) for k in range(1, n_row)]
     tgt_all = [tgt_pair] + [exchange(tgt_pair, "col", k) for k in range(2, n_col, 2)]
+    stack = jnp.stack([bundle] + [exchange(bundle, "col", k) for k in range(2, n_col, 2)])
+    src_all, tgt_all, stack = lax.optimization_barrier((src_all, tgt_all, stack))
+    stacks = [stack] + [exchange(stack, "row", k) for k in range(1, n_row)]
     f_table, g_table = coarse_duals(src_all, tgt_all)
     coarse_f = f_table[0, : src_cent.shape[1]]
     coarse_g = g_table[0, : tgt_cent.shape[1]]
 
-    slots = bundles[:, 2 * BLK // 2 + F :, :].reshape(devices, -1)
-    slots = lax.dynamic_slice_in_dim(slots, me * slots_each, slots_each, 1)
-    slots = slots.reshape(-1).astype(jnp.int32)
+    stacks = [part for own in stacks for part in (own, exchange(own, "col", 1))]
     where = jnp.stack([me, row * src_cent.shape[1], col * tgt_cent.shape[1]]).astype(jnp.int32)
     partial, start_f, fine_g = fine_update(
-        slots,
         where,
-        bundles,
+        stacks,
         tgt_pts,
         tgt_cluster.reshape(2 * TB_DEV, LANES),
         f_table,
         g_table,
         slots_each,
+        stride,
     )
     returned = lax.all_to_all(partial, AXES, split_axis=0, concat_axis=0, tiled=True)
     fine_f = finish(slot_ids, returned, start_f, slots_each)

time: 174 us -> 203 us (1.17); the launches traced: 174 us -> 200 us
  waiting for transfers between devices: 17.6 us -> 33.4 us
  starting transfers between devices: 12.5 us -> 25.9 us
  between operations: 14.1 us -> 0.75 us
  local copies, waits for them, and re-layouts: 6.51 us -> 13.1 us
  Pallas kernels: 118 us -> 124 us
  other arithmetic: 5.05 us -> 2.44 us
    ppermute x7 -> x17, waiting for transfers between devices: 6.41 us -> 26 us  [exchange(): return lax.ppermute(x, axis, [(i, i ^ flip) for i in range(count)])]
    ppermute x7 -> x17, starting transfers between devices: 9.51 us -> 23.1 us  [exchange(): return lax.ppermute(x, axis, [(i, i ^ flip) for i in range(count)])]
    unnamed x13 -> x37, local copies, waits for them, and re-layouts: 3.62 us -> 11.2 us
    pallas_call x1 -> x2, Pallas kernels: 69 us -> 75.1 us  [the longest x1 73.4 us: fine_update(): pl.pallas_call(functools.partial(fine_kernel, len(stacks), slots_each, st...]
    concatenate x4 -> x0, other arithmetic: 3.87 us -> none  [the longest x1 1.57 us: on_device(): jnp.concatenate([tiles, src_cluster.reshape(F, LANES).astype(jnp.float32)...]
  transfers between devices with their start and end apart: 9 -> 18, of which waited for: 5 -> 7; matrix products, arithmetic and copies ran while one was open for 2% -> 1% of each run, Pallas kernels for 27% -> 23%
where the time goes in v3:
time: 203 us; the launch traced here: 200 us
  Pallas kernels  124 us (61%)
  waiting for transfers between devices  33.4 us (16%)
  starting transfers between devices  25.9 us (13%)
  local copies, waits for them, and re-layouts  13.1 us (6%)
  other arithmetic  2.44 us (1%)
    pallas_call x1, Pallas kernels, fine_update(): pl.pallas_call(functools.partial(fine_kernel, len(stacks), slots_each, st...  73.4 us
    pallas_call x1, Pallas kernels, coarse_duals(): pl.pallas_call(functools.partial(coarse_kernel, len(src), len(tgt), store...  46.5 us
    ppermute x17, waiting for transfers between devices, exchange(): return lax.ppermute(x, axis, [(i, i ^ flip) for i in range(count)])  26 us
    ppermute x17, starting transfers between devices, exchange(): return lax.ppermute(x, axis, [(i, i ^ flip) for i in range(count)])  23.1 us
    unnamed x37, local copies, waits for them, and re-layouts  11.2 us
    all_to_all x1, waiting for transfers between devices, on_device(): lax.all_to_all(partial, AXES, split_axis=0, concat_axis=0, tiled=True)  7.36 us
  transfers between devices with their start and end apart: 18, of which 7 were waited for; matrix products, arithmetic and copies ran while one was open for 1% of the time, Pallas kernels for 23%

profile of v3, /device:TPU:0, one launch (start us, length us, event | category | flops | bytes accessed | tf_op | source)
XLA Modules:
  0.0 199.7 jit_solution(15863410516367231047)
XLA Ops:
  0.6 0.8 reshape.147
  1.4 0.2 convert_reduce_fusion
  1.6 0.5 multiply_add_fusion
  2.1 0.7 select_reduce_fusion
  2.8 1.7 prepare.1
  4.4 5.0 %collective-permute-start.9 = (f32[280,128]{1,0:T(8,128)}, f32[280,128]{1,0:T(8,128)S(1)}, u32[]{:S(2)}, u32[]{:S(2)}) collective-permute-start(f32[280,128]{1,0:T(8,128)} %get-tuple-element.23), channel_id=1, source_target_pairs={{0,6},{1,7},{2,4},{3,5},{4,2},{5,3},{6,0},{7,1},{8,14},{9,15},{10,... | collective-permute-start | bytes 430088 | tf_op jit(solution)/shard_map/ppermute | solution.py:549
  9.5 0.6 collective-permute-start.7
  10.1 0.7 constant_dynamic-update-slice_fusion.1
  10.8 0.7 collective-permute-done.3
  11.4 3.8 %collective-permute-start.6 = (f32[2,24,128]{2,1,0:T(8,128)S(1)}, f32[2,24,128]{2,1,0:T(8,128)S(1)}, u32[]{:S(2)}, u32[]{:S(2)}) collective-permute-start(f32[2,24,128]{2,1,0:T(8,128)S(1)} %constant_dynamic-update-slice_fusion.refs_4_), channel_id=1, source_target_pairs={{0,6},{1,7},{2,4},{3,5},{4,2},{5,3},{6,0},{7,1},{8,14},{9,15},{10,... | collective-permute-start | bytes 73736 | tf_op jit(solution)/shard_map/ppermute | solution.py:549
  15.3 2.4 %collective-permute-start.2 = (f32[136,128]{1,0:T(8,128)}, f32[136,128]{1,0:T(8,128)S(1)}, u32[]{:S(2)}, u32[]{:S(2)}) collective-permute-start(f32[136,128]{1,0:T(8,128)} %get-tuple-element.24.refs_0_), channel_id=1, source_target_pairs={{0,24},{8,16},{16,8},{24,0},{1,25},{9,17},{17,9},{25,1},{2,26},{10... | collective-permute-start | bytes 208904 | tf_op jit(solution)/shard_map/ppermute | solution.py:549
  17.7 2.6 %collective-permute-done.6.refs_7_ = f32[2,24,128]{2,1,0:T(8,128)S(1)} collective-permute-done((f32[2,24,128]{2,1,0:T(8,128)S(1)}, f32[2,24,128]{2,1,0:T(8,128)S(1)}, u32[]{:S(2)}, u32[]{:S(2)}) %collective-permute-start.6) | collective-permute-done | bytes 24608 | tf_op jit(solution)/shard_map/ppermute | solution.py:549
  20.3 0.6 copy-done.11
  20.9 1.5 collective-permute-start.1
  22.4 1.5 collective-permute-start
  23.9 0.0 collective-permute-done.8
  23.9 4.2 %collective-permute-start.5 = (f32[2,24,128]{2,1,0:T(8,128)S(1)}, f32[2,24,128]{2,1,0:T(8,128)S(1)}, u32[]{:S(2)}, u32[]{:S(2)}) collective-permute-start(f32[2,24,128]{2,1,0:T(8,128)S(1)} %constant_dynamic-update-slice_fusion.refs_4_), channel_id=1, source_target_pairs={{0,4},{1,5},{2,6},{3,7},{4,0},{5,1},{6,2},{7,3},{8,12},{9,13},{10,... | collective-permute-start | bytes 73736 | tf_op jit(solution)/shard_map/ppermute | solution.py:549
  28.1 1.0 pad_maximum_fusion.refs_0_
  29.1 0.8 collective-permute-done.5.refs_6_
  29.9 0.6 copy-done.13
  30.5 1.4 collective-permute-done.4.refs_5_
  31.9 0.6 copy-done.15
  32.5 0.6 copy-done.5
  33.2 0.6 copy-done.7
  33.8 0.6 copy-done.9
  34.4 0.5 collective-permute-start.15
  34.9 1.5 collective-permute-start.13
  36.4 1.5 collective-permute-start.11
  37.9 13.3 %collective-permute-done.15.refs_6_ = f32[4,280,128]{2,1,0:T(8,128)S(1)} collective-permute-done((f32[4,280,128]{2,1,0:T(8,128)S(1)}, f32[4,280,128]{2,1,0:T(8,128)S(1)}, u32[]{:S(2)}, u32[]{:S(2)}) %collective-permute-start.15) | collective-permute-done | bytes 573472 | tf_op jit(solution)/shard_map/ppermute | solution.py:549
  51.3 7.2 %collective-permute-done.13.refs_4_ = f32[4,280,128]{2,1,0:T(8,128)S(1)} collective-permute-done((f32[4,280,128]{2,1,0:T(8,128)S(1)}, f32[4,280,128]{2,1,0:T(8,128)S(1)}, u32[]{:S(2)}, u32[]{:S(2)}) %collective-permute-start.13) | collective-permute-done | bytes 573472 | tf_op jit(solution)/shard_map/ppermute | solution.py:549
  58.5 0.5 collective-permute-start.12
  59.0 0.1 pad_add_fusion.where_ref
  59.1 0.9 copy-done.6
  60.0 0.9 copy-done.8
  60.8 0.9 copy-done.10
  61.7 0.7 copy-done.12
  62.5 0.7 copy-done.14
  63.2 0.7 copy-done.16
  63.9 46.5 %coarse.1 = (f32[1,4096]{1,0:T(1,128)S(1)}, f32[1,1024]{1,0:T(1,128)S(1)}) custom-call(f32[136,128]{1,0:T(8,128)S(1)} %copy-done.4, f32[136,128]{1,0:T(8,128)S(1)} %copy-done.10, f32[136,128]{1,0:T(8,128)S(1)} %copy-done.8, f32[136,128]{1,0:T(8,128)S(1)} %copy-done.6, f32[2,24,128]{2,1,0:T(8,128)S(1)} %constant_dynamic-update-slice_fusion.refs_4_, ...), custom_call_target="tpu_custom_call" | custom-call | flops 167772160 | bytes 491520 | tf_op jit(solution)/shard_map/coarse/pallas_call | solution.py:276
  110.6 73.4 %fine.1 = (f32[32,1,1280]{2,1,0:T(1,128)S(1)}, f32[16,128]{1,0:T(8,128)S(1)}, f32[64,128]{1,0:T(8,128)}) custom-call(s32[3]{0:T(128)S(1)} %pad_add_fusion.where_ref, f32[4,280,128]{2,1,0:T(8,128)S(1)} %pad_maximum_fusion.refs_0_, f32[4,280,128]{2,1,0:T(8,128)S(1)} %collective-permute-done.10.refs_1_, f32[4,280,128]{2,1,0:T(8,128)S(1)} %collective-permute-done.11.refs_2_, ...), custom_call_target="tpu_custom_call" | custom-call | tf_op jit(solution)/shard_map/fine/pallas_call | solution.py:493
  184.0 0.7 copy-done.1
  184.7 0.6 copy-done.3
  185.3 2.8 %all-to-all-start = ((f32[32,1,1280]{2,1,0:T(1,128)}), f32[32,1,1280]{2,1,0:T(1,128)S(1)}, u32[]{:S(2)}, u32[]{:S(2)}) async-start(f32[32,1,1280]{2,1,0:T(1,128)} %copy-done.1), calls=%async_computation | async-start | bytes 327680 | tf_op jit(solution)/shard_map/all_to_all | solution.py:604
  188.1 0.6 slice.6
  188.7 0.5 slice_bitcast_fusion
  189.2 7.4 %all-to-all-done.partial = f32[32,1,1280]{2,1,0:T(1,128)S(1)} async-done(((f32[32,1,1280]{2,1,0:T(1,128)}), f32[32,1,1280]{2,1,0:T(1,128)S(1)}, u32[]{:S(2)}, u32[]{:S(2)}) %all-to-all-start) | async-done | bytes 163872 | tf_op jit(solution)/shard_map/all_to_all | solution.py:604
  196.6 0.7 copy-done.17
  197.2 2.5 %finish.1 = f32[16,128]{1,0:T(8,128)} custom-call(s32[128]{0:T(128)} %get-tuple-element.38.slot_ref, f32[32,1,1280]{2,1,0:T(1,128)} %copy-done.17, f32[16,128]{1,0:T(8,128)} %copy-done.3), custom_call_target="tpu_custom_call" | custom-call | tf_op jit(solution)/shard_map/finish/pallas_call | solution.py:537
  (39 shorter events, 0.1 us)
Async XLA Ops:
  4.4 18.0 %collective-permute-start.9 = (f32[280,128]{1,0:T(8,128)}, f32[280,128]{1,0:T(8,128)S(1)}, u32[]{:S(2)}, u32[]{:S(2)}) collective-permute-start(f32[280,128]{1,0:T(8,128)} %get-tuple-element.23), channel_id=1, source_target_pairs={{0,6},{1,7},{2,4},{3,5},{4,2},{5,3},{6,0},{7,1},{8,14},{9,15},{10,... | collective-permute-start | bytes 430088 | tf_op jit(solution)/shard_map/ppermute | solution.py:549
  9.5 14.4 %collective-permute-start.8 = (f32[280,128]{1,0:T(8,128)}, f32[280,128]{1,0:T(8,128)S(1)}, u32[]{:S(2)}, u32[]{:S(2)}) collective-permute-start(f32[280,128]{1,0:T(8,128)} %get-tuple-element.23), channel_id=1, source_target_pairs={{0,4},{1,5},{2,6},{3,7},{4,0},{5,1},{6,2},{7,3},{8,12},{9,13},{10,... | collective-permute-start | bytes 430088 | tf_op jit(solution)/shard_map/ppermute | solution.py:549
  9.5 18.6 %collective-permute-start.7 = (f32[280,128]{1,0:T(8,128)}, f32[280,128]{1,0:T(8,128)S(1)}, u32[]{:S(2)}, u32[]{:S(2)}) collective-permute-start(f32[280,128]{1,0:T(8,128)} %get-tuple-element.23), channel_id=1, source_target_pairs={{0,2},{1,3},{2,0},{3,1},{4,6},{5,7},{6,4},{7,5},{8,10},{9,11},{10,... | collective-permute-start | bytes 430088 | tf_op jit(solution)/shard_map/ppermute | solution.py:549
  10.0 1.4 collective-permute-start.3
  11.4 8.8 %collective-permute-start.6 = (f32[2,24,128]{2,1,0:T(8,128)S(1)}, f32[2,24,128]{2,1,0:T(8,128)S(1)}, u32[]{:S(2)}, u32[]{:S(2)}) collective-permute-start(f32[2,24,128]{2,1,0:T(8,128)S(1)} %constant_dynamic-update-slice_fusion.refs_4_), channel_id=1, source_target_pairs={{0,6},{1,7},{2,4},{3,5},{4,2},{5,3},{6,0},{7,1},{8,14},{9,15},{10,... | collective-permute-start | bytes 73736 | tf_op jit(solution)/shard_map/ppermute | solution.py:549
  15.3 17.3 %collective-permute-start.2 = (f32[136,128]{1,0:T(8,128)}, f32[136,128]{1,0:T(8,128)S(1)}, u32[]{:S(2)}, u32[]{:S(2)}) collective-permute-start(f32[136,128]{1,0:T(8,128)} %get-tuple-element.24.refs_0_), channel_id=1, source_target_pairs={{0,24},{8,16},{16,8},{24,0},{1,25},{9,17},{17,9},{25,1},{2,26},{10... | collective-permute-start | bytes 208904 | tf_op jit(solution)/shard_map/ppermute | solution.py:549
  20.3 0.6 copy-start.11
  20.9 12.3 %collective-permute-start.1 = (f32[136,128]{1,0:T(8,128)}, f32[136,128]{1,0:T(8,128)S(1)}, u32[]{:S(2)}, u32[]{:S(2)}) collective-permute-start(f32[136,128]{1,0:T(8,128)} %get-tuple-element.24.refs_0_), channel_id=1, source_target_pairs={{0,16},{8,24},{16,0},{24,8},{1,17},{9,25},{17,1},{25,9},{2,18},{10... | collective-permute-start | bytes 208904 | tf_op jit(solution)/shard_map/ppermute | solution.py:549
  22.4 11.4 %collective-permute-start = (f32[136,128]{1,0:T(8,128)}, f32[136,128]{1,0:T(8,128)S(1)}, u32[]{:S(2)}, u32[]{:S(2)}) collective-permute-start(f32[136,128]{1,0:T(8,128)} %get-tuple-element.24.refs_0_), channel_id=1, source_target_pairs={{0,8},{8,0},{16,24},{24,16},{1,9},{9,1},{17,25},{25,17},{2,10},{10... | collective-permute-start | bytes 208904 | tf_op jit(solution)/shard_map/ppermute | solution.py:549
  23.9 6.0 %collective-permute-start.5 = (f32[2,24,128]{2,1,0:T(8,128)S(1)}, f32[2,24,128]{2,1,0:T(8,128)S(1)}, u32[]{:S(2)}, u32[]{:S(2)}) collective-permute-start(f32[2,24,128]{2,1,0:T(8,128)S(1)} %constant_dynamic-update-slice_fusion.refs_4_), channel_id=1, source_target_pairs={{0,4},{1,5},{2,6},{3,7},{4,0},{5,1},{6,2},{7,3},{8,12},{9,13},{10,... | collective-permute-start | bytes 73736 | tf_op jit(solution)/shard_map/ppermute | solution.py:549
  28.1 3.8 %collective-permute-start.4 = (f32[2,24,128]{2,1,0:T(8,128)S(1)}, f32[2,24,128]{2,1,0:T(8,128)S(1)}, u32[]{:S(2)}, u32[]{:S(2)}) collective-permute-start(f32[2,24,128]{2,1,0:T(8,128)S(1)} %constant_dynamic-update-slice_fusion.refs_4_), channel_id=1, source_target_pairs={{0,2},{1,3},{2,0},{3,1},{4,6},{5,7},{6,4},{7,5},{8,10},{9,11},{10,... | collective-permute-start | bytes 73736 | tf_op jit(solution)/shard_map/ppermute | solution.py:549
  28.1 31.0 %copy-start.4 = (f32[136,128]{1,0:T(8,128)S(1)}, f32[136,128]{1,0:T(8,128)}, u32[]{:S(2)}) copy-start(f32[136,128]{1,0:T(8,128)} %get-tuple-element.24.refs_0_) | copy-start | bytes 208900
  29.9 0.6 copy-start.13
  31.9 0.6 copy-start.15
  32.5 0.6 copy-start.5
  33.2 0.6 copy-start.7
  33.8 0.6 copy-start.9
  34.4 16.8 %collective-permute-start.15 = (f32[4,280,128]{2,1,0:T(8,128)S(1)}, f32[4,280,128]{2,1,0:T(8,128)S(1)}, u32[]{:S(2)}, u32[]{:S(2)}) collective-permute-start(f32[4,280,128]{2,1,0:T(8,128)S(1)} %pad_maximum_fusion.refs_0_), channel_id=1, source_target_pairs={{0,24},{8,16},{16,8},{24,0},{1,25},{9,17},{17,9},{25,1},{2,26},{10... | collective-permute-start | bytes 1720328 | tf_op jit(solution)/shard_map/ppermute | solution.py:549
  34.9 23.6 %collective-permute-start.13 = (f32[4,280,128]{2,1,0:T(8,128)S(1)}, f32[4,280,128]{2,1,0:T(8,128)S(1)}, u32[]{:S(2)}, u32[]{:S(2)}) collective-permute-start(f32[4,280,128]{2,1,0:T(8,128)S(1)} %pad_maximum_fusion.refs_0_), channel_id=1, source_target_pairs={{0,16},{8,24},{16,0},{24,8},{1,17},{9,25},{17,1},{25,9},{2,18},{10... | collective-permute-start | bytes 1720328 | tf_op jit(solution)/shard_map/ppermute | solution.py:549
  36.4 22.1 %collective-permute-start.11 = (f32[4,280,128]{2,1,0:T(8,128)S(1)}, f32[4,280,128]{2,1,0:T(8,128)S(1)}, u32[]{:S(2)}, u32[]{:S(2)}) collective-permute-start(f32[4,280,128]{2,1,0:T(8,128)S(1)} %pad_maximum_fusion.refs_0_), channel_id=1, source_target_pairs={{0,8},{8,0},{16,24},{24,16},{1,9},{9,1},{17,25},{25,17},{2,10},{10... | collective-permute-start | bytes 1720328 | tf_op jit(solution)/shard_map/ppermute | solution.py:549
  37.9 72.6 %collective-permute-start.10 = (f32[4,280,128]{2,1,0:T(8,128)S(1)}, f32[4,280,128]{2,1,0:T(8,128)S(1)}, u32[]{:S(2)}, u32[]{:S(2)}) collective-permute-start(f32[4,280,128]{2,1,0:T(8,128)S(1)} %pad_maximum_fusion.refs_0_), channel_id=1, source_target_pairs={{0,1},{1,0},{2,3},{3,2},{4,5},{5,4},{6,7},{7,6},{8,9},{9,8},{10,11... | collective-permute-start | bytes 1720328 | tf_op jit(solution)/shard_map/ppermute | solution.py:549
  51.3 59.2 %collective-permute-start.16 = (f32[4,280,128]{2,1,0:T(8,128)S(1)}, f32[4,280,128]{2,1,0:T(8,128)S(1)}, u32[]{:S(2)}, u32[]{:S(2)}) collective-permute-start(f32[4,280,128]{2,1,0:T(8,128)S(1)} %collective-permute-done.15.refs_6_), channel_id=1, source_target_pairs={{0,1},{1,0},{2,3},{3,2},{4,5},{5,4},{6,7},{7,6},{8,9},{9,8},{10,11... | collective-permute-start | bytes 1720328 | tf_op jit(solution)/shard_map/ppermute | solution.py:549
  58.5 52.0 %collective-permute-start.14 = (f32[4,280,128]{2,1,0:T(8,128)S(1)}, f32[4,280,128]{2,1,0:T(8,128)}, u32[]{:S(2)}, u32[]{:S(2)}) collective-permute-start(f32[4,280,128]{2,1,0:T(8,128)S(1)} %collective-permute-done.13.refs_4_), channel_id=1, source_target_pairs={{0,1},{1,0},{2,3},{3,2},{4,5},{5,4},{6,7},{7,6},{8,9},{9,8},{10,11... | collective-permute-start | bytes 1720328 | tf_op jit(solution)/shard_map/ppermute | solution.py:549
  58.5 52.0 %collective-permute-start.12 = (f32[4,280,128]{2,1,0:T(8,128)S(1)}, f32[4,280,128]{2,1,0:T(8,128)}, u32[]{:S(2)}, u32[]{:S(2)}) collective-permute-start(f32[4,280,128]{2,1,0:T(8,128)S(1)} %collective-permute-done.11.refs_2_), channel_id=1, source_target_pairs={{0,1},{1,0},{2,3},{3,2},{4,5},{5,4},{6,7},{7,6},{8,9},{9,8},{10,11... | collective-permute-start | bytes 1720328 | tf_op jit(solution)/shard_map/ppermute | solution.py:549
  59.1 0.9 copy-start.6
  60.0 0.9 copy-start.8
  60.8 0.9 copy-start.10
  61.7 0.7 copy-start.12
  62.5 0.7 copy-start.14
  63.2 0.7 copy-start.16
  63.9 46.6 %copy-start = (f32[16,8192]{1,0:T(8,128)S(1)}, f32[16,8192]{1,0:T(8,128)}, u32[]{:S(2)}) copy-start(f32[16,8192]{1,0:T(8,128)} %refs_8_.1) | copy-start | bytes 1572868
  63.9 46.6 %copy-start.2 = (s32[8192]{0:T(1024)S(1)}, s32[8192]{0:T(1024)}, u32[]{:S(2)}) copy-start(s32[8192]{0:T(1024)} %param.16) | copy-start | bytes 98308
  184.0 0.7 copy-start.1
  184.7 0.6 copy-start.3
  185.3 11.3 %all-to-all-start = ((f32[32,1,1280]{2,1,0:T(1,128)}), f32[32,1,1280]{2,1,0:T(1,128)S(1)}, u32[]{:S(2)}, u32[]{:S(2)}) async-start(f32[32,1,1280]{2,1,0:T(1,128)} %copy-done.1), calls=%async_computation | async-start | bytes 327680 | tf_op jit(solution)/shard_map/all_to_all | solution.py:604
  196.6 0.7 copy-start.17

commit v4 on v3

--- a/solution.py
+++ b/solution.py
@@ -589,6 +589,7 @@
     coarse_f = f_table[0, : src_cent.shape[1]]
     coarse_g = g_table[0, : tgt_cent.shape[1]]
 
+    stacks, f_table, g_table = lax.optimization_barrier((stacks, f_table, g_table))
     stacks = [part for own in stacks for part in (own, exchange(own, "col", 1))]
     where = jnp.stack([me, row * src_cent.shape[1], col * tgt_cent.shape[1]]).astype(jnp.int32)
     partial, start_f, fine_g = fine_update(

time: 203 us -> 175 us (0.86); the launches traced: 200 us -> 174 us
  waiting for transfers between devices: 33.4 us -> 19.4 us
  local copies, waits for them, and re-layouts: 13.1 us -> 5.54 us
  starting transfers between devices: 25.9 us -> 22.1 us
    ppermute x17, waiting for transfers between devices: 26 us -> 12.1 us  [exchange(): return lax.ppermute(x, axis, [(i, i ^ flip) for i in range(count)])]
    unnamed x37 -> x13, local copies, waits for them, and re-layouts: 11.2 us -> 3.67 us
    ppermute x17, starting transfers between devices: 23.1 us -> 19.4 us  [exchange(): return lax.ppermute(x, axis, [(i, i ^ flip) for i in range(count)])]
  transfers between devices with their start and end apart: 18 -> 18, of which waited for: 7 -> 9; matrix products, arithmetic and copies ran while one was open for 1% -> 2% of each run, Pallas kernels for 23% -> 27%
where the time goes in v4:
time: 175 us; the launch traced here: 174 us
  Pallas kernels  124 us (71%)
  starting transfers between devices  22.1 us (13%)
  waiting for transfers between devices  19.4 us (11%)
  local copies, waits for them, and re-layouts  5.54 us (3%)
  other arithmetic  2.44 us (1%)
    pallas_call x1, Pallas kernels, fine_update(): pl.pallas_call(functools.partial(fine_kernel, len(stacks), slots_each, st...  73.5 us
    pallas_call x1, Pallas kernels, coarse_duals(): pl.pallas_call(functools.partial(coarse_kernel, len(src), len(tgt), store...  46.6 us
    ppermute x17, starting transfers between devices, exchange(): return lax.ppermute(x, axis, [(i, i ^ flip) for i in range(count)])  19.4 us
    ppermute x17, waiting for transfers between devices, exchange(): return lax.ppermute(x, axis, [(i, i ^ flip) for i in range(count)])  12.1 us
    all_to_all x1, waiting for transfers between devices, on_device(): lax.all_to_all(partial, AXES, split_axis=0, concat_axis=0, tiled=True)  7.36 us
    unnamed x13, local copies, waits for them, and re-layouts  3.67 us
  transfers between devices with their start and end apart: 18, of which 9 were waited for; matrix products, arithmetic and copies ran while one was open for 2% of the time, Pallas kernels for 27%

profile of v4, /device:TPU:0, one launch (start us, length us, event | category | flops | bytes accessed | tf_op | source)
XLA Modules:
  0.0 174.5 jit_solution(2914249167616531744)
XLA Ops:
  0.6 0.8 reshape.147
  1.4 0.2 convert_reduce_fusion
  1.6 0.5 multiply_add_fusion
  2.1 0.7 select_reduce_fusion
  2.8 1.7 prepare.1
  4.4 3.0 %collective-permute-start.7 = (f32[280,128]{1,0:T(8,128)}, f32[280,128]{1,0:T(8,128)S(1)}, u32[]{:S(2)}, u32[]{:S(2)}) collective-permute-start(f32[280,128]{1,0:T(8,128)} %get-tuple-element.29), channel_id=1, source_target_pairs={{0,2},{1,3},{2,0},{3,1},{4,6},{5,7},{6,4},{7,5},{8,10},{9,11},{10,... | collective-permute-start | bytes 430088 | tf_op jit(solution)/shard_map/ppermute | solution.py:549
  7.5 2.6 %collective-permute-start.8 = (f32[280,128]{1,0:T(8,128)}, f32[280,128]{1,0:T(8,128)S(1)}, u32[]{:S(2)}, u32[]{:S(2)}) collective-permute-start(f32[280,128]{1,0:T(8,128)} %get-tuple-element.29), channel_id=1, source_target_pairs={{0,4},{1,5},{2,6},{3,7},{4,0},{5,1},{6,2},{7,3},{8,12},{9,13},{10,... | collective-permute-start | bytes 430088 | tf_op jit(solution)/shard_map/ppermute | solution.py:549
  10.1 0.7 constant_dynamic-update-slice_fusion.1
  10.8 0.7 collective-permute-done.3
  11.5 0.9 collective-permute-start.4
  12.3 1.5 collective-permute-start
  13.8 3.6 %collective-permute-done.4.refs_5_ = f32[2,24,128]{2,1,0:T(8,128)S(1)} collective-permute-done((f32[2,24,128]{2,1,0:T(8,128)S(1)}, f32[2,24,128]{2,1,0:T(8,128)S(1)}, u32[]{:S(2)}, u32[]{:S(2)}) %collective-permute-start.4) | collective-permute-done | bytes 24608 | tf_op jit(solution)/shard_map/ppermute | solution.py:549
  17.4 1.5 collective-permute-start.1
  18.9 0.0 collective-permute-done.7
  18.9 1.4 collective-permute-start.2
  20.4 1.0 collective-permute-done.8
  21.4 2.5 %collective-permute-start.5 = (f32[2,24,128]{2,1,0:T(8,128)S(1)}, f32[2,24,128]{2,1,0:T(8,128)S(1)}, u32[]{:S(2)}, u32[]{:S(2)}) collective-permute-start(f32[2,24,128]{2,1,0:T(8,128)S(1)} %constant_dynamic-update-slice_fusion.refs_4_), channel_id=1, source_target_pairs={{0,4},{1,5},{2,6},{3,7},{4,0},{5,1},{6,2},{7,3},{8,12},{9,13},{10,... | collective-permute-start | bytes 73736 | tf_op jit(solution)/shard_map/ppermute | solution.py:549
  23.9 0.0 collective-permute-done.9
  23.9 1.3 collective-permute-start.6
  25.2 1.0 pad_maximum_fusion.refs_0_
  26.2 0.0 collective-permute-done.5.refs_6_
  26.2 3.3 %collective-permute-done.6.refs_7_ = f32[2,24,128]{2,1,0:T(8,128)S(1)} collective-permute-done((f32[2,24,128]{2,1,0:T(8,128)S(1)}, f32[2,24,128]{2,1,0:T(8,128)S(1)}, u32[]{:S(2)}, u32[]{:S(2)}) %collective-permute-start.6) | collective-permute-done | bytes 24608 | tf_op jit(solution)/shard_map/ppermute | solution.py:549
  29.5 0.0 collective-permute-done.1.refs_2_
  29.5 0.0 collective-permute-done.2.refs_3_
  29.5 0.6 collective-permute-start.10
  30.1 1.5 collective-permute-start.11
  31.6 1.4 collective-permute-start.12
  33.1 46.6 %coarse.1 = (f32[1,4096]{1,0:T(1,128)S(1)}, f32[1,1024]{1,0:T(1,128)S(1)}) custom-call(f32[136,128]{1,0:T(8,128)S(1)} %copy-done.4, f32[136,128]{1,0:T(8,128)S(1)} %collective-permute-done.refs_1_, f32[136,128]{1,0:T(8,128)S(1)} %collective-permute-done.1.refs_2_, f32[136,128]{1,0:T(8,128)S(1)} %collective-permute-done.2.refs_3_, ...), custom_call_target="tpu_custom_call" | custom-call | flops 167772160 | bytes 491520 | tf_op jit(solution)/shard_map/coarse/pallas_call | solution.py:276
  79.6 0.0 collective-permute-done.10.refs_2_
  79.7 0.1 collective-permute-start.13
  79.8 0.5 collective-permute-start.14
  80.2 0.1 collective-permute-start.15
  80.3 0.4 collective-permute-start.16
  80.8 0.1 pad_add_fusion.where_ref
  80.8 0.9 collective-permute-done.13.refs_1_
  81.7 1.6 collective-permute-done.14.refs_3_
  83.4 0.1 collective-permute-done.15.refs_5_
  83.5 0.8 collective-permute-done.16.refs_7_
  84.3 1.0 copy-done
  85.4 73.5 %fine.1 = (f32[32,1,1280]{2,1,0:T(1,128)S(1)}, f32[16,128]{1,0:T(8,128)S(1)}, f32[64,128]{1,0:T(8,128)}) custom-call(s32[3]{0:T(128)S(1)} %pad_add_fusion.where_ref, f32[4,280,128]{2,1,0:T(8,128)S(1)} %pad_maximum_fusion.refs_0_, f32[4,280,128]{2,1,0:T(8,128)S(1)} %collective-permute-done.13.refs_1_, f32[4,280,128]{2,1,0:T(8,128)S(1)} %collective-permute-done.10.refs_2_, ...), custom_call_target="tpu_custom_call" | custom-call | tf_op jit(solution)/shard_map/fine/pallas_call | solution.py:493
  158.9 0.7 copy-done.1
  159.6 0.6 copy-done.3
  160.2 2.7 %all-to-all-start = ((f32[32,1,1280]{2,1,0:T(1,128)}), f32[32,1,1280]{2,1,0:T(1,128)S(1)}, u32[]{:S(2)}, u32[]{:S(2)}) async-start(f32[32,1,1280]{2,1,0:T(1,128)} %copy-done.1), calls=%async_computation | async-start | bytes 327680 | tf_op jit(solution)/shard_map/all_to_all | solution.py:605
  162.8 0.6 slice.6
  163.4 0.5 slice_bitcast_fusion
  164.0 7.4 %all-to-all-done.partial = f32[32,1,1280]{2,1,0:T(1,128)S(1)} async-done(((f32[32,1,1280]{2,1,0:T(1,128)}), f32[32,1,1280]{2,1,0:T(1,128)S(1)}, u32[]{:S(2)}, u32[]{:S(2)}) %all-to-all-start) | async-done | bytes 163872 | tf_op jit(solution)/shard_map/all_to_all | solution.py:605
  171.3 0.7 copy-done.5
  172.0 2.5 %finish.1 = f32[16,128]{1,0:T(8,128)} custom-call(s32[128]{0:T(128)} %get-tuple-element.50.slot_ref, f32[32,1,1280]{2,1,0:T(1,128)} %copy-done.5, f32[16,128]{1,0:T(8,128)} %copy-done.3), custom_call_target="tpu_custom_call" | custom-call | tf_op jit(solution)/shard_map/finish/pallas_call | solution.py:537
  (15 shorter events, 0.0 us)
Async XLA Ops:
  4.4 14.5 %collective-permute-start.7 = (f32[280,128]{1,0:T(8,128)}, f32[280,128]{1,0:T(8,128)S(1)}, u32[]{:S(2)}, u32[]{:S(2)}) collective-permute-start(f32[280,128]{1,0:T(8,128)} %get-tuple-element.29), channel_id=1, source_target_pairs={{0,2},{1,3},{2,0},{3,1},{4,6},{5,7},{6,4},{7,5},{8,10},{9,11},{10,... | collective-permute-start | bytes 430088 | tf_op jit(solution)/shard_map/ppermute | solution.py:549
  7.5 13.9 %collective-permute-start.8 = (f32[280,128]{1,0:T(8,128)}, f32[280,128]{1,0:T(8,128)S(1)}, u32[]{:S(2)}, u32[]{:S(2)}) collective-permute-start(f32[280,128]{1,0:T(8,128)} %get-tuple-element.29), channel_id=1, source_target_pairs={{0,4},{1,5},{2,6},{3,7},{4,0},{5,1},{6,2},{7,3},{8,12},{9,13},{10,... | collective-permute-start | bytes 430088 | tf_op jit(solution)/shard_map/ppermute | solution.py:549
  10.1 13.8 %collective-permute-start.9 = (f32[280,128]{1,0:T(8,128)}, f32[280,128]{1,0:T(8,128)S(1)}, u32[]{:S(2)}, u32[]{:S(2)}) collective-permute-start(f32[280,128]{1,0:T(8,128)} %get-tuple-element.29), channel_id=1, source_target_pairs={{0,6},{1,7},{2,4},{3,5},{4,2},{5,3},{6,0},{7,1},{8,14},{9,15},{10,... | collective-permute-start | bytes 430088 | tf_op jit(solution)/shard_map/ppermute | solution.py:549
  10.1 1.4 collective-permute-start.3
  11.5 6.0 %collective-permute-start.4 = (f32[2,24,128]{2,1,0:T(8,128)S(1)}, f32[2,24,128]{2,1,0:T(8,128)S(1)}, u32[]{:S(2)}, u32[]{:S(2)}) collective-permute-start(f32[2,24,128]{2,1,0:T(8,128)S(1)} %constant_dynamic-update-slice_fusion.refs_4_), channel_id=1, source_target_pairs={{0,2},{1,3},{2,0},{3,1},{4,6},{5,7},{6,4},{7,5},{8,10},{9,11},{10,... | collective-permute-start | bytes 73736 | tf_op jit(solution)/shard_map/ppermute | solution.py:549
  12.3 17.2 %collective-permute-start = (f32[136,128]{1,0:T(8,128)}, f32[136,128]{1,0:T(8,128)S(1)}, u32[]{:S(2)}, u32[]{:S(2)}) collective-permute-start(f32[136,128]{1,0:T(8,128)} %get-tuple-element.30.refs_0_), channel_id=1, source_target_pairs={{0,8},{8,0},{16,24},{24,16},{1,9},{9,1},{17,25},{25,17},{2,10},{10... | collective-permute-start | bytes 208904 | tf_op jit(solution)/shard_map/ppermute | solution.py:549
  17.4 12.1 %collective-permute-start.1 = (f32[136,128]{1,0:T(8,128)}, f32[136,128]{1,0:T(8,128)S(1)}, u32[]{:S(2)}, u32[]{:S(2)}) collective-permute-start(f32[136,128]{1,0:T(8,128)} %get-tuple-element.30.refs_0_), channel_id=1, source_target_pairs={{0,16},{8,24},{16,0},{24,8},{1,17},{9,25},{17,1},{25,9},{2,18},{10... | collective-permute-start | bytes 208904 | tf_op jit(solution)/shard_map/ppermute | solution.py:549
  18.9 10.6 %collective-permute-start.2 = (f32[136,128]{1,0:T(8,128)}, f32[136,128]{1,0:T(8,128)S(1)}, u32[]{:S(2)}, u32[]{:S(2)}) collective-permute-start(f32[136,128]{1,0:T(8,128)} %get-tuple-element.30.refs_0_), channel_id=1, source_target_pairs={{0,24},{8,16},{16,8},{24,0},{1,25},{9,17},{17,9},{25,1},{2,26},{10... | collective-permute-start | bytes 208904 | tf_op jit(solution)/shard_map/ppermute | solution.py:549
  21.4 4.8 %collective-permute-start.5 = (f32[2,24,128]{2,1,0:T(8,128)S(1)}, f32[2,24,128]{2,1,0:T(8,128)S(1)}, u32[]{:S(2)}, u32[]{:S(2)}) collective-permute-start(f32[2,24,128]{2,1,0:T(8,128)S(1)} %constant_dynamic-update-slice_fusion.refs_4_), channel_id=1, source_target_pairs={{0,4},{1,5},{2,6},{3,7},{4,0},{5,1},{6,2},{7,3},{8,12},{9,13},{10,... | collective-permute-start | bytes 73736 | tf_op jit(solution)/shard_map/ppermute | solution.py:549
  23.9 5.6 %collective-permute-start.6 = (f32[2,24,128]{2,1,0:T(8,128)S(1)}, f32[2,24,128]{2,1,0:T(8,128)S(1)}, u32[]{:S(2)}, u32[]{:S(2)}) collective-permute-start(f32[2,24,128]{2,1,0:T(8,128)S(1)} %constant_dynamic-update-slice_fusion.refs_4_), channel_id=1, source_target_pairs={{0,6},{1,7},{2,4},{3,5},{4,2},{5,3},{6,0},{7,1},{8,14},{9,15},{10,... | collective-permute-start | bytes 73736 | tf_op jit(solution)/shard_map/ppermute | solution.py:549
  25.2 7.8 %copy-start.4 = (f32[136,128]{1,0:T(8,128)S(1)}, f32[136,128]{1,0:T(8,128)}, u32[]{:S(2)}) copy-start(f32[136,128]{1,0:T(8,128)} %get-tuple-element.30.refs_0_) | copy-start | bytes 208900
  29.5 50.1 %collective-permute-start.10 = (f32[4,280,128]{2,1,0:T(8,128)S(1)}, f32[4,280,128]{2,1,0:T(8,128)S(1)}, u32[]{:S(2)}, u32[]{:S(2)}) collective-permute-start(f32[4,280,128]{2,1,0:T(8,128)S(1)} %pad_maximum_fusion.refs_0_), channel_id=1, source_target_pairs={{0,8},{8,0},{16,24},{24,16},{1,9},{9,1},{17,25},{25,17},{2,10},{10... | collective-permute-start | bytes 1720328 | tf_op jit(solution)/shard_map/ppermute | solution.py:549
  30.1 49.5 %collective-permute-start.11 = (f32[4,280,128]{2,1,0:T(8,128)S(1)}, f32[4,280,128]{2,1,0:T(8,128)S(1)}, u32[]{:S(2)}, u32[]{:S(2)}) collective-permute-start(f32[4,280,128]{2,1,0:T(8,128)S(1)} %pad_maximum_fusion.refs_0_), channel_id=1, source_target_pairs={{0,16},{8,24},{16,0},{24,8},{1,17},{9,25},{17,1},{25,9},{2,18},{10... | collective-permute-start | bytes 1720328 | tf_op jit(solution)/shard_map/ppermute | solution.py:549
  31.6 48.0 %collective-permute-start.12 = (f32[4,280,128]{2,1,0:T(8,128)S(1)}, f32[4,280,128]{2,1,0:T(8,128)S(1)}, u32[]{:S(2)}, u32[]{:S(2)}) collective-permute-start(f32[4,280,128]{2,1,0:T(8,128)S(1)} %pad_maximum_fusion.refs_0_), channel_id=1, source_target_pairs={{0,24},{8,16},{16,8},{24,0},{1,25},{9,17},{17,9},{25,1},{2,26},{10... | collective-permute-start | bytes 1720328 | tf_op jit(solution)/shard_map/ppermute | solution.py:549
  79.6 4.7 %copy-start.2 = (s32[8192]{0:T(1024)S(1)}, s32[8192]{0:T(1024)}, u32[]{:S(2)}) copy-start(s32[8192]{0:T(1024)} %param.16) | copy-start | bytes 98308
  79.7 2.0 %collective-permute-start.13 = (f32[4,280,128]{2,1,0:T(8,128)S(1)}, f32[4,280,128]{2,1,0:T(8,128)S(1)}, u32[]{:S(2)}, u32[]{:S(2)}) collective-permute-start(f32[4,280,128]{2,1,0:T(8,128)S(1)} %pad_maximum_fusion.refs_0_), channel_id=1, source_target_pairs={{0,1},{1,0},{2,3},{3,2},{4,5},{5,4},{6,7},{7,6},{8,9},{9,8},{10,11... | collective-permute-start | bytes 1720328 | tf_op jit(solution)/shard_map/ppermute | solution.py:549
  79.8 3.6 %collective-permute-start.14 = (f32[4,280,128]{2,1,0:T(8,128)S(1)}, f32[4,280,128]{2,1,0:T(8,128)S(1)}, u32[]{:S(2)}, u32[]{:S(2)}) collective-permute-start(f32[4,280,128]{2,1,0:T(8,128)S(1)} %collective-permute-done.10.refs_2_), channel_id=1, source_target_pairs={{0,1},{1,0},{2,3},{3,2},{4,5},{5,4},{6,7},{7,6},{8,9},{9,8},{10,11... | collective-permute-start | bytes 1720328 | tf_op jit(solution)/shard_map/ppermute | solution.py:549
  80.2 3.2 %collective-permute-start.15 = (f32[4,280,128]{2,1,0:T(8,128)S(1)}, f32[4,280,128]{2,1,0:T(8,128)}, u32[]{:S(2)}, u32[]{:S(2)}) collective-permute-start(f32[4,280,128]{2,1,0:T(8,128)S(1)} %collective-permute-done.11.refs_4_), channel_id=1, source_target_pairs={{0,1},{1,0},{2,3},{3,2},{4,5},{5,4},{6,7},{7,6},{8,9},{9,8},{10,11... | collective-permute-start | bytes 1720328 | tf_op jit(solution)/shard_map/ppermute | solution.py:549
  80.3 4.0 %collective-permute-start.16 = (f32[4,280,128]{2,1,0:T(8,128)S(1)}, f32[4,280,128]{2,1,0:T(8,128)}, u32[]{:S(2)}, u32[]{:S(2)}) collective-permute-start(f32[4,280,128]{2,1,0:T(8,128)S(1)} %collective-permute-done.12.refs_6_), channel_id=1, source_target_pairs={{0,1},{1,0},{2,3},{3,2},{4,5},{5,4},{6,7},{7,6},{8,9},{9,8},{10,11... | collective-permute-start | bytes 1720328 | tf_op jit(solution)/shard_map/ppermute | solution.py:549
  84.3 1.0 copy-start
  158.9 0.7 copy-start.1
  159.6 0.6 copy-start.3
  160.2 11.2 %all-to-all-start = ((f32[32,1,1280]{2,1,0:T(1,128)}), f32[32,1,1280]{2,1,0:T(1,128)S(1)}, u32[]{:S(2)}, u32[]{:S(2)}) async-start(f32[32,1,1280]{2,1,0:T(1,128)} %copy-done.1), calls=%async_computation | async-start | bytes 327680 | tf_op jit(solution)/shard_map/all_to_all | solution.py:605
  171.3 0.7 copy-start.5

commit v5 on v4

--- a/solution.py
+++ b/solution.py
@@ -29,6 +29,8 @@
 SMALL = 2.0**-80
 LARGE = 2.0**100
 MIB = 1024 * 1024
+SLOT_AT = 2 * LANES + F
+TGT_AT = SLOT_AT + 8
 AXES = ("row", "col")
 
 VMEM = pl.BlockSpec(memory_space=pltpu.VMEM)
@@ -97,7 +99,7 @@
 
 
 def prepare_kernel(
-    src_pts, cluster, table, src_cent, src_mass, tgt_cent, tgt_mass, bundle, src_own, tgt_own
+    src_pts, cluster, table, src_cent, src_mass, tgt_a, mass_a, tgt_b, mass_b, bundle, src_own
 ):
     for half in range(2):
         rows = slice(8 * half, 8 * half + 8)
@@ -112,22 +114,23 @@
     bundle[at + F : at + F + table.shape[0], :] = table[...].astype(jnp.float32)
     at = F * src_mass.shape[0]
     src_own[at : at + src_mass.shape[0], :] = src_mass[...]
-    tgt_own[0, 0:F, :] = tgt_cent[...]
-    tgt_own[0, F : F + 8, :] = jnp.broadcast_to(tgt_mass[...], (8, LANES))
-
-
-def prepare(src_pts, cluster, table, src_cent, src_mass, tgt_cent, tgt_mass):
+    bundle[TGT_AT : TGT_AT + F, :] = tgt_a[...]
+    bundle[TGT_AT + F : TGT_AT + 2 * F, :] = tgt_b[...]
+    masses = jnp.concatenate([mass_a[...], mass_b[...], jnp.ones((6, LANES), jnp.float32)], 0)
+    bundle[TGT_AT + 2 * F :, :] = masses
+
+
+def prepare(src_pts, cluster, table, src_cent, src_mass, *tgt):
     return pl.pallas_call(
         prepare_kernel,
         out_shape=(
-            jax.ShapeDtypeStruct((2 * LANES + F + 8, LANES), jnp.float32),
+            jax.ShapeDtypeStruct((TGT_AT + 2 * F + 8, LANES), jnp.float32),
             jax.ShapeDtypeStruct(((F + 1) * src_mass.shape[0], LANES), jnp.float32),
-            jax.ShapeDtypeStruct((1, F + 8, LANES), jnp.float32),
         ),
-        in_specs=[VMEM] * 7,
-        out_specs=(VMEM,) * 3,
+        in_specs=[VMEM] * 9,
+        out_specs=(VMEM,) * 2,
         name="prepare",
-    )(src_pts, cluster, table, src_cent, src_mass, tgt_cent, tgt_mass)
+    )(src_pts, cluster, table, src_cent, src_mass, *tgt)
 
 
 def coarse_kernel(n_src, n_tgt, stored, *refs):
@@ -138,8 +141,11 @@
     wide_src = src[0].shape[0] // (F + 1)
     piece = wide_src * LANES
     tiles = kt // LANES
-    y = jnp.concatenate([ref[e, 0:F, :] for ref in tgt for e in range(2)], 1)
-    b = jnp.concatenate([ref[e, F : F + 1, :] for ref in tgt for e in range(2)], 1)
+    y = jnp.concatenate(
+        [ref[TGT_AT + F * e : TGT_AT + F * e + F, :] for ref in tgt for e in range(2)], 1
+    )
+    at = TGT_AT + 2 * F
+    b = jnp.concatenate([ref[at + e : at + e + 1, :] for ref in tgt for e in range(2)], 1)
     right = pack_right(y, jnp.log2(b) - SCALE * square_norm(y))
     ones = jnp.ones((F, LANES), jnp.bfloat16)
     zero = jnp.zeros((8, kt), jnp.float32)
@@ -271,7 +277,7 @@
 
 def coarse_duals(src, tgt):
     ks = sum(part.shape[0] // (F + 1) * LANES for part in src)
-    kt = sum(2 * part.shape[2] for part in tgt)
+    kt = sum(2 * part.shape[1] for part in tgt)
     stored = ks * kt * 4 <= 16 * MIB
     return pl.pallas_call(
         functools.partial(coarse_kernel, len(src), len(tgt), stored),
@@ -305,33 +311,9 @@
     return out
 
 
-def fine_kernel(n_stacks, slots_each, stride, where_ref, *refs):
-    stacks = refs[:n_stacks]
-    tgt_pts, tgt_cluster, f_table, g_table, partial_out, start_f_out, fine_g_out = refs[
-        n_stacks : n_stacks + 7
-    ]
-    bundle, start_g, packed, col_sum, col_top, codes, arrived, slots, order, count = refs[
-        n_stacks + 7 :
-    ]
-    devices = bundle.shape[0]
-    depth = devices // n_stacks
-    me, src_flip, tgt_flip = where_ref[0], where_ref[1], where_ref[2]
-
-    copies = [
-        pltpu.make_async_copy(
-            stacks[n], bundle.at[pl.ds(n * depth, depth)], arrived.at[n]
-        )
-        for n in range(n_stacks)
-    ]
-    for copy in copies:
-        copy.start()
-
-    def sender(place):
-        stack = place // depth
-        return me ^ (2 * depth * (stack // 2) + 2 * (place % depth) + stack % 2)
-
+def targets_kernel(flip_ref, tgt_pts, tgt_cluster, g_table, packed, start_g):
     for k in range(2 * TB_DEV // 8):
-        index = tgt_cluster[8 * k : 8 * k + 8, :] ^ tgt_flip
+        index = tgt_cluster[8 * k : 8 * k + 8, :] ^ flip_ref[0]
         start_g[8 * k : 8 * k + 8, :] = look_up(g_table, index)
 
     def pack_target(t, carry):
@@ -340,31 +322,72 @@
         rows = pack_right(y, SCALE * (g - square_norm(y)))
         rows = jnp.concatenate([rows, jnp.zeros((LANES - KDIM, BLK), jnp.bfloat16)], 0)
         packed[t] = jnp.transpose(rows.astype(jnp.float32)).astype(jnp.bfloat16)
-        count[t] = 0
         return carry
 
     lax.fori_loop(0, TB_DEV, pack_target, 0, unroll=BLOCKS)
     packed[TB_DEV] = jnp.zeros((BLK, LANES), jnp.bfloat16)
-    count[TB_DEV] = 0
-
-    for copy in copies:
+
+
+def pack_targets(flip, tgt_pts, tgt_cluster, g_table):
+    return pl.pallas_call(
+        targets_kernel,
+        out_shape=(
+            jax.ShapeDtypeStruct((TB_DEV + 1, BLK, LANES), jnp.bfloat16),
+            jax.ShapeDtypeStruct((2 * TB_DEV, LANES), jnp.float32),
+        ),
+        in_specs=[SMEM] + [VMEM] * 3,
+        out_specs=(VMEM, VMEM),
+        compiler_params=pltpu.CompilerParams(vmem_limit_bytes=16 * MIB),
+        name="targets",
+    )(flip, tgt_pts, tgt_cluster, g_table)
+
+
+def fine_kernel(n_stacks, slots_each, stride, where_ref, *refs):
+    stacks = refs[:n_stacks]
+    packed, start_g, f_table, partial_out, start_f_out, fine_g_out = refs[n_stacks : n_stacks + 6]
+    bundle, slot_rows, col_sum, col_top, codes, arrived, slots, order, count = refs[n_stacks + 6 :]
+    devices = bundle.shape[0]
+    depth = devices // n_stacks
+    me, src_flip = where_ref[0], where_ref[1]
+
+    def copy_of(n, first, rows, to, sem):
+        source = stacks[n].at[:, pl.ds(first, rows), :]
+        return pltpu.make_async_copy(source, to.at[pl.ds(n * depth, depth)], arrived.at[sem])
+
+    early = [copy_of(n, SLOT_AT, 8, slot_rows, n) for n in range(n_stacks)]
+    late = [copy_of(n, 0, SLOT_AT, bundle, n_stacks + n) for n in range(n_stacks)]
+    for copy in early + late:
+        copy.start()
+
+    def sender(place):
+        stack = place // depth
+        return me ^ (2 * depth * (stack // 2) + 2 * (place % depth) + stack % 2)
+
+    for t in range(TB_DEV + 1):
+        count[t] = 0
+    for copy in early:
         copy.wait()
-    index = bundle[0, 2 * LANES : 2 * LANES + F, :].astype(jnp.int32) ^ src_flip
-    for half in range(2):
-        rows = slice(8 * half, 8 * half + 8)
-        start_f_out[rows, :] = look_up(f_table, index[rows])
 
     at = me * stride
 
     def slot_row(n, carry):
-        codes[pl.ds(n, 1), :] = bundle[n, pl.ds(2 * LANES + F + at // LANES, 1), :].astype(jnp.int32)
+        codes[pl.ds(n, 1), :] = slot_rows[n, pl.ds(at // LANES, 1), :].astype(jnp.int32)
         return carry
 
     lax.fori_loop(0, devices, slot_row, 0, unroll=BLOCKS)
     codes[...] = pltpu.roll(codes[...], (LANES - at % LANES) % LANES, 1)
-    copy = pltpu.make_async_copy(codes, slots, arrived.at[0])
-    copy.start()
-    copy.wait()
+    to_scalars = pltpu.make_async_copy(codes, slots, arrived.at[2 * n_stacks])
+    to_scalars.start()
+
+    def fill(ref, value):
+        def body(t, carry):
+            ref[t] = jnp.full(ref.shape[1:], value, jnp.float32)
+            return carry
+
+        lax.fori_loop(0, ref.shape[0], body, 0)
+
+    fill(col_sum, 0.0)
+    to_scalars.wait()
 
     total = devices * slots_each
     unroll = math.gcd(PAIRS, total)
@@ -380,6 +403,12 @@
         return used + step, unused - (1 - step)
 
     used, _ = lax.fori_loop(0, total, place, (jnp.int32(0), jnp.int32(total - 1)), unroll=16)
+    for copy in late:
+        copy.wait()
+    index = bundle[0, 2 * LANES : SLOT_AT, :].astype(jnp.int32) ^ src_flip
+    for half in range(2):
+        rows = slice(8 * half, 8 * half + 8)
+        start_f_out[rows, :] = look_up(f_table, index[rows])
 
     def cluster_rows(p):
         code = slots[p // slots_each, p % slots_each] - 1
@@ -413,12 +442,6 @@
         span = pl.ds(pl.multiple_of(p % slots_each * BLK, BLK), BLK)
         partial_out[sender(d), :, span] = value
 
-    def fill(ref, value):
-        def body(t, carry):
-            ref[t] = jnp.full(ref.shape[1:], value, jnp.float32)
-            return carry
-        lax.fori_loop(0, ref.shape[0], body, 0)
-
     def pair(p, f, least, most):
         t, d, f, z = product(p, f)
         e = jnp.exp2(z)
@@ -448,7 +471,6 @@
         fine_g_out[pl.ds(pl.multiple_of(2 * t, 2), 2), :] = 0.5 * (g + term)
         return jnp.minimum(least, s), jnp.maximum(most, s)
 
-    fill(col_sum, 0.0)
     least = jnp.full((1, BLK), jnp.inf, jnp.float32)
     least, most = lax.fori_loop(0, (used + unroll - 1) // unroll, pairs, (least, jnp.zeros((1, BLK), jnp.float32)))
     low, high = jnp.full((2, LANES), jnp.inf, jnp.float32), jnp.zeros((2, LANES), jnp.float32)
@@ -488,7 +510,7 @@
 
         lax.fori_loop(0, TB_DEV, lanes, 0)
 
-def fine_update(where, stacks, tgt_pts, tgt_cluster, f_table, g_table, slots_each, stride):
+def fine_update(where, stacks, packed, start_g, f_table, slots_each, stride):
     devices = sum(stack.shape[0] for stack in stacks)
     return pl.pallas_call(
         functools.partial(fine_kernel, len(stacks), slots_each, stride),
@@ -497,23 +519,22 @@
             jax.ShapeDtypeStruct((F, LANES), jnp.float32),
             jax.ShapeDtypeStruct((2 * TB_DEV, LANES), jnp.float32),
         ),
-        in_specs=[SMEM] + [pl.BlockSpec(memory_space=pl.ANY)] * len(stacks) + [VMEM] * 4,
+        in_specs=[SMEM] + [pl.BlockSpec(memory_space=pl.ANY)] * len(stacks) + [VMEM] * 3,
         out_specs=(VMEM, VMEM, VMEM),
         scratch_shapes=[
-            pltpu.VMEM((devices,) + stacks[0].shape[1:], jnp.float32),
-            pltpu.VMEM((2 * TB_DEV, LANES), jnp.float32),
-            pltpu.VMEM((TB_DEV + 1, BLK, LANES), jnp.bfloat16),
+            pltpu.VMEM((devices, SLOT_AT, LANES), jnp.float32),
+            pltpu.VMEM((devices, 8, LANES), jnp.float32),
             pltpu.VMEM((TB_DEV + 1, BLK, LANES), jnp.float32),
             pltpu.VMEM((TB_DEV + 1, BLK, LANES), jnp.float32),
             pltpu.VMEM((devices, LANES), jnp.int32),
-            pltpu.SemaphoreType.DMA((len(stacks),)),
+            pltpu.SemaphoreType.DMA((2 * len(stacks) + 1,)),
             pltpu.SMEM((devices, LANES), jnp.int32),
             pltpu.SMEM((devices * slots_each,), jnp.int32),
             pltpu.SMEM((TB_DEV + 1,), jnp.int32),
         ],
-        compiler_params=pltpu.CompilerParams(vmem_limit_bytes=48 * MIB),
+        compiler_params=pltpu.CompilerParams(vmem_limit_bytes=44 * MIB),
         name="fine",
-    )(where, *stacks, tgt_pts, tgt_cluster, f_table, g_table)
+    )(where, *stacks, packed, start_g, f_table)
 
 
 def finish_kernel(slots_each, slot_ref, partial, start_f, fine_f_out, gathered):
@@ -569,38 +590,36 @@
     filled = owners * stride + slot_ids % slots_each
     places = jnp.arange(devices * stride, dtype=jnp.int32)
     table = jnp.sum(jnp.where(filled[None, :] == places[:, None], codes[None, :], 0), 1)
-    bundle, src_own, tgt_own = prepare(
+    flat_mass = tgt_mass.reshape(-1, LANES)
+    bundle, src_own = prepare(
         src_pts,
         src_cluster.reshape(F, LANES),
         table.reshape(-1, LANES),
         src_cent,
         src_mass.reshape(-1, LANES),
         tgt_cent,
-        tgt_mass.reshape(-1, LANES),
+        flat_mass,
+        exchange(tgt_cent, "col", 1),
+        exchange(flat_mass, "col", 1),
     )
 
-    tgt_pair = jnp.concatenate([tgt_own, exchange(tgt_own, "col", 1)], 0)
+    along = [bundle] + [exchange(bundle, "col", k) for k in range(2, n_col, 2)]
     src_all = [src_own] + [exchange(src_own, "row", k) for k in range(1, n_row)]
-    tgt_all = [tgt_pair] + [exchange(tgt_pair, "col", k) for k in range(2, n_col, 2)]
-    stack = jnp.stack([bundle] + [exchange(bundle, "col", k) for k in range(2, n_col, 2)])
-    src_all, tgt_all, stack = lax.optimization_barrier((src_all, tgt_all, stack))
+    stack = jnp.stack([part[:TGT_AT] for part in along])
+    src_all, along, stack = lax.optimization_barrier((src_all, along, stack))
     stacks = [stack] + [exchange(stack, "row", k) for k in range(1, n_row)]
-    f_table, g_table = coarse_duals(src_all, tgt_all)
+    f_table, g_table = coarse_duals(src_all, along)
     coarse_f = f_table[0, : src_cent.shape[1]]
     coarse_g = g_table[0, : tgt_cent.shape[1]]
 
     stacks, f_table, g_table = lax.optimization_barrier((stacks, f_table, g_table))
     stacks = [part for own in stacks for part in (own, exchange(own, "col", 1))]
-    where = jnp.stack([me, row * src_cent.shape[1], col * tgt_cent.shape[1]]).astype(jnp.int32)
+    flip = (col * tgt_cent.shape[1]).astype(jnp.int32).reshape(1)
+    tgt_cluster = tgt_cluster.reshape(2 * TB_DEV, LANES)
+    packed, start_g = pack_targets(flip, tgt_pts, tgt_cluster, g_table)
+    where = jnp.stack([me, row * src_cent.shape[1]]).astype(jnp.int32)
     partial, start_f, fine_g = fine_update(
-        where,
-        stacks,
-        tgt_pts,
-        tgt_cluster.reshape(2 * TB_DEV, LANES),
-        f_table,
-        g_table,
-        slots_each,
-        stride,
+        where, stacks, packed, start_g, f_table, slots_each, stride
     )
     returned = lax.all_to_all(partial, AXES, split_axis=0, concat_axis=0, tiled=True)
     fine_f = finish(slot_ids, returned, start_f, slots_each)

time: 175 us -> 175 us (level); the launches traced: 174 us -> 172 us
  waiting for transfers between devices: 19.4 us -> 15.7 us
    all_to_all x1, starting transfers between devices: 2.68 us -> 6.42 us  [on_device(): lax.all_to_all(partial, AXES, split_axis=0, concat_axis=0, tiled=True)]
    ppermute x17 -> x15, waiting for transfers between devices: 12.1 us -> 8.34 us  [exchange(): return lax.ppermute(x, axis, [(i, i ^ flip) for i in range(count)])]
    ppermute x17 -> x15, starting transfers between devices: 19.4 us -> 16.8 us  [exchange(): return lax.ppermute(x, axis, [(i, i ^ flip) for i in range(count)])]
    unnamed x13 -> x18, local copies, waits for them, and re-layouts: 3.67 us -> 3.58 us
  transfers between devices with their start and end apart: 18 -> 16, of which waited for: 9 -> 6; matrix products, arithmetic and copies ran while one was open for 2% -> 3% of each run, Pallas kernels for 27% -> 28%
where the time goes in v5:
time: 175 us; the launch traced here: 172 us
  Pallas kernels  124 us (71%)
  starting transfers between devices  23.2 us (13%)
  waiting for transfers between devices  15.7 us (9%)
  local copies, waits for them, and re-layouts  6.4 us (4%)
    pallas_call x1, Pallas kernels, fine_update(): pl.pallas_call(functools.partial(fine_kernel, len(stacks), slots_each, st...  72.3 us
    pallas_call x1, Pallas kernels, coarse_duals(): pl.pallas_call(functools.partial(coarse_kernel, len(src), len(tgt), store...  46.5 us
    ppermute x15, starting transfers between devices, exchange(): return lax.ppermute(x, axis, [(i, i ^ flip) for i in range(count)])  16.8 us
    ppermute x15, waiting for transfers between devices, exchange(): return lax.ppermute(x, axis, [(i, i ^ flip) for i in range(count)])  8.34 us
    all_to_all x1, waiting for transfers between devices, on_device(): lax.all_to_all(partial, AXES, split_axis=0, concat_axis=0, tiled=True)  7.36 us
    all_to_all x1, starting transfers between devices, on_device(): lax.all_to_all(partial, AXES, split_axis=0, concat_axis=0, tiled=True)  6.42 us
    unnamed x18, local copies, waits for them, and re-layouts  3.58 us
  transfers between devices with their start and end apart: 16, of which 6 were waited for; matrix products, arithmetic and copies ran while one was open for 3% of the time, Pallas kernels for 28%

profile of v5, /device:TPU:0, one launch (start us, length us, event | category | flops | bytes accessed | tf_op | source)
XLA Modules:
  0.0 171.7 jit_solution(16273478330466715487)
XLA Ops:
  0.6 0.5 collective-permute-start.1
  1.1 0.1 collective-permute-start
  1.2 0.8 reshape.150
  2.0 0.2 convert_reduce_fusion
  2.2 0.6 multiply_add_fusion
  2.8 0.7 select_reduce_fusion
  3.5 0.0 collective-permute-done.1.mass_b
  3.5 0.0 collective-permute-done.tgt_b
  3.5 0.5 copy-done.8
  4.0 0.1 copy-done.7
  4.1 1.7 prepare.1
  5.8 5.1 %collective-permute-start.7 = (f32[320,128]{1,0:T(8,128)}, f32[320,128]{1,0:T(8,128)S(1)}, u32[]{:S(2)}, u32[]{:S(2)}) collective-permute-start(f32[320,128]{1,0:T(8,128)} %get-tuple-element.34.refs_4_), channel_id=1, source_target_pairs={{0,6},{1,7},{2,4},{3,5},{4,2},{5,3},{6,0},{7,1},{8,14},{9,15},{10,... | collective-permute-start | bytes 491528 | tf_op jit(solution)/shard_map/ppermute | solution.py:570
  10.9 0.0 collective-permute-start.6
  10.9 0.6 collective-permute-start.5
  11.5 1.6 collective-permute-start.2
  13.2 1.5 collective-permute-start.3
  14.7 0.9 slice_bitcast_fusion.3
  15.6 0.6 collective-permute-done.7.refs_7_
  16.2 2.7 %collective-permute-start.4 = (f32[136,128]{1,0:T(8,128)}, f32[136,128]{1,0:T(8,128)S(1)}, u32[]{:S(2)}, u32[]{:S(2)}) collective-permute-start(f32[136,128]{1,0:T(8,128)} %get-tuple-element.30.refs_0_), channel_id=1, source_target_pairs={{0,24},{8,16},{16,8},{24,0},{1,25},{9,17},{17,9},{25,1},{2,26},{10... | collective-permute-start | bytes 208904 | tf_op jit(solution)/shard_map/ppermute | solution.py:570
  18.9 6.3 %collective-permute-done.6.refs_6_ = f32[320,128]{1,0:T(8,128)S(1)} collective-permute-done((f32[320,128]{1,0:T(8,128)}, f32[320,128]{1,0:T(8,128)S(1)}, u32[]{:S(2)}, u32[]{:S(2)}) %collective-permute-start.6) | collective-permute-done | bytes 163872 | tf_op jit(solution)/shard_map/ppermute | solution.py:570
  25.2 0.0 collective-permute-done.5.refs_5_
  25.3 0.1 pad_maximum_fusion.refs_0_
  25.3 0.0 collective-permute-done.2.refs_1_
  25.3 0.0 collective-permute-done.3.refs_2_
  25.4 2.5 %collective-permute-start.10 = (f32[4,280,128]{2,1,0:T(8,128)S(1)}, f32[4,280,128]{2,1,0:T(8,128)S(1)}, u32[]{:S(2)}, u32[]{:S(2)}) collective-permute-start(f32[4,280,128]{2,1,0:T(8,128)S(1)} %pad_maximum_fusion.refs_0_), channel_id=1, source_target_pairs={{0,24},{8,16},{16,8},{24,0},{1,25},{9,17},{17,9},{25,1},{2,26},{10... | collective-permute-start | bytes 1720328 | tf_op jit(solution)/shard_map/ppermute | solution.py:570
  27.9 0.5 collective-permute-start.8
  28.4 0.5 collective-permute-start.9
  28.9 46.5 %coarse.1 = (f32[1,4096]{1,0:T(1,128)S(1)}, f32[1,1024]{1,0:T(1,128)S(1)}) custom-call(f32[136,128]{1,0:T(8,128)S(1)} %copy-done.5, f32[136,128]{1,0:T(8,128)S(1)} %collective-permute-done.2.refs_1_, f32[136,128]{1,0:T(8,128)S(1)} %collective-permute-done.3.refs_2_, f32[136,128]{1,0:T(8,128)S(1)} %collective-permute-done.4.refs_3_, ...), custom_call_target="tpu_custom_call" | custom-call | flops 167772160 | bytes 491520 | tf_op jit(solution)/shard_map/coarse/pallas_call | solution.py:282
  75.5 0.1 collective-permute-start.11
  75.6 0.5 collective-permute-start.12
  76.1 0.1 collective-permute-start.13
  76.2 0.4 collective-permute-start.14
  76.6 0.1 pad_add_fusion.where_ref
  76.7 1.0 copy-done
  77.7 1.0 targets.1
  78.7 0.0 collective-permute-done.11.refs_1_
  78.8 0.4 collective-permute-done.12.refs_3_
  79.2 0.1 collective-permute-done.13.refs_5_
  79.3 0.8 collective-permute-done.14.refs_7_
  80.1 72.3 %fine.1 = (f32[32,1,1280]{2,1,0:T(1,128)S(1)}, f32[16,128]{1,0:T(8,128)S(1)}, f32[64,128]{1,0:T(8,128)}) custom-call(s32[2]{0:T(128)S(1)} %pad_add_fusion.where_ref, f32[4,280,128]{2,1,0:T(8,128)S(1)} %pad_maximum_fusion.refs_0_, f32[4,280,128]{2,1,0:T(8,128)S(1)} %collective-permute-done.11.refs_1_, f32[4,280,128]{2,1,0:T(8,128)S(1)} %collective-permute-done.8.refs_2_, ...), custom_call_target="tpu_custom_call" | custom-call | tf_op jit(solution)/shard_map/fine/pallas_call | solution.py:515
  152.4 0.7 copy-done.1
  153.1 0.6 copy-done.4
  153.7 6.4 %all-to-all-start = ((f32[32,1,1280]{2,1,0:T(1,128)}), f32[32,1,1280]{2,1,0:T(1,128)S(1)}, u32[]{:S(2)}, u32[]{:S(2)}) async-start(f32[32,1,1280]{2,1,0:T(1,128)} %copy-done.1), calls=%async_computation | async-start | bytes 327680 | tf_op jit(solution)/shard_map/all_to_all | solution.py:624
  160.1 0.6 slice.22
  160.7 0.5 slice_bitcast_fusion.4
  161.2 7.4 %all-to-all-done.partial = f32[32,1,1280]{2,1,0:T(1,128)S(1)} async-done(((f32[32,1,1280]{2,1,0:T(1,128)}), f32[32,1,1280]{2,1,0:T(1,128)S(1)}, u32[]{:S(2)}, u32[]{:S(2)}) %all-to-all-start) | async-done | bytes 163872 | tf_op jit(solution)/shard_map/all_to_all | solution.py:624
  168.6 0.7 copy-done.6
  169.2 2.5 %finish.1 = f32[16,128]{1,0:T(8,128)} custom-call(s32[128]{0:T(128)} %get-tuple-element.52.slot_ref, f32[32,1,1280]{2,1,0:T(1,128)} %copy-done.6, f32[16,128]{1,0:T(8,128)} %copy-done.4), custom_call_target="tpu_custom_call" | custom-call | tf_op jit(solution)/shard_map/finish/pallas_call | solution.py:558
  (20 shorter events, 0.1 us)
Async XLA Ops:
  0.6 2.8 %collective-permute-start.1 = (f32[1,128]{1,0:T(1,128)}, f32[1,128]{1,0:T(1,128)S(1)}, u32[]{:S(2)}, u32[]{:S(2)}) collective-permute-start(f32[1,128]{1,0:T(1,128)} %bitcast.27), channel_id=1, source_target_pairs={{0,1},{1,0},{2,3},{3,2},{4,5},{5,4},{6,7},{7,6},{8,9},{9,8},{10,11... | collective-permute-start | bytes 1544 | tf_op jit(solution)/shard_map/ppermute | solution.py:570
  1.1 2.3 %collective-permute-start = (f32[16,128]{1,0:T(8,128)}, f32[16,128]{1,0:T(8,128)S(1)}, u32[]{:S(2)}, u32[]{:S(2)}) collective-permute-start(f32[16,128]{1,0:T(8,128)} %tgt_a.1), channel_id=1, source_target_pairs={{0,1},{1,0},{2,3},{3,2},{4,5},{5,4},{6,7},{7,6},{8,9},{9,8},{10,11... | collective-permute-start | bytes 24584 | tf_op jit(solution)/shard_map/ppermute | solution.py:570
  3.5 0.5 copy-start.8
  3.5 0.6 copy-start.7
  5.8 23.1 %copy-start.2 = (f32[320,128]{1,0:T(8,128)S(1)}, f32[320,128]{1,0:T(8,128)}, u32[]{:S(2)}) copy-start(f32[320,128]{1,0:T(8,128)} %get-tuple-element.34.refs_4_) | copy-start | bytes 491524
  5.8 23.1 %copy-start.5 = (f32[136,128]{1,0:T(8,128)S(1)}, f32[136,128]{1,0:T(8,128)}, u32[]{:S(2)}) copy-start(f32[136,128]{1,0:T(8,128)} %get-tuple-element.30.refs_0_) | copy-start | bytes 208900
  5.8 10.4 %collective-permute-start.7 = (f32[320,128]{1,0:T(8,128)}, f32[320,128]{1,0:T(8,128)S(1)}, u32[]{:S(2)}, u32[]{:S(2)}) collective-permute-start(f32[320,128]{1,0:T(8,128)} %get-tuple-element.34.refs_4_), channel_id=1, source_target_pairs={{0,6},{1,7},{2,4},{3,5},{4,2},{5,3},{6,0},{7,1},{8,14},{9,15},{10,... | collective-permute-start | bytes 491528 | tf_op jit(solution)/shard_map/ppermute | solution.py:570
  10.9 14.3 %collective-permute-start.6 = (f32[320,128]{1,0:T(8,128)}, f32[320,128]{1,0:T(8,128)S(1)}, u32[]{:S(2)}, u32[]{:S(2)}) collective-permute-start(f32[320,128]{1,0:T(8,128)} %get-tuple-element.34.refs_4_), channel_id=1, source_target_pairs={{0,4},{1,5},{2,6},{3,7},{4,0},{5,1},{6,2},{7,3},{8,12},{9,13},{10,... | collective-permute-start | bytes 491528 | tf_op jit(solution)/shard_map/ppermute | solution.py:570
  10.9 14.4 %collective-permute-start.5 = (f32[320,128]{1,0:T(8,128)}, f32[320,128]{1,0:T(8,128)S(1)}, u32[]{:S(2)}, u32[]{:S(2)}) collective-permute-start(f32[320,128]{1,0:T(8,128)} %get-tuple-element.34.refs_4_), channel_id=1, source_target_pairs={{0,2},{1,3},{2,0},{3,1},{4,6},{5,7},{6,4},{7,5},{8,10},{9,11},{10,... | collective-permute-start | bytes 491528 | tf_op jit(solution)/shard_map/ppermute | solution.py:570
  11.5 13.8 %collective-permute-start.2 = (f32[136,128]{1,0:T(8,128)}, f32[136,128]{1,0:T(8,128)S(1)}, u32[]{:S(2)}, u32[]{:S(2)}) collective-permute-start(f32[136,128]{1,0:T(8,128)} %get-tuple-element.30.refs_0_), channel_id=1, source_target_pairs={{0,8},{8,0},{16,24},{24,16},{1,9},{9,1},{17,25},{25,17},{2,10},{10... | collective-permute-start | bytes 208904 | tf_op jit(solution)/shard_map/ppermute | solution.py:570
  13.2 12.2 %collective-permute-start.3 = (f32[136,128]{1,0:T(8,128)}, f32[136,128]{1,0:T(8,128)S(1)}, u32[]{:S(2)}, u32[]{:S(2)}) collective-permute-start(f32[136,128]{1,0:T(8,128)} %get-tuple-element.30.refs_0_), channel_id=1, source_target_pairs={{0,16},{8,24},{16,0},{24,8},{1,17},{9,25},{17,1},{25,9},{2,18},{10... | collective-permute-start | bytes 208904 | tf_op jit(solution)/shard_map/ppermute | solution.py:570
  16.2 9.2 %collective-permute-start.4 = (f32[136,128]{1,0:T(8,128)}, f32[136,128]{1,0:T(8,128)S(1)}, u32[]{:S(2)}, u32[]{:S(2)}) collective-permute-start(f32[136,128]{1,0:T(8,128)} %get-tuple-element.30.refs_0_), channel_id=1, source_target_pairs={{0,24},{8,16},{16,8},{24,0},{1,25},{9,17},{17,9},{25,1},{2,26},{10... | collective-permute-start | bytes 208904 | tf_op jit(solution)/shard_map/ppermute | solution.py:570
  25.3 51.3 %copy-start.3 = (s32[8192]{0:T(1024)S(1)}, s32[8192]{0:T(1024)}, u32[]{:S(2)}) copy-start(s32[8192]{0:T(1024)} %param.16) | copy-start | bytes 98308
  25.4 50.1 %collective-permute-start.10 = (f32[4,280,128]{2,1,0:T(8,128)S(1)}, f32[4,280,128]{2,1,0:T(8,128)S(1)}, u32[]{:S(2)}, u32[]{:S(2)}) collective-permute-start(f32[4,280,128]{2,1,0:T(8,128)S(1)} %pad_maximum_fusion.refs_0_), channel_id=1, source_target_pairs={{0,24},{8,16},{16,8},{24,0},{1,25},{9,17},{17,9},{25,1},{2,26},{10... | collective-permute-start | bytes 1720328 | tf_op jit(solution)/shard_map/ppermute | solution.py:570
  27.9 47.6 %collective-permute-start.8 = (f32[4,280,128]{2,1,0:T(8,128)S(1)}, f32[4,280,128]{2,1,0:T(8,128)S(1)}, u32[]{:S(2)}, u32[]{:S(2)}) collective-permute-start(f32[4,280,128]{2,1,0:T(8,128)S(1)} %pad_maximum_fusion.refs_0_), channel_id=1, source_target_pairs={{0,8},{8,0},{16,24},{24,16},{1,9},{9,1},{17,25},{25,17},{2,10},{10... | collective-permute-start | bytes 1720328 | tf_op jit(solution)/shard_map/ppermute | solution.py:570
  28.4 47.1 %collective-permute-start.9 = (f32[4,280,128]{2,1,0:T(8,128)S(1)}, f32[4,280,128]{2,1,0:T(8,128)S(1)}, u32[]{:S(2)}, u32[]{:S(2)}) collective-permute-start(f32[4,280,128]{2,1,0:T(8,128)S(1)} %pad_maximum_fusion.refs_0_), channel_id=1, source_target_pairs={{0,16},{8,24},{16,0},{24,8},{1,17},{9,25},{17,1},{25,9},{2,18},{10... | collective-permute-start | bytes 1720328 | tf_op jit(solution)/shard_map/ppermute | solution.py:570
  75.5 3.2 %collective-permute-start.11 = (f32[4,280,128]{2,1,0:T(8,128)S(1)}, f32[4,280,128]{2,1,0:T(8,128)S(1)}, u32[]{:S(2)}, u32[]{:S(2)}) collective-permute-start(f32[4,280,128]{2,1,0:T(8,128)S(1)} %pad_maximum_fusion.refs_0_), channel_id=1, source_target_pairs={{0,1},{1,0},{2,3},{3,2},{4,5},{5,4},{6,7},{7,6},{8,9},{9,8},{10,11... | collective-permute-start | bytes 1720328 | tf_op jit(solution)/shard_map/ppermute | solution.py:570
  75.6 3.6 %collective-permute-start.12 = (f32[4,280,128]{2,1,0:T(8,128)S(1)}, f32[4,280,128]{2,1,0:T(8,128)S(1)}, u32[]{:S(2)}, u32[]{:S(2)}) collective-permute-start(f32[4,280,128]{2,1,0:T(8,128)S(1)} %collective-permute-done.8.refs_2_), channel_id=1, source_target_pairs={{0,1},{1,0},{2,3},{3,2},{4,5},{5,4},{6,7},{7,6},{8,9},{9,8},{10,11... | collective-permute-start | bytes 1720328 | tf_op jit(solution)/shard_map/ppermute | solution.py:570
  76.1 3.2 %collective-permute-start.13 = (f32[4,280,128]{2,1,0:T(8,128)S(1)}, f32[4,280,128]{2,1,0:T(8,128)}, u32[]{:S(2)}, u32[]{:S(2)}) collective-permute-start(f32[4,280,128]{2,1,0:T(8,128)S(1)} %collective-permute-done.9.refs_4_), channel_id=1, source_target_pairs={{0,1},{1,0},{2,3},{3,2},{4,5},{5,4},{6,7},{7,6},{8,9},{9,8},{10,11... | collective-permute-start | bytes 1720328 | tf_op jit(solution)/shard_map/ppermute | solution.py:570
  76.2 4.0 %collective-permute-start.14 = (f32[4,280,128]{2,1,0:T(8,128)S(1)}, f32[4,280,128]{2,1,0:T(8,128)}, u32[]{:S(2)}, u32[]{:S(2)}) collective-permute-start(f32[4,280,128]{2,1,0:T(8,128)S(1)} %collective-permute-done.10.refs_6_), channel_id=1, source_target_pairs={{0,1},{1,0},{2,3},{3,2},{4,5},{5,4},{6,7},{7,6},{8,9},{9,8},{10,11... | collective-permute-start | bytes 1720328 | tf_op jit(solution)/shard_map/ppermute | solution.py:570
  76.7 1.0 copy-start
  152.4 0.7 copy-start.1
  153.1 0.6 copy-start.4
  153.7 14.9 %all-to-all-start = ((f32[32,1,1280]{2,1,0:T(1,128)}), f32[32,1,1280]{2,1,0:T(1,128)S(1)}, u32[]{:S(2)}, u32[]{:S(2)}) async-start(f32[32,1,1280]{2,1,0:T(1,128)} %copy-done.1), calls=%async_computation | async-start | bytes 327680 | tf_op jit(solution)/shard_map/all_to_all | solution.py:624
  168.6 0.7 copy-start.6

commit v6 on v5

v6 whole, which is shorter than its diff:
```python
import functools
import math

import jax
import jax.numpy as jnp
from jax import lax
from jax.experimental import pallas as pl
from jax.experimental.pallas import tpu as pltpu
from jax.sharding import PartitionSpec as P

F = 16
BLK = 256
SUPP = 16
ITERS = 8
SB_DEV = 8
TB_DEV = 32
EPS = 0.1

SCALE = math.log2(math.e) / EPS
KDIM = 7 * F
LANES = 128
ROWS = 256
ROWS_PRODUCT = 1024
ROWS_BEGIN = 1024
ROWS_TURN = 512
PAIRS = 16
BLOCKS = 8
LOW = 2.0**-30
SMALL = 2.0**-80
LARGE = 2.0**100
MIB = 1024 * 1024
SLOT_AT = 2 * LANES + F
TGT_AT = SLOT_AT + 8
AXES = ("row", "chip", "core")
CHIPS = ("row", "chip")

VMEM = pl.BlockSpec(memory_space=pltpu.VMEM)
SMEM = pl.BlockSpec(memory_space=pltpu.SMEM)
CONTRACT_FIRST = (((0,), (0,)), ((), ()))


def split3(x):
    first = x.astype(jnp.bfloat16)
    rest = x - first.astype(jnp.float32)
    second = rest.astype(jnp.bfloat16)
    rest = rest - second.astype(jnp.float32)
    return first, second, rest.astype(jnp.bfloat16)


def constant_rows(values, at, ones_at):
    width = values.shape[1]
    parts = split3(jnp.broadcast_to(values, (F, width)))
    row = lax.broadcasted_iota(jnp.int32, (F, width), 0)
    rows = jnp.zeros((F, width), jnp.float32)
    for k, part in enumerate(parts):
        rows = jnp.where(row == at + k, part.astype(jnp.float32), rows)
    if ones_at is not None:
        rows = jnp.where((row >= ones_at) & (row < ones_at + 3), 1.0, rows)
    return rows.astype(jnp.bfloat16)


def pack_left(x, constant):
    a, b, c = split3(x * (2.0 * SCALE))
    return jnp.concatenate([a, a, b, b, a, c, constant_rows(constant, 0, 3)], 0)


def pack_right(y, constant):
    a, b, c = split3(y)
    return jnp.concatenate([a, b, a, b, c, a, constant_rows(constant, 3, 0)], 0)


def contract(left, right):
    return lax.dot_general(left, right, CONTRACT_FIRST, preferred_element_type=jnp.float32)


def square_norm(x):
    return jnp.sum(x * x, 0, keepdims=True)


def fold(values, combine):
    out = values[0:8]
    for k in range(1, values.shape[0] // 8):
        out = combine(out, values[8 * k : 8 * k + 8])
    return out


def source_columns(ref, count, k, n):
    halves = [
        jnp.concatenate(
            [
                ref[pl.ds(pl.multiple_of(8 * (half * count + k * n + i), 8), 8), :]
                for i in range(n)
            ],
            1,
        )
        for half in range(2)
    ]
    values = [ref[pl.ds(F * count + k * n + i, 1), :] for i in range(n)]
    return jnp.concatenate(halves, 0), jnp.concatenate(values, 1)


def to_tiles(ref, out):
    count = ref.shape[1] // LANES
    for half in range(2):
        for i in range(count):
            at = 8 * (half * count + i)
            out[at : at + 8, :] = ref[8 * half : 8 * half + 8, i * LANES : (i + 1) * LANES]


def prepare_kernel(
    src_pts, cluster, table, src_cent, src_mass, tgt_a, mass_a, tgt_b, mass_b, bundle, src_own
):
    to_tiles(src_cent, src_own)
    src_own[F * src_mass.shape[0] :, :] = src_mass[...]
    to_tiles(src_pts, bundle)
    bundle[2 * LANES : SLOT_AT, :] = cluster[...].astype(jnp.float32)
    bundle[SLOT_AT:TGT_AT, :] = jnp.zeros((TGT_AT - SLOT_AT, LANES), jnp.float32)
    bundle[SLOT_AT : SLOT_AT + table.shape[0], :] = table[...].astype(jnp.float32)
    bundle[TGT_AT : TGT_AT + F, :] = tgt_a[...]
    bundle[TGT_AT + F : TGT_AT + 2 * F, :] = tgt_b[...]
    masses = jnp.concatenate([mass_a[...], mass_b[...], jnp.ones((6, LANES), jnp.float32)], 0)
    bundle[TGT_AT + 2 * F :, :] = masses


def prepare(src_pts, cluster, table, src_cent, src_mass, tgt):
    return pl.pallas_call(
        prepare_kernel,
        out_shape=(
            jax.ShapeDtypeStruct((TGT_AT + 2 * F + 8, LANES), jnp.float32),
            jax.ShapeDtypeStruct(((F + 1) * src_mass.shape[0], LANES), jnp.float32),
        ),
        in_specs=[VMEM] * 9,
        out_specs=(VMEM, VMEM),
        name="prepare",
    )(src_pts, cluster, table, src_cent, src_mass, *tgt)


def coarse_kernel(n_src, n_tgt, stored, *refs):
    given_src = refs[:n_src]
    given_tgt = refs[n_src : n_src + n_tgt]
    f_out, g_out, kernel, mass, dual, sums, all_src, all_tgt, arrived, *ahead = refs[n_src + n_tgt :]
    src = [all_src.at[n] for n in range(n_src)]
    tgt = [all_tgt.at[n] for n in range(n_tgt)]
    copies = [
        pltpu.make_async_copy(given.at[pl.ds(TGT_AT, 2 * F + 8)], held, arrived.at[n])
        for n, (given, held) in enumerate(zip(given_tgt, tgt))
    ]
    copies += [
        pltpu.make_async_copy(given, held, arrived.at[n_tgt + n])
        for n, (given, held) in enumerate(zip(given_src, src))
    ]
    for copy in copies:
        copy.start()
    for copy in copies:
        copy.wait()
    ks, kt = f_out.shape[1], g_out.shape[1]
    wide_src = src[0].shape[0] // (F + 1)
    piece = wide_src * LANES
    tiles = kt // LANES
    y = jnp.concatenate(
        [ref[F * e : F * e + F, :] for ref in tgt for e in range(2)], 1
    )
    at = 2 * F
    b = jnp.concatenate([ref[at + e : at + e + 1, :] for ref in tgt for e in range(2)], 1)
    right = pack_right(y, jnp.log2(b) - SCALE * square_norm(y))
    ones = jnp.ones((F, LANES), jnp.bfloat16)
    zero = jnp.zeros((8, kt), jnp.float32)
    high = jnp.full((8, LANES), jnp.inf, jnp.float32)

    def wide(values):
        return jnp.tile(values, (1, tiles))

    def over_sources(size, body, carry):
        for s in range(n_src):

            def chunk(k, carry, s=s):
                rows = pl.ds(pl.multiple_of(s * piece + k * size, size), size)
                x, values = source_columns(src[s], wide_src, k, size // LANES)
                left = pack_left(x, -SCALE * square_norm(x))
                return body(values, rows, left, carry)

            carry = lax.fori_loop(0, piece // size, chunk, carry)
        return carry

    def over_rows(size, body, carry):
        def chunk(k, carry):
            return body(pl.ds(pl.multiple_of(k * size, size), size), carry)

        return lax.fori_loop(0, ks // size, chunk, carry)

    def weigh(e, weighted, rows, carry):
        total, least = carry
        row_sum = jnp.broadcast_to(jnp.sum(weighted, 1, keepdims=True), (e.shape[0], LANES))
        sums[rows, :] = row_sum
        weight = mass[rows, :] / row_sum
        return total + fold(e * wide(weight), jnp.add), jnp.minimum(least, fold(row_sum, jnp.minimum))

    def close(total, least):
        total = jnp.sum(total, 0, keepdims=True)
        small = jnp.minimum(jnp.min(total), jnp.min(least)) < LOW
        return b / total, small.astype(jnp.int32)

    def spread_mass(values, rows):
        mass[rows, :] = contract(constant_rows(values, 0, None), ones)

    def begin_rows(z, rows, carry):
        top = jnp.max(z, 1, keepdims=True)
        dual[rows, :] = jnp.broadcast_to(-top, (z.shape[0], LANES))
        e = jnp.exp2(z - top)
        if stored:
            kernel[rows, :] = e
        return weigh(e, e, rows, carry)

    def begin(values, rows, left, carry):
        spread_mass(values, rows)
        return begin_rows(contract(left, right), rows, carry)

    if stored:
        def products(s, out):
            rows = slice(s * piece, (s + 1) * piece)
            x, values = source_columns(src[s], wide_src, 0, wide_src)
            out[...] = contract(pack_left(x, -SCALE * square_norm(x)), right)
            spread_mass(values, rows)

        products(0, ahead[0])
        carry = (zero, high)
        for s in range(n_src):
            if s + 1 < n_src:
                products(s + 1, ahead[(s + 1) % 2])
            carry = begin_rows(ahead[s % 2][...], slice(s * piece, (s + 1) * piece), carry)
    else:
        carry = over_sources(ROWS, begin, (zero, high))
    scale, small = close(*carry)
    base = jnp.zeros((1, kt), jnp.float32)

    def rescue(base, scale):
        def rebase(rows, carry):
            dual[rows, :] = dual[rows, :] - jnp.log2(sums[rows, :])
            return carry

        over_rows(ROWS, rebase, 0)

        def tops(_, rows, left, top):
            return jnp.maximum(top, fold(contract(left, right) + wide(dual[rows, :]), jnp.maximum))

        top = jnp.max(over_sources(ROWS, tops, zero - jnp.inf), 0, keepdims=True)

        def step(_, rows, left, total):
            e = jnp.exp2(contract(left, right) + wide(dual[rows, :]) - top)
            return total + fold(e * wide(mass[rows, :]), jnp.add)

        total = jnp.sum(over_sources(ROWS, step, zero), 0, keepdims=True)
        over_rows(ROWS, unit, 0)
        return jnp.log2(b) - (top + jnp.log2(total)), jnp.ones_like(scale)

    def unit(rows, carry):
        sums[rows, :] = jnp.ones((ROWS, LANES), jnp.float32)
        return carry

    base, scale = lax.cond(small > 0, rescue, lambda base, scale: (base, scale), base, scale)

    def renew(base, scale):
        base = base + jnp.log2(scale)

        def step(_, rows, left, carry):
            f = dual[rows, :] - jnp.log2(sums[rows, :])
            dual[rows, :] = f
            e = jnp.exp2(contract(left, right) + wide(f) + base)
            if stored:
                kernel[rows, :] = e
            return weigh(e, e, rows, carry)

        scale, small = close(*over_sources(ROWS, step, (zero, high)))
        return base, scale, small

    def reuse(base, scale):
        def step(rows, carry):
            e = kernel[rows, :]
            return weigh(e, e * scale, rows, carry)

        scale, small = close(*over_rows(ROWS_TURN, step, (zero, high)))
        return base, scale, small

    def turn(_, state):
        base, scale, small = state
        if not stored:
            return renew(base, scale)
        return lax.cond(small > 0, renew, reuse, base, scale)

    base, scale, small = lax.fori_loop(1, ITERS, turn, (base, scale, small))
    g_out[...] = (base + jnp.log2(scale)) * (1.0 / SCALE)
    diagonal = lax.broadcasted_iota(jnp.int32, (LANES, LANES), 0) == lax.broadcasted_iota(
        jnp.int32, (LANES, LANES), 1
    )

    def to_lanes(k, carry):
        span = pl.ds(pl.multiple_of(k * LANES, LANES), LANES)
        f = dual[span, :] - jnp.log2(sums[span, :])
        f_out[:, span] = jnp.sum(jnp.where(diagonal, f, 0.0), 0, keepdims=True) * (1.0 / SCALE)
        return carry

    lax.fori_loop(0, ks // LANES, to_lanes, 0)

def coarse_duals(src, tgt):
    ks = sum(part.shape[0] // (F + 1) * LANES for part in src)
    kt = sum(2 * part.shape[1] for part in tgt)
    stored = ks * kt * 4 <= 16 * MIB
    return pl.pallas_call(
        functools.partial(coarse_kernel, len(src), len(tgt), stored),
        out_shape=(
            jax.ShapeDtypeStruct((1, ks), jnp.float32),
            jax.ShapeDtypeStruct((1, kt), jnp.float32),
        ),
        in_specs=[VMEM] * (len(src) + len(tgt)),
        out_specs=(VMEM, VMEM),
        scratch_shapes=[
            pltpu.VMEM((ks, kt) if stored else (8, LANES), jnp.float32),
        ]
        + [pltpu.VMEM((ks, LANES), jnp.float32)] * 3
        + [
            pltpu.VMEM((len(src),) + src[0].shape, jnp.float32),
            pltpu.VMEM((len(tgt), 2 * F + 8, LANES), jnp.float32),
            pltpu.SemaphoreType.DMA((len(src) + len(tgt),)),
        ]
        + [pltpu.VMEM((ks // len(src), kt) if stored else (8, LANES), jnp.float32)] * 2,
        compiler_params=pltpu.CompilerParams(vmem_limit_bytes=36 * MIB),
        cost_estimate=pl.CostEstimate(
            flops=40 * ks * kt, bytes_accessed=4 * 24 * (ks + kt), transcendentals=9 * ks * kt
        ),
        name="coarse",
    )(*src, *tgt)


def look_up(table_ref, index):
    low = index & (LANES - 1)
    high = index >> 7
    out = jnp.zeros(index.shape, jnp.float32)
    for h in range(table_ref.shape[1] // LANES):
        row = jnp.broadcast_to(table_ref[0:1, h * LANES : (h + 1) * LANES], index.shape)
        out = jnp.where(high == h, jnp.take_along_axis(row, low, axis=1), out)
    return out


def fine_kernel(n_stacks, slots_each, stride, where_ref, *refs):
    stacks = refs[:n_stacks]
    points_a, points_b, cluster_a, cluster_b, f_table, g_table = refs[n_stacks : n_stacks + 6]
    partial_out, kept = refs[n_stacks + 6 : n_stacks + 8]
    bundle, slot_rows, start_g, packed, col_sum, col_top, codes, arrived, slots, count = refs[
        n_stacks + 8 : n_stacks + 18
    ]
    order_t, order_block, order_from, order_span = refs[n_stacks + 18 :]
    senders = bundle.shape[0]
    depth = senders // n_stacks
    blocks = 2 * TB_DEV
    sums_out = kept
    start_g_at = 3 * blocks
    start_f_at = start_g_at + 2 * TB_DEV
    me, core, src_flip, tgt_flip = (where_ref[k] for k in range(4))

    def copy_of(n, first, rows, to, sem):
        source = stacks[n].at[:, pl.ds(first, rows), :]
        return pltpu.make_async_copy(source, to.at[pl.ds(n * depth, depth)], arrived.at[sem])

    early = [copy_of(n, SLOT_AT, 8, slot_rows, n) for n in range(n_stacks)]
    late = [copy_of(n, 0, SLOT_AT, bundle, n_stacks + n) for n in range(n_stacks)]
    for copy in early + late:
        copy.start()

    for side, cluster in enumerate((cluster_a, cluster_b)):
        for k in range(2 * TB_DEV // 8):
            index = cluster[8 * k : 8 * k + 8, :] ^ tgt_flip
            at = 2 * TB_DEV * side + 8 * k
            start_g[at : at + 8, :] = look_up(g_table, index)
    kept[start_g_at:start_f_at, :] = start_g[0 : 2 * TB_DEV, :]
    for t in range(blocks + 1):
        count[t] = 0
    for copy in early:
        copy.wait()

    at = me * 2 * stride

    def slot_row(n, carry):
        codes[pl.ds(n, 1), :] = slot_rows[n, pl.ds(at // LANES, 1), :].astype(jnp.int32)
        return carry

    lax.fori_loop(0, senders, slot_row, 0, unroll=BLOCKS)
    codes[...] = pltpu.roll(codes[...], (LANES - at % LANES) % LANES, 1)
    to_scalars = pltpu.make_async_copy(codes, slots, arrived.at[2 * n_stacks])
    to_scalars.start()

    for side, points in enumerate((points_a, points_b)):

        def pack_target(t, carry, side=side, points=points):
            y = points[:, pl.ds(pl.multiple_of(t * BLK, BLK), BLK)]
            row = 2 * (side * TB_DEV + t)
            g = jnp.concatenate([start_g[pl.ds(row, 1), :], start_g[pl.ds(row + 1, 1), :]], 1)
            rows = pack_right(y, SCALE * (g - square_norm(y)))
            rows = jnp.concatenate([rows, jnp.zeros((LANES - KDIM, BLK), jnp.bfloat16)], 0)
            packed[side * TB_DEV + t] = jnp.transpose(rows.astype(jnp.float32)).astype(jnp.bfloat16)
            col_sum[side * TB_DEV + t] = jnp.zeros((BLK, LANES), jnp.float32)
            return carry

        lax.fori_loop(0, TB_DEV, pack_target, 0, unroll=BLOCKS)
    packed[blocks] = jnp.zeros((BLK, LANES), jnp.bfloat16)
    col_sum[blocks] = jnp.zeros((BLK, LANES), jnp.float32)
    to_scalars.wait()

    each = 2 * slots_each
    total = senders * each
    unroll = math.gcd(PAIRS, total)

    def place(d, carry):
        used, unused = carry
        for rest in range(each):
            owner, s = divmod(rest, slots_each)
            code = slots[d, owner * stride + s]
            valid = code > 0
            t = jnp.where(valid, (code - 1) % TB_DEV + TB_DEV * (owner ^ core), blocks)
            n = jnp.where(valid, used, unused)
            order_t[n] = t
            order_block[n] = jnp.where(valid, (code - 1) // TB_DEV, 0)
            order_from[n] = d
            order_span[n] = rest * BLK
            count[t] = count[t] + 1
            step = valid.astype(jnp.int32)
            used, unused = used + step, unused - (1 - step)
        return used, unused

    used, _ = lax.fori_loop(0, senders, place, (jnp.int32(0), jnp.int32(total - 1)))
    for copy in late:
        copy.wait()
    index = bundle[0, 2 * LANES : SLOT_AT, :].astype(jnp.int32) ^ src_flip
    for half in range(2):
        rows = slice(8 * half, 8 * half + 8)
        at = start_f_at + 8 * half
        kept[at : at + 8, :] = look_up(f_table, index[rows])

    def cluster_rows(n):
        at = 2 * LANES + 2 * order_block[n]
        return [bundle[order_from[n], pl.ds(at + k, 1), :] for k in range(2)]

    def starts(ps):
        out = []
        for n in range(0, len(ps), 4):
            rows = jnp.concatenate([r for p in ps[n:n+4] for r in cluster_rows(p)], 0)
            f = look_up(f_table, rows.astype(jnp.int32) ^ src_flip)
            for m in range(len(ps[n:n+4])):
                out.append(jnp.concatenate([f[2*m:2*m+1], f[2*m+1:2*m+2]], 1))
        return out

    def product(p, f):
        t, block, d = order_t[p], order_block[p], order_from[p]
        tile = [[bundle[d, pl.ds(pl.multiple_of(half * LANES + 16 * block + 8 * k, 8), 8), :] for k in range(2)] for half in range(2)]
        x = jnp.concatenate([jnp.concatenate(row, 1) for row in tile], 0)
        left = pack_left(x, SCALE * (f - square_norm(x)))
        left = jnp.concatenate([left, jnp.zeros((LANES - KDIM, BLK), jnp.bfloat16)], 0)
        z = jnp.dot(packed[t], left, preferred_element_type=jnp.float32)
        return t, d, SCALE * f, z

    def put(p, d, value):
        span = pl.ds(pl.multiple_of(order_span[p], BLK), BLK)
        partial_out[me ^ d, :, span] = value

    def pair(p, f, least, most):
        t, d, f, z = product(p, f)
        e = jnp.exp2(z)
        row = fold(e, jnp.add)
        col_sum[t] = col_sum[t] + (e[:, :LANES] + e[:, LANES:])
        row = jnp.sum(row, 0, keepdims=True)
        put(p, d, jnp.log2(row) - f)
        return jnp.minimum(least, row), jnp.maximum(most, row)

    def pairs(n, carry):
        ps = [unroll * n + u for u in range(unroll)]
        fs = starts(ps)
        for u in range(unroll):
            carry = pair(ps[u], fs[u], *carry)
        return carry

    def lanes(t, carry):
        least, most = carry
        halves = []
        for k in range(2):
            block = jnp.transpose(col_sum[t, k * LANES : (k + 1) * LANES, :])
            halves.append(jnp.sum(block, 0, keepdims=True))
        s = jnp.concatenate(halves, 0)
        sums_out[pl.ds(pl.multiple_of(2 * t, 2), 2), :] = jnp.log2(s)
        sums_out[pl.ds(2 * blocks + t, 1), :] = jnp.full((1, LANES), count[t].astype(jnp.float32))
        return jnp.minimum(least, jnp.where(count[t] > 0, s, LARGE)), jnp.maximum(most, s)

    least = jnp.full((1, BLK), LARGE, jnp.float32)
    most = jnp.zeros((1, BLK), jnp.float32)
    least, most = lax.fori_loop(0, (used + unroll - 1) // unroll, pairs, (least, most))
    low = jnp.full((2, LANES), LARGE, jnp.float32)
    high = jnp.zeros((2, LANES), jnp.float32)
    low, high = lax.fori_loop(0, blocks, lanes, (low, high), unroll=BLOCKS)
    smallest = jnp.minimum(jnp.min(least), jnp.min(low))
    largest = jnp.maximum(jnp.max(most), jnp.max(high))
    fits = (smallest >= SMALL) & (largest <= LARGE)

    @pl.when(jnp.logical_not(fits))
    def _():
        def fill(t, carry):
            col_sum[t] = jnp.zeros((BLK, LANES), jnp.float32)
            col_top[t] = jnp.full((BLK, LANES), -1e30, jnp.float32)
            return carry

        lax.fori_loop(0, blocks + 1, fill, 0)

        def pair(n, carry):
            p = n
            t, d, f, z = product(p, starts([p])[0])
            top = jnp.max(z, 0, keepdims=True)
            put(p, d, top + jnp.log2(jnp.sum(jnp.exp2(z - top), 0, keepdims=True)) - f)
            a, b = z[:, :LANES], z[:, LANES:]
            old = col_top[t]
            new = jnp.maximum(old, jnp.maximum(a, b))
            col_sum[t] = col_sum[t] * jnp.exp2(old - new) + (jnp.exp2(a - new) + jnp.exp2(b - new))
            col_top[t] = new
            return carry

        lax.fori_loop(0, used, pair, 0)

        def lanes(t, carry):
            for k in range(2):
                rows = slice(k * LANES, (k + 1) * LANES)
                top = jnp.transpose(col_top[t, rows, :])
                most = jnp.max(top, 0, keepdims=True)
                s = jnp.sum(jnp.transpose(col_sum[t, rows, :]) * jnp.exp2(top - most), 0, keepdims=True)
                sums_out[pl.ds(2 * t + k, 1), :] = most + jnp.log2(s)
            return carry

        lax.fori_loop(0, blocks, lanes, 0)


def fine_update(where, stacks, points, clusters, f_table, g_table, slots_each, stride):
    senders = sum(stack.shape[0] for stack in stacks)
    blocks = 2 * TB_DEV
    return pl.pallas_call(
        functools.partial(fine_kernel, len(stacks), slots_each, stride),
        out_shape=(
            jax.ShapeDtypeStruct((senders, 1, 2 * slots_each * BLK), jnp.float32),
            jax.ShapeDtypeStruct((3 * blocks + 2 * TB_DEV + F, LANES), jnp.float32),
        ),
        in_specs=[SMEM] + [pl.BlockSpec(memory_space=pl.ANY)] * len(stacks) + [VMEM] * 6,
        out_specs=(VMEM, VMEM),
        scratch_shapes=[
            pltpu.VMEM((senders, SLOT_AT, LANES), jnp.float32),
            pltpu.VMEM((senders, 8, LANES), jnp.float32),
            pltpu.VMEM((2 * blocks, LANES), jnp.float32),
            pltpu.VMEM((blocks + 1, BLK, LANES), jnp.bfloat16),
            pltpu.VMEM((blocks + 1, BLK, LANES), jnp.float32),
            pltpu.VMEM((blocks + 1, BLK, LANES), jnp.float32),
            pltpu.VMEM((senders, LANES), jnp.int32),
            pltpu.SemaphoreType.DMA((2 * len(stacks) + 1,)),
            pltpu.SMEM((senders, LANES), jnp.int32),
            pltpu.SMEM((blocks + 1,), jnp.int32),
        ]
        + [pltpu.SMEM((senders * 2 * slots_each,), jnp.int32)] * 4,
        compiler_params=pltpu.CompilerParams(vmem_limit_bytes=(28 + senders // 8) * MIB),
        name="fine",
    )(where, *stacks, *points, *clusters, f_table, g_table)


def finish_kernel(
    from_ref, span_ref, own, other, partial, fine_f_out, fine_g_out, gathered
):
    rows = 2 * TB_DEV
    a, b = own[0:rows, :], other[rows : 2 * rows, :]
    top = jnp.maximum(a, b)
    lse = top + jnp.log2(jnp.exp2(a - top) + jnp.exp2(b - top))
    counts = 2 * rows
    g = own[3 * rows : 4 * rows, :]
    named = own[counts : counts + TB_DEV, :] + other[counts + TB_DEV : counts + 2 * TB_DEV, :]
    logs = EPS * jnp.log(named * float(BLK))
    base = g - (lse * (1.0 / SCALE) - g)
    for t in range(TB_DEV):
        span = slice(2 * t, 2 * t + 2)
        fine_g_out[span, :] = 0.5 * (base[span, :] + logs[t : t + 1, :])
    for block in range(SB_DEV):
        for k in range(SUPP):
            n = block * SUPP + k
            span = pl.ds(pl.multiple_of(span_ref[n], BLK), BLK)
            gathered[k, block : block + 1, :] = partial[from_ref[n], :, span]
    values = gathered[...]
    top = jnp.max(values, 0)
    lse = top + jnp.log2(jnp.sum(jnp.exp2(values - top[None]), 0))
    term = EPS * math.log(float(SUPP * BLK)) - lse * (1.0 / SCALE)
    for block in range(SB_DEV):
        for k in range(2):
            row = slice(2 * block + k, 2 * block + k + 1)
            piece = term[block : block + 1, k * LANES : (k + 1) * LANES]
            start_f = own[4 * rows + 2 * block + k : 4 * rows + 2 * block + k + 1, :]
            fine_f_out[row, :] = 0.5 * (start_f + piece)


def finish(chips, spans, own, other, partial):
    return pl.pallas_call(
        finish_kernel,
        out_shape=(
            jax.ShapeDtypeStruct((F, LANES), jnp.float32),
            jax.ShapeDtypeStruct((2 * TB_DEV, LANES), jnp.float32),
        ),
        in_specs=[SMEM, SMEM] + [VMEM] * 3,
        out_specs=(VMEM, VMEM),
        scratch_shapes=[pltpu.VMEM((SUPP, SB_DEV, BLK), jnp.float32)],
        name="finish",
    )(chips, spans, own, other, partial)


def exchange(x, axis, flip):
    count = lax.axis_size(axis)
    return lax.ppermute(x, axis, [(i, i ^ flip) for i in range(count)])


def on_device(
    src_cent, tgt_cent, src_mass, tgt_mass, src_pts, tgt_pts, src_cluster, tgt_cluster, support
):
    n_row, n_chip, n_core = (lax.axis_size(axis) for axis in AXES)
    devices = n_row * n_chip * n_core
    row, chip, core = (lax.axis_index(axis) for axis in AXES)

    flat_mass = tgt_mass.reshape(-1, LANES)
    tgt = [tgt_cent, flat_mass, exchange(tgt_cent, "core", 1), exchange(flat_mass, "core", 1)]

    tgt_cluster = tgt_cluster.reshape(2 * TB_DEV, LANES)
    requests_each = SB_DEV * SUPP
    slots_each = requests_each // devices + 1
    stride = 1 << (slots_each - 1).bit_length()
    wanted = support.reshape(-1)
    owners = wanted // TB_DEV
    positions = jnp.arange(requests_each, dtype=jnp.int32)
    earlier = (owners[None, :] == owners[:, None]) & (positions[None, :] < positions[:, None])
    occurs = jnp.sum(earlier.astype(jnp.int32), 1)
    codes = (positions // SUPP) * TB_DEV + wanted % TB_DEV + 1
    places = jnp.arange(devices * stride, dtype=jnp.int32)
    filled = owners * stride + occurs
    table = jnp.sum(jnp.where(filled[None, :] == places[:, None], codes[None, :], 0), 1)
    chips = owners // n_core
    spans = (owners % n_core * slots_each + occurs) * BLK
    bundle, src_own = prepare(
        src_pts,
        src_cluster.reshape(F, LANES),
        table.reshape(-1, LANES),
        src_cent,
        src_mass.reshape(-1, LANES),
        tgt,
    )
    along = [bundle] + [exchange(bundle, "chip", k) for k in range(1, n_chip)]
    src_all = [src_own] + [exchange(src_own, "row", k) for k in range(1, 3)]
    src_own, src_all[1] = lax.optimization_barrier((src_own, src_all[1]))
    src_all += [exchange(src_own, "row", k) for k in range(3, n_row)]
    stack = jnp.stack([part[:TGT_AT] for part in along])
    src_all, along, stack = lax.optimization_barrier((src_all, along, stack))
    stacks = [stack] + [exchange(stack, "row", k) for k in range(1, n_row)]
    f_table, g_table = coarse_duals(src_all, along)
    tgt_pts, tgt_cluster, f_table, g_table = lax.optimization_barrier(
        (tgt_pts, tgt_cluster, f_table, g_table)
    )
    points = [tgt_pts, exchange(tgt_pts, "core", 1)]
    clusters = [tgt_cluster, exchange(tgt_cluster, "core", 1)]
    coarse_f = f_table[0, : src_cent.shape[1]]
    coarse_g = g_table[0, : tgt_cent.shape[1]]

    col = chip * n_core + core
    where = [row * n_chip + chip, core, row * src_cent.shape[1], col * tgt_cent.shape[1]]
    partial, kept = fine_update(
        jnp.stack(where).astype(jnp.int32),
        stacks,
        points,
        clusters,
        f_table,
        g_table,
        slots_each,
        stride,
    )
    returned = lax.all_to_all(partial, CHIPS, split_axis=0, concat_axis=0, tiled=True)
    other = exchange(kept, "core", 1)
    fine_f, fine_g = finish(chips, spans, kept, other, returned)
    return coarse_f, coarse_g, fine_f.reshape(-1), fine_g.reshape(-1)


def solution(mesh):
    n_row, n_col = mesh.devices.shape
    cores = jax.sharding.Mesh(mesh.devices.reshape(n_row, n_col // 2, 2), AXES)
    col = CHIPS[1:] + AXES[2:]
    in_specs = (
        P(None, "row"),
        P(None, col),
        P("row"),
        P(col),
        P(None, AXES),
        P(None, AXES),
        P(AXES),
        P(AXES),
        P(AXES, None),
    )
    out_specs = (P("row"), P(col), P(AXES), P(AXES))
    return jax.shard_map(
        on_device, mesh=cores, in_specs=in_specs, out_specs=out_specs, check_vma=False
    )
```

time: 175 us -> 173 us (0.989); the launches traced: 172 us -> 173 us
  starting transfers between devices: 23.2 us -> 17.2 us
  waiting for transfers between devices: 15.7 us -> 20.4 us
  Pallas kernels: 124 us -> 127 us
    ppermute x15 -> x14, waiting for transfers between devices: 8.34 us -> 13.7 us  [exchange(): return lax.ppermute(x, axis, [(i, i ^ flip) for i in range(count)])]
    pallas_call x1, Pallas kernels: 72.3 us -> 77.3 us  [fine_update(): pl.pallas_call(functools.partial(fine_kernel, len(stacks), slots_each, st...]
    ppermute x15 -> x14, starting transfers between devices: 16.8 us -> 13.3 us  [exchange(): return lax.ppermute(x, axis, [(i, i ^ flip) for i in range(count)])]
    all_to_all x1, starting transfers between devices: 6.42 us -> 3.86 us  [on_device(): lax.all_to_all(partial, CHIPS, split_axis=0, concat_axis=0, tiled=True)]
    pallas_call x2 -> x1, Pallas kernels: 3.51 us -> 1.93 us  [finish(): pl.pallas_call(finish_kernel, out_shape=(jax.ShapeDtypeStruct((F, LANES),...]
    unnamed x18 -> x20, local copies, waits for them, and re-layouts: 3.58 us -> 2.59 us
  transfers between devices with their start and end apart: 16 -> 15, of which waited for: 6 -> 5; matrix products, arithmetic and copies ran while one was open for 3% -> 3% of each run, Pallas kernels for 28% -> 27%
where the time goes in v6:
time: 173 us
  Pallas kernels  127 us (73%)
  waiting for transfers between devices  20.4 us (12%)
  starting transfers between devices  17.2 us (10%)
  local copies, waits for them, and re-layouts  5.44 us (3%)
  other arithmetic  2.15 us (1%)
    pallas_call x1, Pallas kernels, fine_update(): pl.pallas_call(functools.partial(fine_kernel, len(stacks), slots_each, st...  77.3 us
    pallas_call x1, Pallas kernels, coarse_duals(): pl.pallas_call(functools.partial(coarse_kernel, len(src), len(tgt), store...  45.7 us
    ppermute x14, waiting for transfers between devices, exchange(): return lax.ppermute(x, axis, [(i, i ^ flip) for i in range(count)])  13.7 us
    ppermute x14, starting transfers between devices, exchange(): return lax.ppermute(x, axis, [(i, i ^ flip) for i in range(count)])  13.3 us
    all_to_all x1, waiting for transfers between devices, on_device(): lax.all_to_all(partial, CHIPS, split_axis=0, concat_axis=0, tiled=True)  6.71 us
    all_to_all x1, starting transfers between devices, on_device(): lax.all_to_all(partial, CHIPS, split_axis=0, concat_axis=0, tiled=True)  3.86 us
  transfers between devices with their start and end apart: 15, of which 5 were waited for; matrix products, arithmetic and copies ran while one was open for 3% of the time, Pallas kernels for 27%

profile of v6, /device:TPU:0, one launch (start us, length us, event | category | flops | bytes accessed | tf_op | source)
XLA Modules:
  0.0 172.6 jit_solution(11594183562496882508)
XLA Ops:
  0.6 0.0 copy-start.8
  0.6 0.6 copy-done.8
  1.3 0.5 collective-permute-start.1
  1.7 0.1 collective-permute-start
  1.8 0.8 reshape.140
  2.6 0.6 and_select_fusion.1
  3.2 0.2 convert_reduce_fusion
  3.3 0.6 fusion.6
  3.9 0.7 select_reduce_fusion
  4.6 0.0 collective-permute-done.1.mass_b
  4.6 0.0 collective-permute-done.tgt_b
  4.6 0.5 copy-done.9
  5.1 0.1 copy-done.7
  5.2 1.7 prepare.1
  6.9 3.0 %collective-permute-start.3 = (f32[136,128]{1,0:T(8,128)}, f32[136,128]{1,0:T(8,128)S(1)}, u32[]{:S(2)}, u32[]{:S(2)}) collective-permute-start(f32[136,128]{1,0:T(8,128)} %get-tuple-element.31.refs_0_), channel_id=1, source_target_pairs={{0,16},{8,24},{16,0},{24,8},{1,17},{9,25},{17,1},{25,9},{2,18},{10... | collective-permute-start | bytes 208904 | tf_op jit(solution)/shard_map/ppermute | solution.py:613
  9.9 1.5 collective-permute-start.2
  11.3 3.6 %collective-permute-start.7 = (f32[320,128]{1,0:T(8,128)}, f32[320,128]{1,0:T(8,128)S(1)}, u32[]{:S(2)}, u32[]{:S(2)}) collective-permute-start(f32[320,128]{1,0:T(8,128)} %get-tuple-element.35.refs_4_), channel_id=1, source_target_pairs={{0,6},{2,4},{4,2},{6,0},{1,7},{3,5},{5,3},{7,1},{8,14},{10,12},{12... | collective-permute-start | bytes 491528 | tf_op jit(solution)/shard_map/ppermute | solution.py:613
  14.9 1.0 slice_bitcast_fusion.3
  15.9 0.1 collective-permute-start.6
  16.0 0.8 collective-permute-start.5
  16.8 0.0 collective-permute-done.2.refs_1_
  16.8 0.3 collective-permute-start.4
  17.0 3.5 %collective-permute-done.7.refs_7_ = f32[320,128]{1,0:T(8,128)S(1)} collective-permute-done((f32[320,128]{1,0:T(8,128)}, f32[320,128]{1,0:T(8,128)S(1)}, u32[]{:S(2)}, u32[]{:S(2)}) %collective-permute-start.7) | collective-permute-done | bytes 163872 | tf_op jit(solution)/shard_map/ppermute | solution.py:613
  20.5 8.1 %collective-permute-done.6.refs_6_ = f32[320,128]{1,0:T(8,128)S(1)} collective-permute-done((f32[320,128]{1,0:T(8,128)S(1)}, f32[320,128]{1,0:T(8,128)S(1)}, u32[]{:S(2)}, u32[]{:S(2)}) %collective-permute-start.6) | collective-permute-done | bytes 163872 | tf_op jit(solution)/shard_map/ppermute | solution.py:613
  28.7 0.1 pad_maximum_fusion.refs_0_
  28.8 0.0 collective-permute-done.3.refs_2_
  28.8 0.5 collective-permute-start.10
  29.3 1.5 collective-permute-start.9
  30.9 1.5 collective-permute-start.8
  32.3 45.7 %coarse.1 = (f32[1,4096]{1,0:T(1,128)S(1)}, f32[1,1024]{1,0:T(1,128)S(1)}) custom-call(f32[136,128]{1,0:T(8,128)S(1)} %copy-done.4, f32[136,128]{1,0:T(8,128)S(1)} %collective-permute-done.2.refs_1_, f32[136,128]{1,0:T(8,128)S(1)} %collective-permute-done.3.refs_2_, f32[136,128]{1,0:T(8,128)S(1)} %collective-permute-done.4.refs_3_, ...), custom_call_target="tpu_custom_call" | custom-call | flops 167772160 | bytes 491520 | tf_op jit(solution)/shard_map/coarse/pallas_call | solution.py:308
  78.1 0.0 copy-start.3
  78.1 0.1 collective-permute-start.11
  78.2 0.7 copy-done.3
  78.9 0.0 collective-permute-start.12
  78.9 0.1 pad_add_fusion.where_ref
  78.9 1.2 collective-permute-done.12.refs_7_
  80.2 0.0 collective-permute-done.10.refs_3_
  80.2 0.0 collective-permute-done.9.refs_2_
  80.2 0.0 collective-permute-done.8.refs_1_
  80.2 77.3 %fine.1 = (f32[16,1,2560]{2,1,0:T(1,128)}, f32[272,128]{1,0:T(8,128)S(1)}) custom-call(s32[4]{0:T(128)S(1)} %pad_add_fusion.where_ref, f32[4,280,128]{2,1,0:T(8,128)S(1)} %pad_maximum_fusion.refs_0_, f32[4,280,128]{2,1,0:T(8,128)S(1)} %collective-permute-done.8.refs_1_, f32[4,280,128]{2,1,0:T(8,128)S(1)} %collective-permute-done.9.refs_2_, ...), custom_call_target="tpu_custom_call" | custom-call | tf_op jit(solution)/shard_map/fine/pallas_call | solution.py:539
  157.5 3.9 %all-to-all-start = ((f32[16,1,2560]{2,1,0:T(1,128)}), f32[16,1,2560]{2,1,0:T(1,128)S(1)}, u32[]{:S(2)}, u32[]{:S(2)}) async-start(f32[16,1,2560]{2,1,0:T(1,128)} %get-tuple-element.47), calls=%async_computation | async-start | bytes 327680 | tf_op jit(solution)/shard_map/all_to_all | solution.py:677
  161.3 0.6 slice.22
  161.9 0.0 collective-permute-start.13
  161.9 0.5 slice_bitcast_fusion.4
  162.5 0.8 collective-permute-done.13.other
  163.3 6.7 %all-to-all-done.partial = f32[16,1,2560]{2,1,0:T(1,128)S(1)} async-done(((f32[16,1,2560]{2,1,0:T(1,128)}), f32[16,1,2560]{2,1,0:T(1,128)S(1)}, u32[]{:S(2)}, u32[]{:S(2)}) %all-to-all-start) | async-done | bytes 163872 | tf_op jit(solution)/shard_map/all_to_all | solution.py:677
  170.0 0.7 copy-done.5
  170.7 1.9 %finish.1 = (f32[16,128]{1,0:T(8,128)}, f32[64,128]{1,0:T(8,128)}) custom-call(s32[128]{0:T(128)} %get-tuple-element.50.from_ref, s32[128]{0:T(128)} %get-tuple-element.52.span_ref, f32[272,128]{1,0:T(8,128)} %copy-done.1, f32[272,128]{1,0:T(8,128)} %copy-done.6, f32[16,1,2560]{2,1,0:T(1,128)} %copy-done.5), custom_call_target="tpu_custom_call" | custom-call | tf_op jit(solution)/shard_map/finish/pallas_call | solution.py:598
  (19 shorter events, 0.1 us)
Async XLA Ops:
  0.6 0.7 copy-start.8
  1.3 3.3 %collective-permute-start.1 = (f32[1,128]{1,0:T(1,128)S(1)}, f32[1,128]{1,0:T(1,128)S(1)}, u32[]{:S(2)}, u32[]{:S(2)}) collective-permute-start(f32[1,128]{1,0:T(1,128)S(1)} %bitcast.29), channel_id=1, source_target_pairs={{0,1},{1,0},{2,3},{3,2},{4,5},{5,4},{6,7},{7,6},{8,9},{9,8},{10,11... | collective-permute-start | bytes 1544 | tf_op jit(solution)/shard_map/ppermute | solution.py:613
  1.7 2.8 %collective-permute-start = (f32[16,128]{1,0:T(8,128)}, f32[16,128]{1,0:T(8,128)S(1)}, u32[]{:S(2)}, u32[]{:S(2)}) collective-permute-start(f32[16,128]{1,0:T(8,128)} %tgt_a.1), channel_id=1, source_target_pairs={{0,1},{1,0},{2,3},{3,2},{4,5},{5,4},{6,7},{7,6},{8,9},{9,8},{10,11... | collective-permute-start | bytes 24584 | tf_op jit(solution)/shard_map/ppermute | solution.py:613
  4.6 0.5 copy-start.9
  4.6 0.6 copy-start.7
  6.9 9.0 %copy-start.2 = (f32[320,128]{1,0:T(8,128)S(1)}, f32[320,128]{1,0:T(8,128)}, u32[]{:S(2)}) copy-start(f32[320,128]{1,0:T(8,128)} %get-tuple-element.35.refs_4_) | copy-start | bytes 491524
  6.9 21.9 %collective-permute-start.3 = (f32[136,128]{1,0:T(8,128)}, f32[136,128]{1,0:T(8,128)S(1)}, u32[]{:S(2)}, u32[]{:S(2)}) collective-permute-start(f32[136,128]{1,0:T(8,128)} %get-tuple-element.31.refs_0_), channel_id=1, source_target_pairs={{0,16},{8,24},{16,0},{24,8},{1,17},{9,25},{17,1},{25,9},{2,18},{10... | collective-permute-start | bytes 208904 | tf_op jit(solution)/shard_map/ppermute | solution.py:613
  9.9 6.9 %collective-permute-start.2 = (f32[136,128]{1,0:T(8,128)}, f32[136,128]{1,0:T(8,128)S(1)}, u32[]{:S(2)}, u32[]{:S(2)}) collective-permute-start(f32[136,128]{1,0:T(8,128)} %get-tuple-element.31.refs_0_), channel_id=1, source_target_pairs={{0,8},{8,0},{16,24},{24,16},{1,9},{9,1},{17,25},{25,17},{2,10},{10... | collective-permute-start | bytes 208904 | tf_op jit(solution)/shard_map/ppermute | solution.py:613
  11.3 5.4 %copy-start.4 = (f32[136,128]{1,0:T(8,128)S(1)}, f32[136,128]{1,0:T(8,128)}, u32[]{:S(2)}) copy-start(f32[136,128]{1,0:T(8,128)} %get-tuple-element.31.refs_0_) | copy-start | bytes 208900
  11.3 9.2 %collective-permute-start.7 = (f32[320,128]{1,0:T(8,128)}, f32[320,128]{1,0:T(8,128)S(1)}, u32[]{:S(2)}, u32[]{:S(2)}) collective-permute-start(f32[320,128]{1,0:T(8,128)} %get-tuple-element.35.refs_4_), channel_id=1, source_target_pairs={{0,6},{2,4},{4,2},{6,0},{1,7},{3,5},{5,3},{7,1},{8,14},{10,12},{12... | collective-permute-start | bytes 491528 | tf_op jit(solution)/shard_map/ppermute | solution.py:613
  15.9 12.7 %collective-permute-start.6 = (f32[320,128]{1,0:T(8,128)S(1)}, f32[320,128]{1,0:T(8,128)S(1)}, u32[]{:S(2)}, u32[]{:S(2)}) collective-permute-start(f32[320,128]{1,0:T(8,128)S(1)} %copy-done.2), channel_id=1, source_target_pairs={{0,4},{2,6},{4,0},{6,2},{1,5},{3,7},{5,1},{7,3},{8,12},{10,14},{12... | collective-permute-start | bytes 491528 | tf_op jit(solution)/shard_map/ppermute | solution.py:613
  16.0 12.7 %collective-permute-start.5 = (f32[320,128]{1,0:T(8,128)S(1)}, f32[320,128]{1,0:T(8,128)S(1)}, u32[]{:S(2)}, u32[]{:S(2)}) collective-permute-start(f32[320,128]{1,0:T(8,128)S(1)} %copy-done.2), channel_id=1, source_target_pairs={{0,2},{2,0},{4,6},{6,4},{1,3},{3,1},{5,7},{7,5},{8,10},{10,8},{12,... | collective-permute-start | bytes 491528 | tf_op jit(solution)/shard_map/ppermute | solution.py:613
  16.8 12.0 %collective-permute-start.4 = (f32[136,128]{1,0:T(8,128)S(1)}, f32[136,128]{1,0:T(8,128)S(1)}, u32[]{:S(2)}, u32[]{:S(2)}) collective-permute-start(f32[136,128]{1,0:T(8,128)S(1)} %copy-done.4), channel_id=1, source_target_pairs={{0,24},{8,16},{16,8},{24,0},{1,25},{9,17},{17,9},{25,1},{2,26},{10... | collective-permute-start | bytes 208904 | tf_op jit(solution)/shard_map/ppermute | solution.py:613
  28.8 49.4 %copy-start = (f32[16,8192]{1,0:T(8,128)S(1)}, f32[16,8192]{1,0:T(8,128)}, u32[]{:S(2)}) copy-start(f32[16,8192]{1,0:T(8,128)} %refs_4_) | copy-start | bytes 1572868
  28.8 51.4 %collective-permute-start.10 = (f32[4,280,128]{2,1,0:T(8,128)S(1)}, f32[4,280,128]{2,1,0:T(8,128)S(1)}, u32[]{:S(2)}, u32[]{:S(2)}) collective-permute-start(f32[4,280,128]{2,1,0:T(8,128)S(1)} %pad_maximum_fusion.refs_0_), channel_id=1, source_target_pairs={{0,24},{8,16},{16,8},{24,0},{1,25},{9,17},{17,9},{25,1},{2,26},{10... | collective-permute-start | bytes 1720328 | tf_op jit(solution)/shard_map/ppermute | solution.py:613
  29.3 50.8 %collective-permute-start.9 = (f32[4,280,128]{2,1,0:T(8,128)S(1)}, f32[4,280,128]{2,1,0:T(8,128)S(1)}, u32[]{:S(2)}, u32[]{:S(2)}) collective-permute-start(f32[4,280,128]{2,1,0:T(8,128)S(1)} %pad_maximum_fusion.refs_0_), channel_id=1, source_target_pairs={{0,16},{8,24},{16,0},{24,8},{1,17},{9,25},{17,1},{25,9},{2,18},{10... | collective-permute-start | bytes 1720328 | tf_op jit(solution)/shard_map/ppermute | solution.py:613
  30.9 49.3 %collective-permute-start.8 = (f32[4,280,128]{2,1,0:T(8,128)S(1)}, f32[4,280,128]{2,1,0:T(8,128)S(1)}, u32[]{:S(2)}, u32[]{:S(2)}) collective-permute-start(f32[4,280,128]{2,1,0:T(8,128)S(1)} %pad_maximum_fusion.refs_0_), channel_id=1, source_target_pairs={{0,8},{8,0},{16,24},{24,16},{1,9},{9,1},{17,25},{25,17},{2,10},{10... | collective-permute-start | bytes 1720328 | tf_op jit(solution)/shard_map/ppermute | solution.py:613
  78.1 0.8 copy-start.3
  78.1 2.0 %collective-permute-start.11 = (f32[16,8192]{1,0:T(8,128)S(1)}, f32[16,8192]{1,0:T(8,128)S(1)}, u32[]{:S(2)}, u32[]{:S(2)}) collective-permute-start(f32[16,8192]{1,0:T(8,128)S(1)} %copy-done), channel_id=1, source_target_pairs={{0,1},{1,0},{2,3},{3,2},{4,5},{5,4},{6,7},{7,6},{8,9},{9,8},{10,11... | collective-permute-start | bytes 1572872 | tf_op jit(solution)/shard_map/ppermute | solution.py:613
  78.9 1.3 collective-permute-start.12
  157.5 4.5 %copy-start.1 = (f32[272,128]{1,0:T(8,128)}, f32[272,128]{1,0:T(8,128)S(1)}, u32[]{:S(2)}) copy-start(f32[272,128]{1,0:T(8,128)S(1)} %get-tuple-element.46.own) | copy-start | bytes 417796
  157.5 12.5 %all-to-all-start = ((f32[16,1,2560]{2,1,0:T(1,128)}), f32[16,1,2560]{2,1,0:T(1,128)S(1)}, u32[]{:S(2)}, u32[]{:S(2)}) async-start(f32[16,1,2560]{2,1,0:T(1,128)} %get-tuple-element.47), calls=%async_computation | async-start | bytes 327680 | tf_op jit(solution)/shard_map/all_to_all | solution.py:677
  161.9 1.4 collective-permute-start.13
  163.3 6.7 %copy-start.6 = (f32[272,128]{1,0:T(8,128)}, f32[272,128]{1,0:T(8,128)S(1)}, u32[]{:S(2)}) copy-start(f32[272,128]{1,0:T(8,128)S(1)} %collective-permute-done.13.other) | copy-start | bytes 417796
  170.0 0.7 copy-start.5

commit v7 on v6

--- a/solution.py
+++ b/solution.py
@@ -23,8 +23,8 @@
 ROWS_PRODUCT = 1024
 ROWS_BEGIN = 1024
 ROWS_TURN = 512
-PAIRS = 16
-BLOCKS = 8
+PAIRS = 32
+BLOCKS = 16
 LOW = 2.0**-30
 SMALL = 2.0**-80
 LARGE = 2.0**100
@@ -108,31 +108,55 @@
 
 
 def prepare_kernel(
-    src_pts, cluster, table, src_cent, src_mass, tgt_a, mass_a, tgt_b, mass_b, bundle, src_own
+    rows, slots_each, stride, wanted, src_pts, cluster, src_cent, src_mass, tgt_a, mass_a, tgt_b, mass_b,
+    bundle, src_own, places,
 ):
+    shape = (LANES, LANES)
+    down = lax.broadcasted_iota(jnp.int32, shape, 0)
+    across = lax.broadcasted_iota(jnp.int32, shape, 1)
+    block_bits = TB_DEV.bit_length() - 1
+    entry = wanted[...]
+    owners = entry >> block_bits
+
+    def turned(values):
+        return jnp.transpose(jnp.broadcast_to(values.astype(jnp.float32), shape))
+
+    same = turned(owners) == jnp.broadcast_to(owners.astype(jnp.float32), shape)
+    earlier = jnp.where(same & (down < across), 1.0, 0.0)
+    occurs = jnp.sum(earlier, 0, keepdims=True).astype(jnp.int32)
+    number = lax.broadcasted_iota(jnp.int32, entry.shape, 1)
+    codes = number // SUPP * TB_DEV + (entry & (TB_DEV - 1)) + 1
+    filled, codes = turned(owners * stride + occurs), turned(codes)
+    places[0:1, :] = owners >> 1
+    places[1:2, :] = ((owners & 1) * slots_each + occurs) * BLK
+    bundle[SLOT_AT:TGT_AT, :] = jnp.zeros((TGT_AT - SLOT_AT, LANES), jnp.float32)
+    for k in range(rows):
+        here = filled == (across + k * LANES).astype(jnp.float32)
+        bundle[SLOT_AT + k : SLOT_AT + k + 1, :] = jnp.sum(
+            jnp.where(here, codes, 0.0), 0, keepdims=True
+        )
     to_tiles(src_cent, src_own)
     src_own[F * src_mass.shape[0] :, :] = src_mass[...]
     to_tiles(src_pts, bundle)
     bundle[2 * LANES : SLOT_AT, :] = cluster[...].astype(jnp.float32)
-    bundle[SLOT_AT:TGT_AT, :] = jnp.zeros((TGT_AT - SLOT_AT, LANES), jnp.float32)
-    bundle[SLOT_AT : SLOT_AT + table.shape[0], :] = table[...].astype(jnp.float32)
     bundle[TGT_AT : TGT_AT + F, :] = tgt_a[...]
     bundle[TGT_AT + F : TGT_AT + 2 * F, :] = tgt_b[...]
     masses = jnp.concatenate([mass_a[...], mass_b[...], jnp.ones((6, LANES), jnp.float32)], 0)
     bundle[TGT_AT + 2 * F :, :] = masses
 
 
-def prepare(src_pts, cluster, table, src_cent, src_mass, tgt):
+def prepare(wanted, src_pts, cluster, src_cent, src_mass, tgt, devices, slots_each, stride):
     return pl.pallas_call(
-        prepare_kernel,
+        functools.partial(prepare_kernel, devices * stride // LANES, slots_each, stride),
         out_shape=(
             jax.ShapeDtypeStruct((TGT_AT + 2 * F + 8, LANES), jnp.float32),
             jax.ShapeDtypeStruct(((F + 1) * src_mass.shape[0], LANES), jnp.float32),
+            jax.ShapeDtypeStruct((2, LANES), jnp.int32),
         ),
         in_specs=[VMEM] * 9,
-        out_specs=(VMEM, VMEM),
+        out_specs=(VMEM, VMEM, VMEM),
         name="prepare",
-    )(src_pts, cluster, table, src_cent, src_mass, *tgt)
+    )(wanted, src_pts, cluster, src_cent, src_mass, *tgt)
 
 
 def coarse_kernel(n_src, n_tgt, stored, *refs):
@@ -562,9 +586,7 @@
     )(where, *stacks, *points, *clusters, f_table, g_table)
 
 
-def finish_kernel(
-    from_ref, span_ref, own, other, partial, fine_f_out, fine_g_out, gathered
-):
+def finish_kernel(place_ref, own, other, partial, fine_f_out, fine_g_out, gathered):
     rows = 2 * TB_DEV
     a, b = own[0:rows, :], other[rows : 2 * rows, :]
     top = jnp.maximum(a, b)
@@ -580,8 +602,8 @@
     for block in range(SB_DEV):
         for k in range(SUPP):
             n = block * SUPP + k
-            span = pl.ds(pl.multiple_of(span_ref[n], BLK), BLK)
-            gathered[k, block : block + 1, :] = partial[from_ref[n], :, span]
+            span = pl.ds(pl.multiple_of(place_ref[1, n], BLK), BLK)
+            gathered[k, block : block + 1, :] = partial[place_ref[0, n], :, span]
     values = gathered[...]
     top = jnp.max(values, 0)
     lse = top + jnp.log2(jnp.sum(jnp.exp2(values - top[None]), 0))
@@ -590,22 +612,22 @@
         for k in range(2):
             row = slice(2 * block + k, 2 * block + k + 1)
             piece = term[block : block + 1, k * LANES : (k + 1) * LANES]
-            start_f = own[4 * rows + 2 * block + k : 4 * rows + 2 * block + k + 1, :]
+            start_f = own[8 * TB_DEV + 2 * block + k : 8 * TB_DEV + 2 * block + k + 1, :]
             fine_f_out[row, :] = 0.5 * (start_f + piece)
 
 
-def finish(chips, spans, own, other, partial):
+def finish(places, own, other, partial):
     return pl.pallas_call(
         finish_kernel,
         out_shape=(
             jax.ShapeDtypeStruct((F, LANES), jnp.float32),
             jax.ShapeDtypeStruct((2 * TB_DEV, LANES), jnp.float32),
         ),
-        in_specs=[SMEM, SMEM] + [VMEM] * 3,
+        in_specs=[SMEM] + [VMEM] * 3,
         out_specs=(VMEM, VMEM),
         scratch_shapes=[pltpu.VMEM((SUPP, SB_DEV, BLK), jnp.float32)],
         name="finish",
-    )(chips, spans, own, other, partial)
+    )(places, own, other, partial)
 
 
 def exchange(x, axis, flip):
@@ -627,24 +649,16 @@
     requests_each = SB_DEV * SUPP
     slots_each = requests_each // devices + 1
     stride = 1 << (slots_each - 1).bit_length()
-    wanted = support.reshape(-1)
-    owners = wanted // TB_DEV
-    positions = jnp.arange(requests_each, dtype=jnp.int32)
-    earlier = (owners[None, :] == owners[:, None]) & (positions[None, :] < positions[:, None])
-    occurs = jnp.sum(earlier.astype(jnp.int32), 1)
-    codes = (positions // SUPP) * TB_DEV + wanted % TB_DEV + 1
-    places = jnp.arange(devices * stride, dtype=jnp.int32)
-    filled = owners * stride + occurs
-    table = jnp.sum(jnp.where(filled[None, :] == places[:, None], codes[None, :], 0), 1)
-    chips = owners // n_core
-    spans = (owners % n_core * slots_each + occurs) * BLK
-    bundle, src_own = prepare(
+    bundle, src_own, places = prepare(
+        support.reshape(1, requests_each),
         src_pts,
         src_cluster.reshape(F, LANES),
-        table.reshape(-1, LANES),
         src_cent,
         src_mass.reshape(-1, LANES),
         tgt,
+        devices,
+        slots_each,
+        stride,
     )
     along = [bundle] + [exchange(bundle, "chip", k) for k in range(1, n_chip)]
     src_all = [src_own] + [exchange(src_own, "row", k) for k in range(1, 3)]
@@ -676,7 +690,7 @@
     )
     returned = lax.all_to_all(partial, CHIPS, split_axis=0, concat_axis=0, tiled=True)
     other = exchange(kept, "core", 1)
-    fine_f, fine_g = finish(chips, spans, kept, other, returned)
+    fine_f, fine_g = finish(places, kept, other, returned)
     return coarse_f, coarse_g, fine_f.reshape(-1), fine_g.reshape(-1)
 
 

time: 173 us -> 171 us (0.988)
  other arithmetic: 2.15 us -> 0.14 us
  transfers between devices with their start and end apart: 15 -> 15, of which waited for: 5 -> 5; matrix products, arithmetic and copies ran while one was open for 3% -> 2% of each run, Pallas kernels for 27% -> 27%
where the time goes in v7:
time: 171 us
  Pallas kernels  126 us (74%)
  waiting for transfers between devices  20.9 us (12%)
  starting transfers between devices  17.2 us (10%)
  local copies, waits for them, and re-layouts  5.43 us (3%)
    pallas_call x1, Pallas kernels, fine_update(): pl.pallas_call(functools.partial(fine_kernel, len(stacks), slots_each, st...  76.6 us
    pallas_call x1, Pallas kernels, coarse_duals(): pl.pallas_call(functools.partial(coarse_kernel, len(src), len(tgt), store...  45.9 us
    ppermute x14, waiting for transfers between devices, exchange(): return lax.ppermute(x, axis, [(i, i ^ flip) for i in range(count)])  14.2 us
    ppermute x14, starting transfers between devices, exchange(): return lax.ppermute(x, axis, [(i, i ^ flip) for i in range(count)])  13.3 us
    all_to_all x1, waiting for transfers between devices, on_device(): lax.all_to_all(partial, CHIPS, split_axis=0, concat_axis=0, tiled=True)  6.72 us
    all_to_all x1, starting transfers between devices, on_device(): lax.all_to_all(partial, CHIPS, split_axis=0, concat_axis=0, tiled=True)  3.86 us
  transfers between devices with their start and end apart: 15, of which 5 were waited for; matrix products, arithmetic and copies ran while one was open for 2% of the time, Pallas kernels for 27%

profile of v7, /device:TPU:0, one launch (start us, length us, event | category | flops | bytes accessed | tf_op | source)
XLA Modules:
  0.0 170.7 jit_solution(16636998545402565971)
XLA Ops:
  0.6 0.0 copy-start.8
  0.6 0.5 collective-permute-start
  1.2 0.1 copy-done.8
  1.3 0.5 collective-permute-start.1
  1.7 1.3 reshape.30.wanted
  3.0 0.0 collective-permute-done.1.mass_b
  3.0 0.0 collective-permute-done.tgt_b
  3.0 0.0 copy-start.7
  3.0 0.5 copy-done.9
  3.5 0.1 copy-done.7
  3.6 1.8 %prepare.1 = (f32[320,128]{1,0:T(8,128)}, f32[136,128]{1,0:T(8,128)}, s32[2,128]{1,0:T(2,128)}) custom-call(s32[1,128]{1,0:T(1,128)} %reshape.30.wanted, f32[16,2048]{1,0:T(8,128)} %src_pts.1, s32[16,128]{1,0:T(8,128)} %bitcast.23, f32[16,1024]{1,0:T(8,128)} %src_cent.1, f32[8,128]{1,0:T(8,128)} %bitcast.24, f32[16,128]{1,0:T(8,128)} %tgt_a.1, ...), custom_call_target="tpu_custom_call" | custom-call | tf_op jit(solution)/shard_map/prepare/pallas_call | solution.py:149
  5.4 2.5 %collective-permute-start.3 = (f32[136,128]{1,0:T(8,128)}, f32[136,128]{1,0:T(8,128)S(1)}, u32[]{:S(2)}, u32[]{:S(2)}) collective-permute-start(f32[136,128]{1,0:T(8,128)} %get-tuple-element.32.refs_0_), channel_id=1, source_target_pairs={{0,16},{8,24},{16,0},{24,8},{1,17},{9,25},{17,1},{25,9},{2,18},{10... | collective-permute-start | bytes 208904 | tf_op jit(solution)/shard_map/ppermute | solution.py:635
  8.0 1.5 collective-permute-start.2
  9.4 3.6 %collective-permute-start.7 = (f32[320,128]{1,0:T(8,128)}, f32[320,128]{1,0:T(8,128)S(1)}, u32[]{:S(2)}, u32[]{:S(2)}) collective-permute-start(f32[320,128]{1,0:T(8,128)} %get-tuple-element.36.refs_4_), channel_id=1, source_target_pairs={{0,6},{2,4},{4,2},{6,0},{1,7},{3,5},{5,3},{7,1},{8,14},{10,12},{12... | collective-permute-start | bytes 491528 | tf_op jit(solution)/shard_map/ppermute | solution.py:635
  13.1 1.0 slice_bitcast_fusion.3
  14.0 0.1 collective-permute-start.6
  14.1 0.8 collective-permute-start.5
  14.9 0.0 collective-permute-done.2.refs_1_
  14.9 0.3 collective-permute-start.4
  15.1 3.5 %collective-permute-done.7.refs_7_ = f32[320,128]{1,0:T(8,128)S(1)} collective-permute-done((f32[320,128]{1,0:T(8,128)}, f32[320,128]{1,0:T(8,128)S(1)}, u32[]{:S(2)}, u32[]{:S(2)}) %collective-permute-start.7) | collective-permute-done | bytes 163872 | tf_op jit(solution)/shard_map/ppermute | solution.py:635
  18.6 8.6 %collective-permute-done.6.refs_6_ = f32[320,128]{1,0:T(8,128)S(1)} collective-permute-done((f32[320,128]{1,0:T(8,128)S(1)}, f32[320,128]{1,0:T(8,128)S(1)}, u32[]{:S(2)}, u32[]{:S(2)}) %collective-permute-start.6) | collective-permute-done | bytes 163872 | tf_op jit(solution)/shard_map/ppermute | solution.py:635
  27.3 0.0 collective-permute-done.5.refs_5_
  27.3 0.1 pad_maximum_fusion.refs_0_
  27.4 0.0 collective-permute-done.3.refs_2_
  27.4 0.0 collective-permute-done.4.refs_3_
  27.4 0.5 collective-permute-start.10
  27.9 1.5 collective-permute-start.9
  29.5 1.5 collective-permute-start.8
  31.0 45.9 %coarse.1 = (f32[1,4096]{1,0:T(1,128)S(1)}, f32[1,1024]{1,0:T(1,128)S(1)}) custom-call(f32[136,128]{1,0:T(8,128)S(1)} %copy-done.4, f32[136,128]{1,0:T(8,128)S(1)} %collective-permute-done.2.refs_1_, f32[136,128]{1,0:T(8,128)S(1)} %collective-permute-done.3.refs_2_, f32[136,128]{1,0:T(8,128)S(1)} %collective-permute-done.4.refs_3_, ...), custom_call_target="tpu_custom_call" | custom-call | flops 167772160 | bytes 491520 | tf_op jit(solution)/shard_map/coarse/pallas_call | solution.py:332
  76.9 0.0 copy-start.3
  76.9 0.1 collective-permute-start.11
  77.0 0.7 copy-done.3
  77.6 0.0 collective-permute-start.12
  77.6 0.1 pad_add_fusion.where_ref
  77.7 1.2 collective-permute-done.12.refs_7_
  78.9 0.0 collective-permute-done.11.refs_5_
  78.9 0.0 collective-permute-done.10.refs_3_
  78.9 0.0 collective-permute-done.9.refs_2_
  78.9 0.0 collective-permute-done.8.refs_1_
  78.9 76.6 %fine.1 = (f32[16,1,2560]{2,1,0:T(1,128)}, f32[272,128]{1,0:T(8,128)S(1)}) custom-call(s32[4]{0:T(128)S(1)} %pad_add_fusion.where_ref, f32[4,280,128]{2,1,0:T(8,128)S(1)} %pad_maximum_fusion.refs_0_, f32[4,280,128]{2,1,0:T(8,128)S(1)} %collective-permute-done.8.refs_1_, f32[4,280,128]{2,1,0:T(8,128)S(1)} %collective-permute-done.9.refs_2_, ...), custom_call_target="tpu_custom_call" | custom-call | tf_op jit(solution)/shard_map/fine/pallas_call | solution.py:563
  155.5 3.9 %all-to-all-start = ((f32[16,1,2560]{2,1,0:T(1,128)}), f32[16,1,2560]{2,1,0:T(1,128)S(1)}, u32[]{:S(2)}, u32[]{:S(2)}) async-start(f32[16,1,2560]{2,1,0:T(1,128)} %get-tuple-element.49), calls=%async_computation | async-start | bytes 327680 | tf_op jit(solution)/shard_map/all_to_all | solution.py:691
  159.4 0.6 slice.22
  160.0 0.0 collective-permute-start.13
  160.0 0.5 slice_bitcast_fusion.4
  160.5 0.8 collective-permute-done.13.other
  161.4 6.7 %all-to-all-done.partial = f32[16,1,2560]{2,1,0:T(1,128)S(1)} async-done(((f32[16,1,2560]{2,1,0:T(1,128)}), f32[16,1,2560]{2,1,0:T(1,128)S(1)}, u32[]{:S(2)}, u32[]{:S(2)}) %all-to-all-start) | async-done | bytes 163872 | tf_op jit(solution)/shard_map/all_to_all | solution.py:691
  168.1 0.7 copy-done.5
  168.7 1.9 %finish.1 = (f32[16,128]{1,0:T(8,128)}, f32[64,128]{1,0:T(8,128)}) custom-call(s32[2,128]{1,0:T(2,128)} %get-tuple-element.44.place_ref, f32[272,128]{1,0:T(8,128)} %copy-done.1, f32[272,128]{1,0:T(8,128)} %copy-done.6, f32[16,1,2560]{2,1,0:T(1,128)} %copy-done.5), custom_call_target="tpu_custom_call" | custom-call | tf_op jit(solution)/shard_map/finish/pallas_call | solution.py:620
  (15 shorter events, 0.1 us)
Async XLA Ops:
  0.6 0.7 copy-start.8
  0.6 2.4 %collective-permute-start = (f32[16,128]{1,0:T(8,128)}, f32[16,128]{1,0:T(8,128)S(1)}, u32[]{:S(2)}, u32[]{:S(2)}) collective-permute-start(f32[16,128]{1,0:T(8,128)} %tgt_a.1), channel_id=1, source_target_pairs={{0,1},{1,0},{2,3},{3,2},{4,5},{5,4},{6,7},{7,6},{8,9},{9,8},{10,11... | collective-permute-start | bytes 24584 | tf_op jit(solution)/shard_map/ppermute | solution.py:635
  1.3 1.7 %collective-permute-start.1 = (f32[1,128]{1,0:T(1,128)S(1)}, f32[1,128]{1,0:T(1,128)S(1)}, u32[]{:S(2)}, u32[]{:S(2)}) collective-permute-start(f32[1,128]{1,0:T(1,128)S(1)} %bitcast.27), channel_id=1, source_target_pairs={{0,1},{1,0},{2,3},{3,2},{4,5},{5,4},{6,7},{7,6},{8,9},{9,8},{10,11... | collective-permute-start | bytes 1544 | tf_op jit(solution)/shard_map/ppermute | solution.py:635
  3.0 0.5 copy-start.9
  3.0 0.6 copy-start.7
  5.4 8.6 %copy-start.2 = (f32[320,128]{1,0:T(8,128)S(1)}, f32[320,128]{1,0:T(8,128)}, u32[]{:S(2)}) copy-start(f32[320,128]{1,0:T(8,128)} %get-tuple-element.36.refs_4_) | copy-start | bytes 491524
  5.4 21.9 %collective-permute-start.3 = (f32[136,128]{1,0:T(8,128)}, f32[136,128]{1,0:T(8,128)S(1)}, u32[]{:S(2)}, u32[]{:S(2)}) collective-permute-start(f32[136,128]{1,0:T(8,128)} %get-tuple-element.32.refs_0_), channel_id=1, source_target_pairs={{0,16},{8,24},{16,0},{24,8},{1,17},{9,25},{17,1},{25,9},{2,18},{10... | collective-permute-start | bytes 208904 | tf_op jit(solution)/shard_map/ppermute | solution.py:635
  8.0 6.9 %collective-permute-start.2 = (f32[136,128]{1,0:T(8,128)}, f32[136,128]{1,0:T(8,128)S(1)}, u32[]{:S(2)}, u32[]{:S(2)}) collective-permute-start(f32[136,128]{1,0:T(8,128)} %get-tuple-element.32.refs_0_), channel_id=1, source_target_pairs={{0,8},{8,0},{16,24},{24,16},{1,9},{9,1},{17,25},{25,17},{2,10},{10... | collective-permute-start | bytes 208904 | tf_op jit(solution)/shard_map/ppermute | solution.py:635
  9.4 5.4 %copy-start.4 = (f32[136,128]{1,0:T(8,128)S(1)}, f32[136,128]{1,0:T(8,128)}, u32[]{:S(2)}) copy-start(f32[136,128]{1,0:T(8,128)} %get-tuple-element.32.refs_0_) | copy-start | bytes 208900
  9.4 9.2 %collective-permute-start.7 = (f32[320,128]{1,0:T(8,128)}, f32[320,128]{1,0:T(8,128)S(1)}, u32[]{:S(2)}, u32[]{:S(2)}) collective-permute-start(f32[320,128]{1,0:T(8,128)} %get-tuple-element.36.refs_4_), channel_id=1, source_target_pairs={{0,6},{2,4},{4,2},{6,0},{1,7},{3,5},{5,3},{7,1},{8,14},{10,12},{12... | collective-permute-start | bytes 491528 | tf_op jit(solution)/shard_map/ppermute | solution.py:635
  14.0 13.2 %collective-permute-start.6 = (f32[320,128]{1,0:T(8,128)S(1)}, f32[320,128]{1,0:T(8,128)S(1)}, u32[]{:S(2)}, u32[]{:S(2)}) collective-permute-start(f32[320,128]{1,0:T(8,128)S(1)} %copy-done.2), channel_id=1, source_target_pairs={{0,4},{2,6},{4,0},{6,2},{1,5},{3,7},{5,1},{7,3},{8,12},{10,14},{12... | collective-permute-start | bytes 491528 | tf_op jit(solution)/shard_map/ppermute | solution.py:635
  14.1 13.2 %collective-permute-start.5 = (f32[320,128]{1,0:T(8,128)S(1)}, f32[320,128]{1,0:T(8,128)S(1)}, u32[]{:S(2)}, u32[]{:S(2)}) collective-permute-start(f32[320,128]{1,0:T(8,128)S(1)} %copy-done.2), channel_id=1, source_target_pairs={{0,2},{2,0},{4,6},{6,4},{1,3},{3,1},{5,7},{7,5},{8,10},{10,8},{12,... | collective-permute-start | bytes 491528 | tf_op jit(solution)/shard_map/ppermute | solution.py:635
  14.9 12.5 %collective-permute-start.4 = (f32[136,128]{1,0:T(8,128)S(1)}, f32[136,128]{1,0:T(8,128)S(1)}, u32[]{:S(2)}, u32[]{:S(2)}) collective-permute-start(f32[136,128]{1,0:T(8,128)S(1)} %copy-done.4), channel_id=1, source_target_pairs={{0,24},{8,16},{16,8},{24,0},{1,25},{9,17},{17,9},{25,1},{2,26},{10... | collective-permute-start | bytes 208904 | tf_op jit(solution)/shard_map/ppermute | solution.py:635
  27.4 49.5 %copy-start = (f32[16,8192]{1,0:T(8,128)S(1)}, f32[16,8192]{1,0:T(8,128)}, u32[]{:S(2)}) copy-start(f32[16,8192]{1,0:T(8,128)} %refs_4_) | copy-start | bytes 1572868
  27.4 51.5 %collective-permute-start.10 = (f32[4,280,128]{2,1,0:T(8,128)S(1)}, f32[4,280,128]{2,1,0:T(8,128)S(1)}, u32[]{:S(2)}, u32[]{:S(2)}) collective-permute-start(f32[4,280,128]{2,1,0:T(8,128)S(1)} %pad_maximum_fusion.refs_0_), channel_id=1, source_target_pairs={{0,24},{8,16},{16,8},{24,0},{1,25},{9,17},{17,9},{25,1},{2,26},{10... | collective-permute-start | bytes 1720328 | tf_op jit(solution)/shard_map/ppermute | solution.py:635
  27.9 51.0 %collective-permute-start.9 = (f32[4,280,128]{2,1,0:T(8,128)S(1)}, f32[4,280,128]{2,1,0:T(8,128)S(1)}, u32[]{:S(2)}, u32[]{:S(2)}) collective-permute-start(f32[4,280,128]{2,1,0:T(8,128)S(1)} %pad_maximum_fusion.refs_0_), channel_id=1, source_target_pairs={{0,16},{8,24},{16,0},{24,8},{1,17},{9,25},{17,1},{25,9},{2,18},{10... | collective-permute-start | bytes 1720328 | tf_op jit(solution)/shard_map/ppermute | solution.py:635
  29.5 49.5 %collective-permute-start.8 = (f32[4,280,128]{2,1,0:T(8,128)S(1)}, f32[4,280,128]{2,1,0:T(8,128)S(1)}, u32[]{:S(2)}, u32[]{:S(2)}) collective-permute-start(f32[4,280,128]{2,1,0:T(8,128)S(1)} %pad_maximum_fusion.refs_0_), channel_id=1, source_target_pairs={{0,8},{8,0},{16,24},{24,16},{1,9},{9,1},{17,25},{25,17},{2,10},{10... | collective-permute-start | bytes 1720328 | tf_op jit(solution)/shard_map/ppermute | solution.py:635
  76.9 0.8 copy-start.3
  76.9 2.0 %collective-permute-start.11 = (f32[16,8192]{1,0:T(8,128)S(1)}, f32[16,8192]{1,0:T(8,128)S(1)}, u32[]{:S(2)}, u32[]{:S(2)}) collective-permute-start(f32[16,8192]{1,0:T(8,128)S(1)} %copy-done), channel_id=1, source_target_pairs={{0,1},{1,0},{2,3},{3,2},{4,5},{5,4},{6,7},{7,6},{8,9},{9,8},{10,11... | collective-permute-start | bytes 1572872 | tf_op jit(solution)/shard_map/ppermute | solution.py:635
  77.6 1.3 collective-permute-start.12
  155.5 4.5 %copy-start.1 = (f32[272,128]{1,0:T(8,128)}, f32[272,128]{1,0:T(8,128)S(1)}, u32[]{:S(2)}) copy-start(f32[272,128]{1,0:T(8,128)S(1)} %get-tuple-element.48.own) | copy-start | bytes 417796
  155.5 12.6 %all-to-all-start = ((f32[16,1,2560]{2,1,0:T(1,128)}), f32[16,1,2560]{2,1,0:T(1,128)S(1)}, u32[]{:S(2)}, u32[]{:S(2)}) async-start(f32[16,1,2560]{2,1,0:T(1,128)} %get-tuple-element.49), calls=%async_computation | async-start | bytes 327680 | tf_op jit(solution)/shard_map/all_to_all | solution.py:691
  160.0 1.4 collective-permute-start.13
  161.4 6.7 %copy-start.6 = (f32[272,128]{1,0:T(8,128)}, f32[272,128]{1,0:T(8,128)S(1)}, u32[]{:S(2)}) copy-start(f32[272,128]{1,0:T(8,128)S(1)} %collective-permute-done.13.other) | copy-start | bytes 417796
  168.1 0.7 copy-start.5

commit v8 on v7

--- a/solution.py
+++ b/solution.py
@@ -22,7 +22,7 @@
 ROWS = 256
 ROWS_PRODUCT = 1024
 ROWS_BEGIN = 1024
-ROWS_TURN = 512
+ROWS_TURN = 1024
 PAIRS = 32
 BLOCKS = 16
 LOW = 2.0**-30
@@ -323,7 +323,7 @@
         f_out[:, span] = jnp.sum(jnp.where(diagonal, f, 0.0), 0, keepdims=True) * (1.0 / SCALE)
         return carry
 
-    lax.fori_loop(0, ks // LANES, to_lanes, 0)
+    lax.fori_loop(0, ks // LANES, to_lanes, 0, unroll=8)
 
 def coarse_duals(src, tgt):
     ks = sum(part.shape[0] // (F + 1) * LANES for part in src)
@@ -450,7 +450,7 @@
             used, unused = used + step, unused - (1 - step)
         return used, unused
 
-    used, _ = lax.fori_loop(0, senders, place, (jnp.int32(0), jnp.int32(total - 1)))
+    used, _ = lax.fori_loop(0, senders, place, (jnp.int32(0), jnp.int32(total - 1)), unroll=4)
     for copy in late:
         copy.wait()
     index = bundle[0, 2 * LANES : SLOT_AT, :].astype(jnp.int32) ^ src_flip

time: 171 us -> 170 us (level)
  no operation moved by 1% of the time
where the time goes in v8:
time: 170 us; the launch traced here: 169 us
  Pallas kernels  125 us (74%)
  waiting for transfers between devices  20.9 us (12%)
  starting transfers between devices  17.2 us (10%)
  local copies, waits for them, and re-layouts  5.43 us (3%)
    pallas_call x1, Pallas kernels, fine_update(): pl.pallas_call(functools.partial(fine_kernel, len(stacks), slots_each, st...  76.2 us
    pallas_call x1, Pallas kernels, coarse_duals(): pl.pallas_call(functools.partial(coarse_kernel, len(src), len(tgt), store...  45 us
    ppermute x14, waiting for transfers between devices, exchange(): return lax.ppermute(x, axis, [(i, i ^ flip) for i in range(count)])  14.2 us
    ppermute x14, starting transfers between devices, exchange(): return lax.ppermute(x, axis, [(i, i ^ flip) for i in range(count)])  13.3 us
    all_to_all x1, waiting for transfers between devices, on_device(): lax.all_to_all(partial, CHIPS, split_axis=0, concat_axis=0, tiled=True)  6.68 us
    all_to_all x1, starting transfers between devices, on_device(): lax.all_to_all(partial, CHIPS, split_axis=0, concat_axis=0, tiled=True)  3.87 us
  transfers between devices with their start and end apart: 15, of which 5 were waited for; matrix products, arithmetic and copies ran while one was open for 2% of the time, Pallas kernels for 27%

profile of v8, /device:TPU:0, one launch (start us, length us, event | category | flops | bytes accessed | tf_op | source)
XLA Modules:
  0.0 169.3 jit_solution(15889316259820210075)
XLA Ops:
  0.6 0.0 copy-start.8
  0.6 0.5 collective-permute-start
  1.2 0.1 copy-done.8
  1.3 0.5 collective-permute-start.1
  1.7 1.3 reshape.30.wanted
  3.0 0.0 collective-permute-done.1.mass_b
  3.0 0.0 collective-permute-done.tgt_b
  3.0 0.0 copy-start.7
  3.0 0.5 copy-done.9
  3.5 0.1 copy-done.7
  3.6 1.8 %prepare.1 = (f32[320,128]{1,0:T(8,128)}, f32[136,128]{1,0:T(8,128)}, s32[2,128]{1,0:T(2,128)}) custom-call(s32[1,128]{1,0:T(1,128)} %reshape.30.wanted, f32[16,2048]{1,0:T(8,128)} %src_pts.1, s32[16,128]{1,0:T(8,128)} %bitcast.23, f32[16,1024]{1,0:T(8,128)} %src_cent.1, f32[8,128]{1,0:T(8,128)} %bitcast.24, f32[16,128]{1,0:T(8,128)} %tgt_a.1, ...), custom_call_target="tpu_custom_call" | custom-call | tf_op jit(solution)/shard_map/prepare/pallas_call | solution.py:149
  5.4 2.5 %collective-permute-start.3 = (f32[136,128]{1,0:T(8,128)}, f32[136,128]{1,0:T(8,128)S(1)}, u32[]{:S(2)}, u32[]{:S(2)}) collective-permute-start(f32[136,128]{1,0:T(8,128)} %get-tuple-element.32.refs_0_), channel_id=1, source_target_pairs={{0,16},{8,24},{16,0},{24,8},{1,17},{9,25},{17,1},{25,9},{2,18},{10... | collective-permute-start | bytes 208904 | tf_op jit(solution)/shard_map/ppermute | solution.py:635
  8.0 1.5 collective-permute-start.2
  9.4 3.6 %collective-permute-start.7 = (f32[320,128]{1,0:T(8,128)}, f32[320,128]{1,0:T(8,128)S(1)}, u32[]{:S(2)}, u32[]{:S(2)}) collective-permute-start(f32[320,128]{1,0:T(8,128)} %get-tuple-element.36.refs_4_), channel_id=1, source_target_pairs={{0,6},{2,4},{4,2},{6,0},{1,7},{3,5},{5,3},{7,1},{8,14},{10,12},{12... | collective-permute-start | bytes 491528 | tf_op jit(solution)/shard_map/ppermute | solution.py:635
  13.1 1.0 slice_bitcast_fusion.3
  14.0 0.1 collective-permute-start.6
  14.1 0.8 collective-permute-start.5
  14.9 0.0 collective-permute-done.2.refs_1_
  14.9 0.3 collective-permute-start.4
  15.1 3.5 %collective-permute-done.7.refs_7_ = f32[320,128]{1,0:T(8,128)S(1)} collective-permute-done((f32[320,128]{1,0:T(8,128)}, f32[320,128]{1,0:T(8,128)S(1)}, u32[]{:S(2)}, u32[]{:S(2)}) %collective-permute-start.7) | collective-permute-done | bytes 163872 | tf_op jit(solution)/shard_map/ppermute | solution.py:635
  18.6 8.6 %collective-permute-done.6.refs_6_ = f32[320,128]{1,0:T(8,128)S(1)} collective-permute-done((f32[320,128]{1,0:T(8,128)S(1)}, f32[320,128]{1,0:T(8,128)S(1)}, u32[]{:S(2)}, u32[]{:S(2)}) %collective-permute-start.6) | collective-permute-done | bytes 163872 | tf_op jit(solution)/shard_map/ppermute | solution.py:635
  27.3 0.0 collective-permute-done.5.refs_5_
  27.3 0.1 pad_maximum_fusion.refs_0_
  27.4 0.0 collective-permute-done.3.refs_2_
  27.4 0.0 collective-permute-done.4.refs_3_
  27.4 0.5 collective-permute-start.10
  27.9 1.5 collective-permute-start.9
  29.5 1.5 collective-permute-start.8
  31.0 45.0 %coarse.1 = (f32[1,4096]{1,0:T(1,128)S(1)}, f32[1,1024]{1,0:T(1,128)S(1)}) custom-call(f32[136,128]{1,0:T(8,128)S(1)} %copy-done.4, f32[136,128]{1,0:T(8,128)S(1)} %collective-permute-done.2.refs_1_, f32[136,128]{1,0:T(8,128)S(1)} %collective-permute-done.3.refs_2_, f32[136,128]{1,0:T(8,128)S(1)} %collective-permute-done.4.refs_3_, ...), custom_call_target="tpu_custom_call" | custom-call | flops 167772160 | bytes 491520 | tf_op jit(solution)/shard_map/coarse/pallas_call | solution.py:332
  75.9 0.0 copy-start.3
  76.0 0.1 collective-permute-start.11
  76.1 0.7 copy-done.3
  76.7 0.0 collective-permute-start.12
  76.7 0.1 pad_add_fusion.where_ref
  76.8 1.2 collective-permute-done.12.refs_7_
  78.0 0.0 collective-permute-done.11.refs_5_
  78.0 0.0 collective-permute-done.10.refs_3_
  78.0 0.0 collective-permute-done.9.refs_2_
  78.0 0.0 collective-permute-done.8.refs_1_
  78.0 76.2 %fine.1 = (f32[16,1,2560]{2,1,0:T(1,128)}, f32[272,128]{1,0:T(8,128)S(1)}) custom-call(s32[4]{0:T(128)S(1)} %pad_add_fusion.where_ref, f32[4,280,128]{2,1,0:T(8,128)S(1)} %pad_maximum_fusion.refs_0_, f32[4,280,128]{2,1,0:T(8,128)S(1)} %collective-permute-done.8.refs_1_, f32[4,280,128]{2,1,0:T(8,128)S(1)} %collective-permute-done.9.refs_2_, ...), custom_call_target="tpu_custom_call" | custom-call | tf_op jit(solution)/shard_map/fine/pallas_call | solution.py:563
  154.2 3.9 %all-to-all-start = ((f32[16,1,2560]{2,1,0:T(1,128)}), f32[16,1,2560]{2,1,0:T(1,128)S(1)}, u32[]{:S(2)}, u32[]{:S(2)}) async-start(f32[16,1,2560]{2,1,0:T(1,128)} %get-tuple-element.49), calls=%async_computation | async-start | bytes 327680 | tf_op jit(solution)/shard_map/all_to_all | solution.py:691
  158.1 0.6 slice.22
  158.7 0.0 collective-permute-start.13
  158.7 0.5 slice_bitcast_fusion.4
  159.2 0.8 collective-permute-done.13.other
  160.0 6.7 %all-to-all-done.partial = f32[16,1,2560]{2,1,0:T(1,128)S(1)} async-done(((f32[16,1,2560]{2,1,0:T(1,128)}), f32[16,1,2560]{2,1,0:T(1,128)S(1)}, u32[]{:S(2)}, u32[]{:S(2)}) %all-to-all-start) | async-done | bytes 163872 | tf_op jit(solution)/shard_map/all_to_all | solution.py:691
  166.7 0.7 copy-done.5
  167.4 1.9 %finish.1 = (f32[16,128]{1,0:T(8,128)}, f32[64,128]{1,0:T(8,128)}) custom-call(s32[2,128]{1,0:T(2,128)} %get-tuple-element.44.place_ref, f32[272,128]{1,0:T(8,128)} %copy-done.1, f32[272,128]{1,0:T(8,128)} %copy-done.6, f32[16,1,2560]{2,1,0:T(1,128)} %copy-done.5), custom_call_target="tpu_custom_call" | custom-call | tf_op jit(solution)/shard_map/finish/pallas_call | solution.py:620
  (15 shorter events, 0.1 us)
Async XLA Ops:
  0.6 0.7 copy-start.8
  0.6 2.4 %collective-permute-start = (f32[16,128]{1,0:T(8,128)}, f32[16,128]{1,0:T(8,128)S(1)}, u32[]{:S(2)}, u32[]{:S(2)}) collective-permute-start(f32[16,128]{1,0:T(8,128)} %tgt_a.1), channel_id=1, source_target_pairs={{0,1},{1,0},{2,3},{3,2},{4,5},{5,4},{6,7},{7,6},{8,9},{9,8},{10,11... | collective-permute-start | bytes 24584 | tf_op jit(solution)/shard_map/ppermute | solution.py:635
  1.3 1.7 %collective-permute-start.1 = (f32[1,128]{1,0:T(1,128)S(1)}, f32[1,128]{1,0:T(1,128)S(1)}, u32[]{:S(2)}, u32[]{:S(2)}) collective-permute-start(f32[1,128]{1,0:T(1,128)S(1)} %bitcast.27), channel_id=1, source_target_pairs={{0,1},{1,0},{2,3},{3,2},{4,5},{5,4},{6,7},{7,6},{8,9},{9,8},{10,11... | collective-permute-start | bytes 1544 | tf_op jit(solution)/shard_map/ppermute | solution.py:635
  3.0 0.5 copy-start.9
  3.0 0.6 copy-start.7
  5.4 8.6 %copy-start.2 = (f32[320,128]{1,0:T(8,128)S(1)}, f32[320,128]{1,0:T(8,128)}, u32[]{:S(2)}) copy-start(f32[320,128]{1,0:T(8,128)} %get-tuple-element.36.refs_4_) | copy-start | bytes 491524
  5.4 21.9 %collective-permute-start.3 = (f32[136,128]{1,0:T(8,128)}, f32[136,128]{1,0:T(8,128)S(1)}, u32[]{:S(2)}, u32[]{:S(2)}) collective-permute-start(f32[136,128]{1,0:T(8,128)} %get-tuple-element.32.refs_0_), channel_id=1, source_target_pairs={{0,16},{8,24},{16,0},{24,8},{1,17},{9,25},{17,1},{25,9},{2,18},{10... | collective-permute-start | bytes 208904 | tf_op jit(solution)/shard_map/ppermute | solution.py:635
  8.0 6.9 %collective-permute-start.2 = (f32[136,128]{1,0:T(8,128)}, f32[136,128]{1,0:T(8,128)S(1)}, u32[]{:S(2)}, u32[]{:S(2)}) collective-permute-start(f32[136,128]{1,0:T(8,128)} %get-tuple-element.32.refs_0_), channel_id=1, source_target_pairs={{0,8},{8,0},{16,24},{24,16},{1,9},{9,1},{17,25},{25,17},{2,10},{10... | collective-permute-start | bytes 208904 | tf_op jit(solution)/shard_map/ppermute | solution.py:635
  9.4 5.4 %copy-start.4 = (f32[136,128]{1,0:T(8,128)S(1)}, f32[136,128]{1,0:T(8,128)}, u32[]{:S(2)}) copy-start(f32[136,128]{1,0:T(8,128)} %get-tuple-element.32.refs_0_) | copy-start | bytes 208900
  9.4 9.2 %collective-permute-start.7 = (f32[320,128]{1,0:T(8,128)}, f32[320,128]{1,0:T(8,128)S(1)}, u32[]{:S(2)}, u32[]{:S(2)}) collective-permute-start(f32[320,128]{1,0:T(8,128)} %get-tuple-element.36.refs_4_), channel_id=1, source_target_pairs={{0,6},{2,4},{4,2},{6,0},{1,7},{3,5},{5,3},{7,1},{8,14},{10,12},{12... | collective-permute-start | bytes 491528 | tf_op jit(solution)/shard_map/ppermute | solution.py:635
  14.0 13.2 %collective-permute-start.6 = (f32[320,128]{1,0:T(8,128)S(1)}, f32[320,128]{1,0:T(8,128)S(1)}, u32[]{:S(2)}, u32[]{:S(2)}) collective-permute-start(f32[320,128]{1,0:T(8,128)S(1)} %copy-done.2), channel_id=1, source_target_pairs={{0,4},{2,6},{4,0},{6,2},{1,5},{3,7},{5,1},{7,3},{8,12},{10,14},{12... | collective-permute-start | bytes 491528 | tf_op jit(solution)/shard_map/ppermute | solution.py:635
  14.1 13.2 %collective-permute-start.5 = (f32[320,128]{1,0:T(8,128)S(1)}, f32[320,128]{1,0:T(8,128)S(1)}, u32[]{:S(2)}, u32[]{:S(2)}) collective-permute-start(f32[320,128]{1,0:T(8,128)S(1)} %copy-done.2), channel_id=1, source_target_pairs={{0,2},{2,0},{4,6},{6,4},{1,3},{3,1},{5,7},{7,5},{8,10},{10,8},{12,... | collective-permute-start | bytes 491528 | tf_op jit(solution)/shard_map/ppermute | solution.py:635
  14.9 12.5 %collective-permute-start.4 = (f32[136,128]{1,0:T(8,128)S(1)}, f32[136,128]{1,0:T(8,128)S(1)}, u32[]{:S(2)}, u32[]{:S(2)}) collective-permute-start(f32[136,128]{1,0:T(8,128)S(1)} %copy-done.4), channel_id=1, source_target_pairs={{0,24},{8,16},{16,8},{24,0},{1,25},{9,17},{17,9},{25,1},{2,26},{10... | collective-permute-start | bytes 208904 | tf_op jit(solution)/shard_map/ppermute | solution.py:635
  27.4 48.6 %copy-start = (f32[16,8192]{1,0:T(8,128)S(1)}, f32[16,8192]{1,0:T(8,128)}, u32[]{:S(2)}) copy-start(f32[16,8192]{1,0:T(8,128)} %refs_4_) | copy-start | bytes 1572868
  27.4 50.6 %collective-permute-start.10 = (f32[4,280,128]{2,1,0:T(8,128)S(1)}, f32[4,280,128]{2,1,0:T(8,128)S(1)}, u32[]{:S(2)}, u32[]{:S(2)}) collective-permute-start(f32[4,280,128]{2,1,0:T(8,128)S(1)} %pad_maximum_fusion.refs_0_), channel_id=1, source_target_pairs={{0,24},{8,16},{16,8},{24,0},{1,25},{9,17},{17,9},{25,1},{2,26},{10... | collective-permute-start | bytes 1720328 | tf_op jit(solution)/shard_map/ppermute | solution.py:635
  27.9 50.1 %collective-permute-start.9 = (f32[4,280,128]{2,1,0:T(8,128)S(1)}, f32[4,280,128]{2,1,0:T(8,128)S(1)}, u32[]{:S(2)}, u32[]{:S(2)}) collective-permute-start(f32[4,280,128]{2,1,0:T(8,128)S(1)} %pad_maximum_fusion.refs_0_), channel_id=1, source_target_pairs={{0,16},{8,24},{16,0},{24,8},{1,17},{9,25},{17,1},{25,9},{2,18},{10... | collective-permute-start | bytes 1720328 | tf_op jit(solution)/shard_map/ppermute | solution.py:635
  29.5 48.5 %collective-permute-start.8 = (f32[4,280,128]{2,1,0:T(8,128)S(1)}, f32[4,280,128]{2,1,0:T(8,128)S(1)}, u32[]{:S(2)}, u32[]{:S(2)}) collective-permute-start(f32[4,280,128]{2,1,0:T(8,128)S(1)} %pad_maximum_fusion.refs_0_), channel_id=1, source_target_pairs={{0,8},{8,0},{16,24},{24,16},{1,9},{9,1},{17,25},{25,17},{2,10},{10... | collective-permute-start | bytes 1720328 | tf_op jit(solution)/shard_map/ppermute | solution.py:635
  75.9 0.8 copy-start.3
  76.0 2.0 %collective-permute-start.11 = (f32[16,8192]{1,0:T(8,128)S(1)}, f32[16,8192]{1,0:T(8,128)S(1)}, u32[]{:S(2)}, u32[]{:S(2)}) collective-permute-start(f32[16,8192]{1,0:T(8,128)S(1)} %copy-done), channel_id=1, source_target_pairs={{0,1},{1,0},{2,3},{3,2},{4,5},{5,4},{6,7},{7,6},{8,9},{9,8},{10,11... | collective-permute-start | bytes 1572872 | tf_op jit(solution)/shard_map/ppermute | solution.py:635
  76.7 1.3 collective-permute-start.12
  154.2 4.5 %copy-start.1 = (f32[272,128]{1,0:T(8,128)}, f32[272,128]{1,0:T(8,128)S(1)}, u32[]{:S(2)}) copy-start(f32[272,128]{1,0:T(8,128)S(1)} %get-tuple-element.48.own) | copy-start | bytes 417796
  154.2 12.5 %all-to-all-start = ((f32[16,1,2560]{2,1,0:T(1,128)}), f32[16,1,2560]{2,1,0:T(1,128)S(1)}, u32[]{:S(2)}, u32[]{:S(2)}) async-start(f32[16,1,2560]{2,1,0:T(1,128)} %get-tuple-element.49), calls=%async_computation | async-start | bytes 327680 | tf_op jit(solution)/shard_map/all_to_all | solution.py:691
  158.7 1.4 collective-permute-start.13
  160.0 6.7 %copy-start.6 = (f32[272,128]{1,0:T(8,128)}, f32[272,128]{1,0:T(8,128)S(1)}, u32[]{:S(2)}) copy-start(f32[272,128]{1,0:T(8,128)S(1)} %collective-permute-done.13.other) | copy-start | bytes 417796
  166.7 0.7 copy-start.5
